TPU v7x, 256 devices: a whole 4x4x8 slice. The times are simulated.
256 devices in a mesh: lat: 16 (over x_lo, y, core), lon: 16 (over x_hi, z).
Axes of the slice: x: 4 (x_hi: 2, x_lo: 2; x = x_hi * 2 + x_lo), y: 4, z: 8, core: 2. Of those that a mesh axis runs over, the one named last changes fastest.
Arguments:
- out_first: float32 [2, 192, 384, 192], P(None, 'lat', 'lon'), may hold values from -6 to 6
- out_second: float32 [2, 192, 384, 192], P(None, 'lat', 'lon'), may hold values from -6 to 6
- cot_first: bfloat16 [2, 192, 384, 192], P(None, 'lat', 'lon'), may hold values from -6 to 6
- cot_second: bfloat16 [2, 192, 384, 192], P(None, 'lat', 'lon'), may hold values from -6 to 6
- gain_attn: float32 [192], replicated, may hold values from 0.5 to 1.5
- w_qkv: bfloat16 [192, 576], replicated, may hold values from -0.4375 to 0.4375
- w_proj: bfloat16 [192, 192], replicated, may hold values from -0.4375 to 0.4375
- earth_bias: bfloat16 [32, 1, 6, 144, 144], P('lat'), may hold values from -3 to 303
- gain_mlp: float32 [192], replicated, may hold values from 0.5 to 1.5
- w_up: bfloat16 [192, 768], replicated, may hold values from -0.4375 to 0.4375
- w_down: bfloat16 [768, 192], replicated, may hold values from -0.21875 to 0.21875
Outputs:
- in_first: float32 [2, 192, 384, 192], P(None, 'lat', 'lon')
- in_second: float32 [2, 192, 384, 192], P(None, 'lat', 'lon')
- grad_first: float32 [2, 192, 384, 192], P(None, 'lat', 'lon')
- grad_second: float32 [2, 192, 384, 192], P(None, 'lat', 'lon')
- grad_gain_attn: float32 [192], replicated
- grad_qkv: float32 [192, 576], replicated
- grad_proj: float32 [192, 192], replicated
- grad_bias: float32 [32, 1, 6, 144, 144], P('lat')
- grad_gain_mlp: float32 [192], replicated
- grad_up: float32 [192, 768], replicated
- grad_down: float32 [768, 192], replicated
All inputs are finite; a program needn't handle non-finite values.
Results may differ from a plain program's by a relative error of at most 0.0099.
Values sent between devices are 32-bit elements; how exact they have to be, the bound alone decides.
No kernel may reach another device: no remote copies, remote signals or barrier semaphores. Data moves between devices by JAX's collectives and lax.ppermute only.
A program may use at most 64 MiB of HBM per device.

v0:
```python
import jax
import jax.numpy as jnp
from jax import lax
from jax.sharding import PartitionSpec as P

HEADS = 6
HEAD_DIM = 32
WIN_LEV = 2
WIN_LAT = 6
WIN_LON = 12


norm_eps = 1e-05
gelu_scale = 0.7978845608028654
gelu_cubic = 0.044715
masked_score = -1000000000.0


def shifted(value, axis, by):
    count = lax.axis_size(axis)
    return lax.ppermute(value, axis, [(i, (i + by) % count) for i in range(count)])


def norm_parts(field):
    average = jnp.mean(field, -1, keepdims=True)
    centred = field - average
    inverse = lax.rsqrt(jnp.mean(centred * centred, -1, keepdims=True) + norm_eps)
    return (centred * inverse, inverse)


def norm_back(cot_normed, norm_gain, unit_field, inverse):
    cot_unit = cot_normed * norm_gain
    return inverse * (
        cot_unit
        - jnp.mean(cot_unit, -1, keepdims=True)
        - unit_field * jnp.mean(cot_unit * unit_field, -1, keepdims=True)
    )


def feedforward_pass(tokens, cot_branch, norm_gain, w_up, w_down):
    unit_field, inverse = norm_parts(tokens)
    normed = (unit_field * norm_gain).astype(jnp.bfloat16)
    up_proj = jnp.dot(normed, w_up, preferred_element_type=jnp.float32)
    tanh_val = jnp.tanh(gelu_scale * (up_proj + gelu_cubic * up_proj * up_proj * up_proj))
    hidden = (0.5 * up_proj * (1.0 + tanh_val)).astype(jnp.bfloat16)
    branch = jnp.dot(hidden, w_down, preferred_element_type=jnp.float32)
    grad_down = jnp.einsum("nf,nd->fd", hidden, cot_branch, preferred_element_type=jnp.float32)
    cot_hidden = jnp.einsum("nd,fd->nf", cot_branch, w_down, preferred_element_type=jnp.float32)
    slope = 0.5 * (1.0 + tanh_val) + 0.5 * up_proj * (1.0 - tanh_val * tanh_val) * gelu_scale * (
        1.0 + 3.0 * gelu_cubic * up_proj * up_proj
    )
    cot_up = (cot_hidden * slope).astype(jnp.bfloat16)
    grad_up = jnp.einsum("nc,nf->cf", normed, cot_up, preferred_element_type=jnp.float32)
    cot_normed = jnp.einsum("nf,cf->nc", cot_up, w_up, preferred_element_type=jnp.float32)
    grad_gain = jnp.sum(cot_normed * unit_field, 0)
    cot_tokens = norm_back(cot_normed, norm_gain, unit_field, inverse)
    return (branch, cot_tokens, grad_gain, grad_up, grad_down)


def group_codes(window_rows, total_lat, levels):
    position = jnp.arange(WIN_LEV * WIN_LAT * WIN_LON, dtype=jnp.int32)
    level_pos = position // (WIN_LAT * WIN_LON)
    lat_pos = position // WIN_LON % WIN_LAT
    level_roll = (
        jnp.arange(levels // WIN_LEV, dtype=jnp.int32)[:, None] * WIN_LEV + level_pos[None, :]
    )
    level_group = ((level_roll - WIN_LEV // 2) % levels + WIN_LEV // 2) // WIN_LEV
    lat_roll = window_rows[:, None] * WIN_LAT + lat_pos[None, :]
    lat_group = ((lat_roll - WIN_LAT // 2) % total_lat + WIN_LAT // 2) // WIN_LAT
    return level_group[None, :, :] * (total_lat + 1) + lat_group[:, None, :]


def into_windows(field):
    levels, lat_rows, columns, channels = field.shape
    shaped = field.reshape(
        levels // WIN_LEV,
        WIN_LEV,
        lat_rows // WIN_LAT,
        WIN_LAT,
        columns // WIN_LON,
        WIN_LON,
        channels,
    )
    shaped = shaped.transpose(2, 0, 4, 1, 3, 5, 6)
    return shaped.reshape(
        lat_rows // WIN_LAT,
        levels // WIN_LEV,
        columns // WIN_LON,
        WIN_LEV * WIN_LAT * WIN_LON,
        channels,
    )


def from_windows(windows):
    bands, groups, sectors, cells, channels = windows.shape
    shaped = windows.reshape(bands, groups, sectors, WIN_LEV, WIN_LAT, WIN_LON, channels)
    shaped = shaped.transpose(1, 3, 0, 4, 2, 5, 6)
    return shaped.reshape(groups * WIN_LEV, bands * WIN_LAT, sectors * WIN_LON, channels)


def attention_pass(windows, cot_windows, bias_table, group_code, norm_gain, w_qkv, w_proj):
    unit_field, inverse = norm_parts(windows)
    normed = (unit_field * norm_gain).astype(jnp.bfloat16)
    qkv = jnp.einsum("blowc,ce->blowe", normed, w_qkv, preferred_element_type=jnp.float32).astype(
        jnp.bfloat16
    )
    split_qkv = qkv.reshape(qkv.shape[:4] + (3, HEADS, HEAD_DIM))
    queries = split_qkv[..., 0, :, :]
    key_part = split_qkv[..., 1, :, :]
    value_part = split_qkv[..., 2, :, :]
    score_scale = HEAD_DIM ** (-0.5)
    scores = (
        jnp.einsum("blowhe,blovhe->blohwv", queries, key_part, preferred_element_type=jnp.float32)
        * score_scale
    )
    scores = scores + bias_table.astype(jnp.float32)[:, :, None]
    same_group = group_code[:, :, None, None, :, None] == group_code[:, :, None, None, None, :]
    scores = jnp.where(same_group, scores, masked_score)
    row_max = jnp.max(scores, -1, keepdims=True)
    exponent = jnp.exp(scores - row_max)
    probability = exponent / jnp.sum(exponent, -1, keepdims=True)
    weights = probability.astype(jnp.bfloat16)
    attended = jnp.einsum(
        "blohwv,blovhe->blowhe", weights, value_part, preferred_element_type=jnp.float32
    ).astype(jnp.bfloat16)
    attended = attended.reshape(qkv.shape[:4] + (HEADS * HEAD_DIM,))
    branch = jnp.einsum("blowc,cd->blowd", attended, w_proj, preferred_element_type=jnp.float32)
    cot_low = cot_windows.astype(jnp.bfloat16)
    grad_proj = jnp.einsum("blowc,blowd->cd", attended, cot_low, preferred_element_type=jnp.float32)
    cot_attended = jnp.einsum(
        "blowd,cd->blowc", cot_low, w_proj, preferred_element_type=jnp.float32
    ).astype(jnp.bfloat16)
    cot_attended = cot_attended.reshape(queries.shape)
    cot_weights = jnp.einsum(
        "blowhe,blovhe->blohwv", cot_attended, value_part, preferred_element_type=jnp.float32
    )
    cot_value = jnp.einsum(
        "blohwv,blowhe->blovhe", weights, cot_attended, preferred_element_type=jnp.float32
    )
    cot_scores = probability * (cot_weights - jnp.sum(cot_weights * probability, -1, keepdims=True))
    grad_bias = jnp.sum(cot_scores, 2)
    cot_scaled = (cot_scores * score_scale).astype(jnp.bfloat16)
    cot_query = jnp.einsum(
        "blohwv,blovhe->blowhe", cot_scaled, key_part, preferred_element_type=jnp.float32
    )
    cot_key = jnp.einsum(
        "blohwv,blowhe->blovhe", cot_scaled, queries, preferred_element_type=jnp.float32
    )
    cot_qkv = jnp.stack([cot_query, cot_key, cot_value], -3).reshape(qkv.shape).astype(jnp.bfloat16)
    grad_qkv = jnp.einsum("blowc,blowe->ce", normed, cot_qkv, preferred_element_type=jnp.float32)
    cot_normed = jnp.einsum("blowe,ce->blowc", cot_qkv, w_qkv, preferred_element_type=jnp.float32)
    grad_gain = jnp.sum(cot_normed * unit_field, (0, 1, 2, 3))
    cot_inputs = norm_back(cot_normed, norm_gain, unit_field, inverse)
    return (branch, cot_inputs, grad_gain, grad_qkv, grad_proj, grad_bias)


def latitude_step(field, offset):
    strip_rows = WIN_LAT // 2
    count = field.shape[2]
    boundary = field[:, :, count - strip_rows :] if offset == 1 else field[:, :, :strip_rows]
    received = shifted(boundary, "lat", offset)
    if offset == 1:
        return jnp.concatenate([received, field[:, :, : count - strip_rows]], axis=2)
    return jnp.concatenate([field[:, :, strip_rows:], received], axis=2)


def longitude_step(field, offset):
    strip_cols = WIN_LON // 2
    count = field.shape[3]
    boundary = field[:, :, :, count - strip_cols :] if offset == 1 else field[:, :, :, :strip_cols]
    received = shifted(boundary, "lon", offset)
    if offset == 1:
        return jnp.concatenate([received, field[:, :, :, : count - strip_cols]], axis=3)
    return jnp.concatenate([field[:, :, :, strip_cols:], received], axis=3)


def shift_both(field, offset):
    return longitude_step(latitude_step(field, offset), offset)


def body(
    out_first,
    out_second,
    cot_first,
    cot_second,
    gain_attn,
    w_qkv,
    w_proj,
    earth_bias,
    gain_mlp,
    w_up,
    w_down,
):
    field_shape = out_first.shape
    channels = field_shape[3]
    results = feedforward_pass(
        out_first.reshape(-1, channels), cot_second.reshape(-1, channels), gain_mlp, w_up, w_down
    )
    mlp_branch, cot_mlp, gain_mlp_part, up_part, down_part = results
    in_second = out_second - mlp_branch.reshape(field_shape)
    grad_first = cot_first.astype(jnp.float32) + cot_mlp.reshape(field_shape)
    stacked = jnp.roll(jnp.stack([in_second, grad_first]), WIN_LEV // 2, axis=1)
    rolled = shift_both(stacked, 1)
    bands = field_shape[1] // WIN_LAT
    total_lat = field_shape[1] * lax.axis_size("lat")
    window_rows = lax.axis_index("lat") * bands + jnp.arange(bands, dtype=jnp.int32)
    group_code = group_codes(window_rows, total_lat, field_shape[0])
    results = attention_pass(
        into_windows(rolled[0]),
        into_windows(rolled[1]),
        earth_bias,
        group_code,
        gain_attn,
        w_qkv,
        w_proj,
    )
    attn_branch, cot_attn, gain_attn_part, qkv_part, proj_part, bias_part = results
    returned = shift_both(jnp.stack([from_windows(attn_branch), from_windows(cot_attn)]), -1)
    returned = jnp.roll(returned, -(WIN_LEV // 2), axis=1)
    in_first = out_first - returned[0]
    grad_second = cot_second.astype(jnp.float32) + returned[1]
    grad_bias = lax.psum(bias_part, "lon")
    summed = lax.psum(
        (gain_attn_part, qkv_part, proj_part, gain_mlp_part, up_part, down_part), ("lat", "lon")
    )
    return (
        in_first,
        in_second,
        grad_first,
        grad_second,
        summed[0],
        summed[1],
        summed[2],
        grad_bias,
        summed[3],
        summed[4],
        summed[5],
    )


def solution(mesh):
    placed = (
        P(None, "lat", "lon", None),
        P(None, "lat", "lon", None),
        P(None, "lat", "lon", None),
        P(None, "lat", "lon", None),
        P(),
        P(),
        P(),
        P("lat", None, None, None, None),
        P(),
        P(),
        P(),
    )
    return jax.shard_map(
        body,
        mesh=mesh,
        in_specs=placed,
        out_specs=(
            P(None, "lat", "lon", None),
            P(None, "lat", "lon", None),
            P(None, "lat", "lon", None),
            P(None, "lat", "lon", None),
            P(),
            P(),
            P(),
            P("lat", None, None, None, None),
            P(),
            P(),
            P(),
        ),
        check_vma=False,
    )
```

profile of v0, /device:TPU:1, one launch (start us, length us, event | category | flops | bytes accessed | tf_op | source)
XLA Modules:
  0.0 530.9 jit_solution(16587720936160129919)
XLA Ops:
  16.9 2.7 collective-permute-start
  22.2 2.5 bitcast_convert_fusion
  24.7 3.0 copy.89
  28.7 1.7 collective-permute-start.1
  30.6 15.3 %collective-permute-done.1 = f32[2,2,12,6,192]{4,3,2,1,0:T(8,128)S(1)} collective-permute-done((f32[2,2,12,6,192]{4,3,2,1,0:T(8,128)S(1)}, f32[2,2,12,6,192]{4,3,2,1,0:T(8,128)S(1)}, u32[]{:S(2)}, u32[]{:S(2)}) %collective-permute-start.1) | collective-permute-done | bytes 221216 | tf_op jit(solution)/shard_map/ppermute | solution.py:21
  50.3 1.6 multiply_convert_fusion.4
  54.4 4.7 fusion.66
  59.1 2.5 convolution_convert_fusion.1
  62.3 1.4 convolution_bitcast_fusion
  63.7 2.5 fusion.30
  66.2 6.9 %convolution_bitcast_fusion.1 = bf16[2,1,2,144,1,6,32]{3,6,5,2,0,4,1:T(8,128)(2,1)} fusion(bf16[2,1,2,144,3,6,32]{3,6,5,4,2,0,1:T(8,128)(2,1)S(1)} %bitcast.165, f32[2,2,6,144,144]{3,4,2,1,0:T(8,128)} %fusion.30, f32[2,2,6,144,144]{3,4,2,1,0:T(8,128)} %get-tuple-element.51, f32[2,2,6,144]{3,2,1,0:T(8,128)S(1)} %get-tuple-element.50), kind=kOutput, calls=%fused_computation.27 | convolution fusion | flops 35337744 | bytes 14835712 | tf_op jit(solution)/shard_map/blohwv,blowhe->blovhe/dot_general | solution.py:146
  73.1 7.0 %convolution_bitcast_fusion.2 = bf16[2,1,2,144,1,6,32]{3,6,5,2,0,4,1:T(8,128)(2,1)} fusion(bf16[2,1,2,144,3,6,32]{3,6,5,4,2,0,1:T(8,128)(2,1)S(1)} %bitcast.166, f32[2,2,6,144,144]{3,4,2,1,0:T(8,128)} %fusion.30, f32[2,2,6,144,144]{3,4,2,1,0:T(8,128)} %get-tuple-element.51, f32[2,2,6,144]{3,2,1,0:T(8,128)S(1)} %get-tuple-element.50), kind=kOutput, calls=%fused_computation.28 | convolution fusion | flops 35337744 | bytes 14835712 | tf_op jit(solution)/shard_map/blohwv,blovhe->blowhe/dot_general | solution.py:143
  80.2 7.4 %fusion.67 = f32[2,6,144,144]{2,3,1,0:T(8,128)} fusion(f32[2,2,6,144,144]{3,4,2,1,0:T(8,128)} %fusion.30, f32[2,2,6,144,144]{3,4,2,1,0:T(8,128)} %get-tuple-element.51, f32[2,2,6,144]{3,2,1,0:T(8,128)S(1)} %get-tuple-element.50), kind=kOutput, calls=%fused_computation.140 | output fusion | flops 2740751 | bytes 4990464 | tf_op jit(solution)/shard_map/sub | solution.py:140
  88.2 1.5 reshape.549
  91.5 2.0 multiply_reduce_fusion.1
  97.1 1.4 convolution_bitcast_fusion.4
  99.9 3.5 collective-permute-done.2
  104.5 1.7 collective-permute-start.3
  106.2 78.3 %all-reduce = (f32[192]{0:T(256)}, f32[192]{0:T(256)}) all-reduce(f32[192]{0:T(256)S(1)} %get-tuple-element.33, f32[192]{0:T(256)S(1)} %get-tuple-element.35), channel_id=1, replica_groups=mesh['lat'=16,'lon'=16] {'lat','lon'}, use_global_device_ids=true, to_apply=%region_12.13 | all-reduce | flops 384 | bytes 3072 | tf_op jit(solution)/shard_map/psum | solution.py:223
  190.6 52.3 %all-reduce.5.cloned.1.call-done = f32[2,1,6,144,144]{3,4,2,0,1:T(8,128)} async-done(((f32[2,1,6,144,144]{3,4,2,0,1:T(8,128)}), f32[2,1,6,144,144]{3,4,2,0,1:T(8,128)}) %all-reduce.5.cloned.1.call-update) | async-done | bytes 995344 | tf_op jit(solution)/shard_map/psum | solution.py:222
  242.9 3.0 copy.114
  245.9 273.0 %all-reduce.7.cloned.1.call-done = (f32[192,576]{1,0:T(8,128)}, f32[192,192]{1,0:T(8,128)}, f32[192,768]{1,0:T(8,128)}, f32[768,192]{0,1:T(8,128)}) async-done(((f32[192,576]{1,0:T(8,128)}, f32[192,192]{1,0:T(8,128)}, f32[192,768]{1,0:T(8,128)}, f32[768,192]{0,1:T(8,128)}), (f32[192,576]{1,0:T(8,128)}, f32[192,192]{1,0:T(8,128)}, f32[192,768]{1,0:T(8,128)}, ...) | async-done | bytes 1769488 | tf_op jit(solution)/shard_map/psum | solution.py:223
  518.8 1.9 copy.158
  520.8 1.6 copy.159
  (120 shorter events, 36.6 us)
Async XLA Ops:
  7.2 4.2 copy-start
  7.2 4.2 copy-start.21
  7.2 235.7 %all-reduce.5.cloned.1.call-start = ((), (), s32[]{:S(2)}) async-start(), calls=%async_computation | async-start | bytes 3538944 | tf_op jit(solution)/shard_map/psum | solution.py:222
  15.7 30.2 %copy-start.2 = (f32[2,12,24,192]{3,2,1,0:T(8,128)}, f32[2,12,24,192]{3,2,1,0:T(8,128)S(1)}, u32[]{:S(2)}) copy-start(f32[2,12,24,192]{3,2,1,0:T(8,128)S(1)} %convert_add_fusion) | copy-start | bytes 1327108
  16.1 29.8 %copy-start.1 = (f32[2,12,24,192]{3,2,1,0:T(8,128)}, f32[2,12,24,192]{3,2,1,0:T(8,128)S(1)}, u32[]{:S(2)}) copy-start(f32[2,12,24,192]{3,2,1,0:T(8,128)S(1)} %sub.115) | copy-start | bytes 1327108
  16.1 3.5 copy-start.11
  16.2 4.7 copy-start.7
  16.9 10.9 %collective-permute-start = (f32[2,2,3,24,192]{4,3,2,1,0:T(8,128)}, f32[2,2,3,24,192]{4,3,2,1,0:T(8,128)}, u32[]{:S(2)}, u32[]{:S(2)}) collective-permute-start(f32[2,2,3,24,192]{4,3,2,1,0:T(8,128)} %pad_maximum_fusion.7), channel_id=1, source_target_pairs={{0,16},{16,32},{32,48},{48,64},{64,80},{80,96},{96,112},{112,128},... | collective-permute-start | bytes 663560 | tf_op jit(solution)/shard_map/ppermute | solution.py:21
  28.7 17.1 %collective-permute-start.1 = (f32[2,2,12,6,192]{4,3,2,1,0:T(8,128)S(1)}, f32[2,2,12,6,192]{4,3,2,1,0:T(8,128)S(1)}, u32[]{:S(2)}, u32[]{:S(2)}) collective-permute-start(f32[2,2,12,6,192]{4,3,2,1,0:T(8,128)S(1)} %pad_maximum_fusion.4), channel_id=1, source_target_pairs={{0,1},{1,2},{2,3},{3,4},{4,5},{5,6},{6,7},{7,8},{8,9},{9,10},{10,1... | collective-permute-start | bytes 663560 | tf_op jit(solution)/shard_map/ppermute | solution.py:21
  48.3 2.1 copy-start.20
  49.3 2.7 copy-start.16
  49.9 3.4 copy-start.19
  59.1 2.5 copy-start.4
  59.1 3.2 copy-start.22
  87.6 2.1 copy-start.15
  91.2 2.3 copy-start.5
  91.2 427.6 %all-reduce.7.cloned.1.call-start = ((), (), s32[]{:S(2)}) async-start(), calls=%async_computation.1 | async-start | bytes 3735552 | tf_op jit(solution)/shard_map/psum | solution.py:223
  91.5 2.3 copy-start.9
  96.7 6.8 %collective-permute-start.2 = (f32[2,2,3,24,192]{4,1,3,2,0:T(2,128)}, f32[2,2,3,24,192]{4,1,3,2,0:T(2,128)}, u32[]{:S(2)}, u32[]{:S(2)}) collective-permute-start(f32[2,2,3,24,192]{4,1,3,2,0:T(2,128)} %pad_maximum_fusion.6), channel_id=1, source_target_pairs={{0,240},{16,0},{32,16},{48,32},{64,48},{80,64},{96,80},{112,96},{1... | collective-permute-start | bytes 663560 | tf_op jit(solution)/shard_map/ppermute | solution.py:21
  104.5 81.3 %collective-permute-start.3 = (f32[2,2,12,6,192]{4,1,3,2,0:T(2,128)S(1)}, f32[2,2,12,6,192]{4,1,3,2,0:T(2,128)S(1)}, u32[]{:S(2)}, u32[]{:S(2)}) collective-permute-start(f32[2,2,12,6,192]{4,1,3,2,0:T(2,128)S(1)} %pad_maximum_fusion.5), channel_id=1, source_target_pairs={{0,15},{1,0},{2,1},{3,2},{4,3},{5,4},{6,5},{7,6},{8,7},{9,8},{10,9... | collective-permute-start | bytes 663560 | tf_op jit(solution)/shard_map/ppermute | solution.py:21
  186.6 1.2 copy-start.3
  186.6 1.2 copy-start.8
  518.8 3.6 copy-start.14
  518.8 4.4 copy-start.13
  (5 other events, 5.0 us)
Sparse Core Ops, SparseCore 0:
  91.3 151.5 all-reduce.4
  251.1 267.7 all-reduce.6
where the time goes:
time: 533 us; the launch traced here: 531 us
  waiting for transfers between devices  344 us (65%)
  blocking collectives  78.3 us (15%)
  matrix products  36.2 us (7%)
  other arithmetic  27.2 us (5%)
  local copies, waits for them, and re-layouts  23.7 us (4%)
  between operations  14.7 us (3%)
  starting transfers between devices  6.78 us (1%)
    psum x1, waiting for transfers between devices, body(): lax.psum((gain_attn_part, qkv_part, proj_part, gain_mlp_part, up_part, do...  273 us
    psum x1, blocking collectives, body(): lax.psum((gain_attn_part, qkv_part, proj_part, gain_mlp_part, up_part, do...  78.3 us
    psum x1, waiting for transfers between devices, body(): grad_bias = lax.psum(bias_part, 'lon')  52.3 us
    ppermute x4, waiting for transfers between devices, shifted(): lax.ppermute(value, axis, [(i, (i + by) % count) for i in range(count)])  18.9 us
    unnamed x53, local copies, waits for them, and re-layouts  11.7 us
  transfers between devices with their start and end apart: 6, of which 4 were waited for; matrix products, arithmetic and copies ran while one was open for 5% of the time, Pallas kernels for 0%

commit v1 on v0

v1 whole, which is shorter than its diff:
```python
import functools

import jax
import jax.numpy as jnp
from jax import lax
from jax.experimental import pallas as pl
from jax.experimental.pallas import tpu as pltpu
from jax.sharding import PartitionSpec as P

HEADS = 6
HEAD_DIM = 32
D = 192
FF = 768
LEV = 2
WIN_LAT = 6
WIN_LON = 12
CELLS = WIN_LAT * WIN_LON
BANDS = 2
SECTORS = 2
ROWS = BANDS * WIN_LAT
COLS = SECTORS * WIN_LON
TOKENS = LEV * ROWS * COLS
HALF_LAT = WIN_LAT // 2
HALF_LON = WIN_LON // 2
STACK = HEADS * CELLS
LANES = 128

norm_eps = 1e-05
gelu_scale = 0.7978845608028654
gelu_cubic = 0.044715
masked_score = -1000000000.0
padded_score = -1e30
score_scale = HEAD_DIM ** (-0.5)

f32 = jnp.float32
bf16 = jnp.bfloat16


def nn(a, b):
    return lax.dot_general(a, b, (((1,), (0,)), ((), ())), preferred_element_type=f32)


def nt(a, b):
    return lax.dot_general(a, b, (((1,), (1,)), ((), ())), preferred_element_type=f32)


def tn(a, b):
    return lax.dot_general(a, b, (((0,), (0,)), ((), ())), preferred_element_type=f32)


def norm_parts(field):
    average = jnp.mean(field, -1, keepdims=True)
    centred = field - average
    inverse = lax.rsqrt(jnp.mean(centred * centred, -1, keepdims=True) + norm_eps)
    return (centred * inverse, inverse)


def norm_back(cot_normed, norm_gain, unit_field, inverse):
    cot_unit = cot_normed * norm_gain
    return inverse * (
        cot_unit
        - jnp.mean(cot_unit, -1, keepdims=True)
        - unit_field * jnp.mean(cot_unit * unit_field, -1, keepdims=True)
    )


def two_halves(first, second, keep_ref, send_ref, where):
    mine = lax.rem(lax.axis_index("lat"), 2) == 0
    keep_ref[where] = jnp.where(mine, first, second)
    send_ref[where] = jnp.where(mine, second, first)


def lat_row(array, level, row):
    return ((array * LEV + level) * HALF_LAT + row) * (COLS - HALF_LON)


def lon_row(array, level, row):
    return ((array * LEV + level) * (ROWS - HALF_LAT) + row) * HALF_LON


def cor_row(array, level, row):
    return ((array * LEV + level) * HALF_LAT + row) * HALF_LON


LAT_ROWS = lat_row(2, 0, 0)
LON_ROWS = lon_row(2, 0, 0)
COR_ROWS = cor_row(2, 0, 0)
KEEP_R = ROWS - HALF_LAT
KEEP_C = COLS - HALF_LON


def ff_kernel(
    first_ref, second_ref, cot_first_ref, cot_second_ref, gain_ref, up_ref, down_ref,
    in_second_ref, grad_first_ref, lat_ref, lon_ref, cor_ref, keep_ref, send_ref, gain_out_ref,
    hidden_ref, cot_up_ref, normed_ref,
):
    tokens = first_ref[...].reshape(TOKENS, D)
    gain = gain_ref[...]
    unit_field, inverse = norm_parts(tokens)
    normed_ref[...] = (unit_field * gain).astype(bf16)
    cot = cot_second_ref[...].astype(f32).reshape(TOKENS, D).astype(bf16)
    w_up = up_ref[...]
    w_down = down_ref[...]
    step = 96
    for i in range(TOKENS // step):
        part = pl.ds(i * step, step)
        up_proj = nn(normed_ref[part, :], w_up)
        square = up_proj * up_proj
        half = 0.5 * (1.0 + jnp.tanh(up_proj * (gelu_scale + gelu_scale * gelu_cubic * square)))
        hidden_ref[part, :] = (up_proj * half).astype(bf16)
        cot_hidden = nt(cot[i * step : (i + 1) * step], w_down)
        slope = half + (half * (1.0 - half)) * up_proj * (
            2.0 * gelu_scale + 6.0 * gelu_scale * gelu_cubic * square
        )
        cot_up_ref[part, :] = (cot_hidden * slope).astype(bf16)
    hidden = hidden_ref[...]
    cot_up = cot_up_ref[...]
    shape = (LEV, ROWS, COLS, D)
    in_second_ref[...] = second_ref[...] - nn(hidden, w_down).reshape(shape)
    cot_normed = nt(cot_up, w_up)
    gain_out_ref[...] = jnp.sum(cot_normed * unit_field, 0, keepdims=True)
    back = norm_back(cot_normed, gain, unit_field, inverse)
    grad_first_ref[...] = cot_first_ref[...].astype(f32) + back.reshape(shape)
    for array, ref in enumerate((in_second_ref, grad_first_ref)):
        for level in range(LEV):
            for row in range(HALF_LAT):
                at = lat_row(array, level, row)
                lat_ref[at : at + KEEP_C, :] = ref[level, KEEP_R + row, 0:KEEP_C, :]
                at = cor_row(array, level, row)
                cor_ref[at : at + HALF_LON, :] = ref[level, KEEP_R + row, KEEP_C:COLS, :]
            for row in range(KEEP_R):
                at = lon_row(array, level, row)
                lon_ref[at : at + HALF_LON, :] = ref[level, row, KEEP_C:COLS, :]
    grad_up = tn(normed_ref[...], cot_up)
    grad_down = tn(cot, hidden)
    for k, grad in enumerate((grad_up, grad_down)):
        tiles = [grad[:, t * LANES : (t + 1) * LANES] for t in range(6)]
        halves = [jnp.concatenate(tiles[3 * h : 3 * h + 3], 0).reshape(8, CELLS, LANES) for h in range(2)]
        two_halves(*halves, keep_ref, send_ref, (slice(None), slice(k * CELLS, (k + 1) * CELLS), slice(None)))


def window_of(band, level, sector):
    return (band * LEV + level) * SECTORS + sector


def pieces(band, sector):
    for row in range(WIN_LAT):
        rolled = band * WIN_LAT + row
        edge = rolled < HALF_LAT
        line = rolled if edge else rolled - HALF_LAT
        if sector == 0:
            yield row, 0, HALF_LON, "cor" if edge else "lon", line, 0
            yield row, HALF_LON, HALF_LON, "lat" if edge else "own", line, 0
        else:
            yield row, 0, WIN_LON, "lat" if edge else "own", line, HALF_LON


def strip_row(source, array, level, line, column):
    place = {"lat": lat_row, "lon": lon_row, "cor": cor_row}[source]
    return place(array, level, line) + column


def attention_kernel(
    in_second_ref, grad_first_ref, lat_ref, lon_ref, cor_ref,
    bias_ref, gain_ref, qkv_ref, proj_ref, gain_mlp_ref,
    own_f_ref, own_c_ref, out_lat_ref, out_lon_ref, out_cor_ref, bias_out_ref, keep_ref, send_ref,
    x_ref, g_ref, q_ref, k_ref, v_ref, ca_ref, att_ref, cq_ref, ck_ref, cv_ref,
):
    strips = {"lat": lat_ref, "lon": lon_ref, "cor": cor_ref}
    for band in range(BANDS):
        for level in range(LEV):
            initial = (level - LEV // 2) % LEV
            for sector in range(SECTORS):
                base = window_of(band, level, sector) * CELLS
                for row, col, count, source, line, start in pieces(band, sector):
                    at = base + row * WIN_LON + col
                    for array, (dst, own) in enumerate(((x_ref, in_second_ref), (g_ref, grad_first_ref))):
                        if source == "own":
                            dst[at : at + count, :] = own[initial, line, start : start + count, :]
                        else:
                            src = strip_row(source, array, initial, line, start)
                            dst[at : at + count, :] = strips[source][src : src + count, :]
    gain = gain_ref[...]
    unit_field, inverse = norm_parts(x_ref[...])
    normed = (unit_field * gain).astype(bf16)
    weights_qkv = [qkv_ref[:, i * D : (i + 1) * D] for i in range(3)]
    w_proj = proj_ref[...]
    for ref, weight in zip((q_ref, k_ref, v_ref), weights_qkv):
        ref[...] = nn(normed, weight).astype(bf16).astype(f32)
    cot_low = g_ref[...].astype(bf16)
    ca_ref[...] = nt(cot_low, w_proj).astype(bf16).astype(f32)

    lane_head = lax.broadcasted_iota(jnp.int32, (CELLS, D), 1) // HEAD_DIM
    of_head = [lane_head == h for h in range(HEADS)]
    pad = jnp.zeros((LANES - CELLS, D), f32)

    def stacked(value):
        return jnp.concatenate([jnp.where(m, value, 0.0) for m in of_head], 0).astype(bf16)

    def gathered(value):
        total = jnp.where(of_head[0], value[:CELLS], 0.0)
        for h in range(1, HEADS):
            total = jnp.where(of_head[h], value[h * CELLS : (h + 1) * CELLS], total)
        return total

    first_band = lax.axis_index("lat") == 0
    query_low = lax.broadcasted_iota(jnp.int32, (CELLS, LANES), 0) < CELLS // 2
    key = lax.broadcasted_iota(jnp.int32, (CELLS, LANES), 1)
    apart = jnp.logical_and(query_low != (key < CELLS // 2), first_band)
    lane = lax.broadcasted_iota(jnp.int32, (STACK, LANES), 1)
    bias_grads = []
    for band in range(BANDS):
        for level in range(LEV):
            tables = []
            low = level * CELLS
            for h in range(HEADS):
                table = bias_ref[band, 0, h].astype(f32)[low : low + CELLS, low : low + CELLS]
                table = jnp.concatenate([table, jnp.full((CELLS, LANES - CELLS), padded_score, f32)], 1)
                if band == 0:
                    table = jnp.where(jnp.logical_and(apart, key < CELLS), masked_score, table)
                tables.append(table)
            table = jnp.concatenate(tables, 0)
            bias_grad = None
            for sector in range(SECTORS):
                base = window_of(band, level, sector) * CELLS
                part = slice(base, base + CELLS)
                queries = stacked(q_ref[part, :])
                key_part = jnp.concatenate([k_ref[part, :], pad], 0).astype(bf16)
                value_part = jnp.concatenate([v_ref[part, :], pad], 0).astype(bf16)
                scores = nt(queries, key_part) * score_scale + table
                exponent = jnp.exp(scores - jnp.max(scores, -1, keepdims=True))
                probability = exponent * (1.0 / jnp.sum(exponent, -1, keepdims=True))
                weights = probability.astype(bf16)
                att_ref[part, :] = gathered(nn(weights, value_part))
                cot_att = stacked(ca_ref[part, :])
                cot_weights = nt(cot_att, value_part)
                cv_ref[part, :] = tn(weights, cot_att)[:CELLS]
                inner = jnp.sum(cot_weights * probability, -1, keepdims=True)
                cot_scores = probability * (cot_weights - inner)
                bias_grad = cot_scores if bias_grad is None else bias_grad + cot_scores
                scaled = (cot_scores * score_scale).astype(bf16)
                cq_ref[part, :] = gathered(nn(scaled, key_part))
                ck_ref[part, :] = tn(scaled, queries)[:CELLS]
            bias_grads.append(bias_grad)
    left = [
        jnp.where(lane < 64, bias_grads[2 * b], pltpu.roll(bias_grads[2 * b + 1], 64, 1))
        for b in range(BANDS)
    ]
    lane3 = lane[: STACK // 3]
    rest = jnp.zeros((STACK // 3, LANES), f32)
    for g in range(3):
        for k in range(4):
            place = g * 32 + k * 8
            piece = bias_grads[k][g * (STACK // 3) : (g + 1) * (STACK // 3)]
            inside = jnp.logical_and(lane3 >= place, lane3 < place + 8)
            rest = jnp.where(inside, pltpu.roll(piece, (place - 64) % LANES, 1), rest)
    packed = jnp.concatenate([*left, rest, jnp.zeros((16, LANES), f32)], 0)
    bias_out_ref[...] = packed.reshape(16, 64, LANES)

    attended = att_ref[...].astype(bf16)
    branch = nn(attended, w_proj)
    grads = []
    cot_normed = None
    for ref, weight in zip((cq_ref, ck_ref, cv_ref), weights_qkv):
        cot_part = ref[...].astype(bf16)
        grads.append(tn(normed, cot_part))
        term = nt(cot_part, weight)
        cot_normed = term if cot_normed is None else cot_normed + term
    grads.append(tn(attended, cot_low))
    gain_part = jnp.sum(cot_normed * unit_field, 0, keepdims=True)
    x_ref[...] = branch
    g_ref[...] = norm_back(cot_normed, gain, unit_field, inverse)
    out_strips = {"lat": out_lat_ref, "lon": out_lon_ref, "cor": out_cor_ref}
    for band in range(BANDS):
        for level in range(LEV):
            initial = (level - LEV // 2) % LEV
            for sector in range(SECTORS):
                base = window_of(band, level, sector) * CELLS
                for row, col, count, source, line, start in pieces(band, sector):
                    at = base + row * WIN_LON + col
                    for array, (src, own) in enumerate(((x_ref, own_f_ref), (g_ref, own_c_ref))):
                        if source == "own":
                            own[initial, line, start : start + count, :] = src[at : at + count, :]
                        else:
                            dst = strip_row(source, array, initial, line, start)
                            out_strips[source][dst : dst + count, :] = src[at : at + count, :]
    tiles = [g[:, :LANES] for g in grads]
    tiles += [jnp.concatenate([grads[i][:, LANES:], grads[i + 1][:, LANES:]], 1) for i in (0, 2)]
    halves = [jnp.concatenate(tiles[3 * h : 3 * h + 3], 0).reshape(8, CELLS, LANES) for h in range(2)]
    two_halves(*halves, keep_ref, send_ref, (slice(None), slice(0, CELLS), slice(None)))
    gains = jnp.concatenate([gain_mlp_ref[...], gain_part], 0)
    right = jnp.concatenate([gains[:, LANES:], jnp.zeros((2, LANES - 64), f32)], 1)
    block = jnp.concatenate([gains[:, :LANES], right, jnp.zeros((4, LANES), f32)], 0)
    for ref in (keep_ref, send_ref):
        ref[:, CELLS : CELLS + 8, :] = jnp.broadcast_to(block[None], (8, 8, LANES))


def join_kernel(bias_ref, attn_ref, ff_ref, out_ref):
    attn = jnp.sum(attn_ref[...], 0)
    weights = jnp.concatenate(
        [attn[:CELLS], jnp.sum(ff_ref[...], 0), attn[CELLS:], jnp.zeros((32, LANES), f32)], 0
    )
    out_ref[:, :64, :] = bias_ref[...]
    out_ref[:, 64:, :] = weights.reshape(16, 16, LANES)


def total_kernel(in_ref, out_ref):
    out_ref[...] = jnp.broadcast_to(jnp.sum(in_ref[...], 0)[None], out_ref.shape)


def spread_kernel(in_ref, out_ref):
    weights = in_ref[:, 64:, :].reshape(256, LANES)[: 3 * CELLS]
    out_ref[...] = jnp.broadcast_to(weights[None], out_ref.shape)


def last_kernel(
    sums_ref, mine_ref, other_ref,
    gain_attn_ref, qkv_ref, proj_ref, bias_ref, gain_mlp_ref, up_ref, down_ref,
):
    packed = sums_ref[:, :64, :].reshape(1024, LANES)
    lane = lax.broadcasted_iota(jnp.int32, (STACK, LANES), 1)
    third = STACK // 3
    rest = packed[2 * STACK : 2 * STACK + third]
    zeros = jnp.zeros((CELLS, LANES), f32)
    for band in range(BANDS):
        for level in range(LEV):
            table = packed[band * STACK : (band + 1) * STACK]
            if level == 1:
                table = pltpu.roll(table, 64, 1)
            k = band * LEV + level
            tail = jnp.concatenate([pltpu.roll(rest, (64 - g * 32 - k * 8) % LANES, 1) for g in range(3)], 0)
            table = jnp.where(lane < 64, table, jnp.where(lane < CELLS, tail, 0.0))
            for h in range(HEADS):
                rows = jnp.concatenate([table[h * CELLS : (h + 1) * CELLS], zeros], 1)
                if level == 1:
                    rows = pltpu.roll(rows, CELLS, 1)
                bias_ref[band, 0, h, level * CELLS : (level + 1) * CELLS, :] = rows[:, : 2 * CELLS]
    gains = sums_ref[:, 64:, :].reshape(256, LANES)[3 * CELLS : 3 * CELLS + 8]
    gains = jnp.concatenate([gains[:2], gains[2:4, :64]], 1)
    gain_mlp_ref[...] = gains[0:1]
    gain_attn_ref[...] = gains[1:2]
    own = lax.rem(lax.axis_index("lat"), 2) == 0
    mine, other = mine_ref[...], other_ref[...]
    halves = [jnp.where(own, mine, other), jnp.where(own, other, mine)]

    def tiles_of(k):
        found = []
        for half in halves:
            rows = half[:, k * CELLS : (k + 1) * CELLS].reshape(8 * CELLS, LANES)
            found += [rows[t * D : (t + 1) * D] for t in range(3)]
        return found

    tiles = tiles_of(0)
    parts = [
        jnp.concatenate([tiles[i], tiles[4 + i // 2][:, 64 * (i % 2) : 64 * (i % 2) + 64]], 1)
        for i in range(4)
    ]
    qkv_ref[...] = jnp.concatenate(parts[:3], 1)
    proj_ref[...] = parts[3]
    up_ref[...] = jnp.concatenate(tiles_of(1), 1)
    for t, tile in enumerate(tiles_of(2)):
        down_ref[t * LANES : (t + 1) * LANES, :] = tile.T


def stream_kernel(
    first_ref, cot_second_ref, own_f_ref, own_c_ref, lat_ref, lon_ref, cor_ref,
    in_first_ref, grad_second_ref, cot_ref,
):
    cot_ref[...] = cot_second_ref[...].astype(f32)
    inner = (slice(None), slice(0, KEEP_R), slice(0, KEEP_C))
    in_first_ref[inner] = first_ref[inner] - own_f_ref[inner]
    grad_second_ref[inner] = cot_ref[inner] + own_c_ref[inner]

    def edge(level, row, cols, ref, place):
        count = cols.stop - cols.start
        at = place(0)
        in_first_ref[level, row, cols] = first_ref[level, row, cols] - ref[at : at + count, :]
        at = place(1)
        grad_second_ref[level, row, cols] = cot_ref[level, row, cols] + ref[at : at + count, :]

    for level in range(LEV):
        for row in range(HALF_LAT):
            edge(level, KEEP_R + row, slice(0, KEEP_C), lat_ref, lambda a: lat_row(a, level, row))
            edge(level, KEEP_R + row, slice(KEEP_C, COLS), cor_ref, lambda a: cor_row(a, level, row))
        for row in range(KEEP_R):
            edge(level, row, slice(KEEP_C, COLS), lon_ref, lambda a: lon_row(a, level, row))


def kernel(fn, out_shape, scratch=(), name=None, flops=0, nbytes=0):
    return pl.pallas_call(
        fn,
        out_shape=[jax.ShapeDtypeStruct(s, f32) for s in out_shape],
        scratch_shapes=[pltpu.VMEM(s, d) for s, d in scratch],
        compiler_params=pltpu.CompilerParams(vmem_limit_bytes=48 * 1024 * 1024),
        cost_estimate=pl.CostEstimate(flops=flops, bytes_accessed=nbytes, transcendentals=0),
        name=name,
    )


def body(
    out_first, out_second, cot_first, cot_second,
    gain_attn, w_qkv, w_proj, earth_bias, gain_mlp, w_up, w_down,
):
    lat_count, lon_count = lax.axis_size("lat"), lax.axis_size("lon")
    both = ("lat", "lon")
    shape = (LEV, ROWS, COLS, D)

    def halo(lat, lon, cor, by):
        ring = lambda n: [(i, (i + by) % n) for i in range(n)]
        diagonal = [
            (a * lon_count + o, ((a + by) % lat_count) * lon_count + (o + by) % lon_count)
            for a in range(lat_count)
            for o in range(lon_count)
        ]
        return (
            lax.ppermute(lat, "lat", ring(lat_count)),
            lax.ppermute(lon, "lon", ring(lon_count)),
            lax.ppermute(cor, both, diagonal),
        )

    def other_core(value):
        return lax.ppermute(value, "lat", [(i, i ^ 1) for i in range(lat_count)])

    same_core = [list(range(c, lat_count, 2)) for c in range(2)]

    def swap_lat(value):
        return lax.all_to_all(value, "lat", 0, 0, tiled=True, axis_index_groups=same_core)

    def swap_lon(value):
        return lax.all_to_all(value, "lon", 0, 0, tiled=True)

    strip_shapes = [(LAT_ROWS, D), (LON_ROWS, D), (COR_ROWS, D)]
    in_second, grad_first, lat, lon, cor, ff_keep, ff_send, gain_mlp_part = kernel(
        ff_kernel,
        [shape, shape, *strip_shapes, (8, 2 * CELLS, LANES), (8, 2 * CELLS, LANES), (1, D)],
        [((TOKENS, FF), bf16), ((TOKENS, FF), bf16), ((TOKENS, D), bf16)],
        "feedforward",
        flops=12 * TOKENS * D * FF,
        nbytes=6_000_000,
    )(out_first, out_second, cot_first, cot_second, gain_mlp.reshape(1, D), w_up, w_down)
    lat, lon, cor = halo(lat, lon, cor, 1)
    ff_parts = swap_lat(ff_keep + other_core(ff_send))
    own_f, own_c, lat, lon, cor, bias_part, at_keep, at_send = kernel(
        attention_kernel,
        [shape, shape, *strip_shapes, (16, 64, LANES), (8, CELLS + 8, LANES), (8, CELLS + 8, LANES)],
        [((TOKENS, D), f32)] * 10,
        "attention",
        flops=4_000_000_000,
        nbytes=6_000_000,
    )(
        in_second, grad_first, lat, lon, cor,
        earth_bias, gain_attn.reshape(1, D), w_qkv, w_proj, gain_mlp_part,
    )
    lat, lon, cor = halo(lat, lon, cor, -1)
    at_parts = swap_lat(at_keep + other_core(at_send))
    (joined,) = kernel(join_kernel, [(16, 80, LANES)], name="join")(bias_part, at_parts, ff_parts)
    (totals,) = kernel(total_kernel, [(16, 80, LANES)], name="total")(swap_lon(joined))
    sums = swap_lon(totals)
    (spread,) = kernel(spread_kernel, [(8, 3 * CELLS, LANES)], name="spread")(sums)
    mine = swap_lat(spread)
    other = other_core(mine)
    in_first, grad_second = kernel(
        stream_kernel, [shape, shape], [(shape, f32)], "streams", nbytes=3_000_000
    )(out_first, cot_second, own_f, own_c, lat, lon, cor)
    grad_gain_attn, grad_qkv, grad_proj, grad_bias, grad_gain_mlp, grad_up, grad_down = kernel(
        last_kernel,
        [(1, D), (D, 3 * D), (D, D), (BANDS, 1, HEADS, 2 * CELLS, 2 * CELLS), (1, D), (D, FF), (FF, D)],
        name="last",
        nbytes=6_000_000,
    )(sums, mine, other)
    return (
        in_first, in_second, grad_first, grad_second,
        grad_gain_attn.reshape(D), grad_qkv, grad_proj, grad_bias,
        grad_gain_mlp.reshape(D), grad_up, grad_down,
    )


def solution(mesh):
    field = P(None, "lat", "lon", None)
    placed = (field,) * 4 + (P(), P(), P(), P("lat", None, None, None, None), P(), P(), P())
    return jax.shard_map(body, mesh=mesh, in_specs=placed, out_specs=placed, check_vma=False)
```

time: 533 us -> 146 us (0.27)
  waiting for transfers between devices: 344 us -> 20.9 us
  matrix products: 36.2 us -> 0 us
  other arithmetic: 27.2 us -> 1.91 us
  starting transfers between devices: 6.78 us -> 24.4 us
  Pallas kernels: 0 us -> 14.1 us
  between operations: 14.7 us -> 0.76 us
  local copies, waits for them, and re-layouts: 23.7 us -> 10.7 us
    psum x2 -> x0, waiting for transfers between devices: 325 us -> none  [the longest x1 273 us: body(): lax.psum((gain_attn_part, qkv_part, proj_part, gain_mlp_part, up_part, do...]
    psum x1 -> x0, blocking collectives: 78.3 us -> none  [body(): lax.psum((gain_attn_part, qkv_part, proj_part, gain_mlp_part, up_part, do...]
    all_to_all x0 -> x4, blocking collectives: none -> 73 us  [the longest x2 46.1 us: swap_lon(): return lax.all_to_all(value, 'lon', 0, 0, tiled=True)]
    dot_general x17 -> x0, matrix products: 31.4 us -> none  [the longest x1 7.03 us: attention_pass(): jnp.einsum('blohwv,blovhe->blowhe', cot_scaled, key_part, preferred_eleme...]
    ppermute x4 -> x9, starting transfers between devices: 6.48 us -> 20.9 us  [the longest x3 9.52 us: other_core(): return lax.ppermute(value, 'lat', [(i, i ^ 1) for i in range(lat_count)])]
    pallas_call x0 -> x7, Pallas kernels: none -> 14.1 us  [the longest x1 7.03 us: body(): kernel(attention_kernel, [shape, shape, *strip_shapes, (16, 64, LANES), (...]
    sub x2 -> x0, other arithmetic: 7.52 us -> none  [the longest x1 7.45 us: attention_pass(): cot_weights - jnp.sum(cot_weights * probability, -1, keepdims=True)]
    concatenate x5 -> x0, other arithmetic: 5.49 us -> none  [the longest x2 2.42 us: latitude_step(): return jnp.concatenate([field[:, :, strip_rows:], received], axis=2)]
  transfers between devices with their start and end apart: 6 -> 10, of which waited for: 4 -> 5; matrix products, arithmetic and copies ran while one was open for 5% -> 1% of each run, Pallas kernels for 0% -> 1%
where the time goes in v1:
time: 146 us
  blocking collectives  73 us (50%)
  starting transfers between devices  24.4 us (17%)
  waiting for transfers between devices  20.9 us (14%)
  Pallas kernels  14.1 us (10%)
  local copies, waits for them, and re-layouts  10.7 us (7%)
  other arithmetic  1.91 us (1%)
    all_to_all x2, blocking collectives, swap_lon(): return lax.all_to_all(value, 'lon', 0, 0, tiled=True)  46.1 us
    all_to_all x2, blocking collectives, swap_lat(): lax.all_to_all(value, 'lat', 0, 0, tiled=True, axis_index_groups=same_core)  26.9 us
    ppermute x2, waiting for transfers between devices, halo(): lax.ppermute(cor, both, diagonal)  13.6 us
    unnamed x34, local copies, waits for them, and re-layouts  10.7 us
    ppermute x3, starting transfers between devices, other_core(): return lax.ppermute(value, 'lat', [(i, i ^ 1) for i in range(lat_count)])  9.52 us
    pallas_call x1, Pallas kernels, body(): kernel(attention_kernel, [shape, shape, *strip_shapes, (16, 64, LANES), (...  7.03 us
    all_to_all x1, waiting for transfers between devices, swap_lat(): lax.all_to_all(value, 'lat', 0, 0, tiled=True, axis_index_groups=same_core)  5.38 us
    ppermute x2, starting transfers between devices, halo(): lax.ppermute(lon, 'lon', ring(lon_count))  4.81 us
  transfers between devices with their start and end apart: 10, of which 5 were waited for; matrix products, arithmetic and copies ran while one was open for 1% of the time, Pallas kernels for 1%

profile of v1, /device:TPU:1, one launch (start us, length us, event | category | flops | bytes accessed | tf_op | source)
XLA Modules:
  0.0 145.7 jit_solution(18237567601358621066)
XLA Ops:
  0.6 1.1 copy.22.down_ref
  3.8 1.1 copy-done.5
  7.5 3.4 %feedforward.1 = (f32[2,12,24,192]{3,2,1,0:T(8,128)}, f32[2,12,24,192]{3,2,1,0:T(8,128)}, f32[216,192]{1,0:T(8,128)S(1)}, f32[216,192]{1,0:T(8,128)S(1)}, f32[72...) custom-call(f32[2,12,24,192]{3,2,1,0:T(8,128)S(1)} %copy-done, ...), custom_call_target="tpu_custom_call" | custom-call | flops 1019215872 | bytes 6000000 | tf_op jit(solution)/shard_map/feedforward/pallas_call | solution.py:433
  10.9 2.7 %collective-permute-start = (f32[216,192]{1,0:T(8,128)S(1)}, f32[216,192]{1,0:T(8,128)S(1)}, u32[]{:S(2)}, u32[]{:S(2)}) collective-permute-start(f32[216,192]{1,0:T(8,128)S(1)} %get-tuple-element.38), channel_id=1, source_target_pairs={{0,16},{16,32},{32,48},{48,64},{64,80},{80,96},{96,112},{112,128},... | collective-permute-start | bytes 497672 | tf_op jit(solution)/shard_map/ppermute | solution.py:416
  13.6 1.6 %collective-permute-start.1 = (f32[216,192]{1,0:T(8,128)S(1)}, f32[216,192]{1,0:T(8,128)S(1)}, u32[]{:S(2)}, u32[]{:S(2)}) collective-permute-start(f32[216,192]{1,0:T(8,128)S(1)} %get-tuple-element.39), channel_id=1, source_target_pairs={{0,1},{1,2},{2,3},{3,4},{4,5},{5,6},{6,7},{7,8},{8,9},{9,10},{10,1... | collective-permute-start | bytes 497672 | tf_op jit(solution)/shard_map/ppermute | solution.py:417
  15.2 1.6 %collective-permute-start.2 = (f32[72,192]{1,0:T(8,128)S(1)}, f32[72,192]{1,0:T(8,128)S(1)}, u32[]{:S(2)}, u32[]{:S(2)}) collective-permute-start(f32[72,192]{1,0:T(8,128)S(1)} %get-tuple-element.40), channel_id=1, source_target_pairs={{0,17},{1,18},{2,19},{3,20},{4,21},{5,22},{6,23},{7,24},{8,25},{9,... | collective-permute-start | bytes 165896 | tf_op jit(solution)/shard_map/ppermute | solution.py:418
  16.9 10.0 %collective-permute-done.2.cor_ref = f32[72,192]{1,0:T(8,128)S(1)} collective-permute-done((f32[72,192]{1,0:T(8,128)S(1)}, f32[72,192]{1,0:T(8,128)S(1)}, u32[]{:S(2)}, u32[]{:S(2)}) %collective-permute-start.2) | collective-permute-done | bytes 55328 | tf_op jit(solution)/shard_map/ppermute | solution.py:418
  29.3 7.0 %attention.1 = (f32[2,12,24,192]{3,2,1,0:T(8,128)S(1)}, f32[2,12,24,192]{3,2,1,0:T(8,128)S(1)}, f32[216,192]{1,0:T(8,128)S(1)}, f32[216,192]{1,0:T(8,128)S(1)}, ...) custom-call(f32[2,12,24,192]{3,2,1,0:T(8,128)S(1)} %copy-done.14, ...), custom_call_target="tpu_custom_call" | custom-call | flops 4000000000 | bytes 6000000 | tf_op jit(solution)/shard_map/attention/pallas_call | solution.py:443
  37.0 3.9 %collective-permute-start.6 = (f32[8,80,128]{2,1,0:T(8,128)S(1)}, f32[8,80,128]{2,1,0:T(8,128)S(1)}, u32[]{:S(2)}, u32[]{:S(2)}) collective-permute-start(f32[8,80,128]{2,1,0:T(8,128)S(1)} %get-tuple-element.51), channel_id=1, source_target_pairs={{0,16},{16,0},{32,48},{48,32},{64,80},{80,64},{96,112},{112,96},{1... | collective-permute-start | bytes 983048 | tf_op jit(solution)/shard_map/ppermute | solution.py:422
  40.8 1.7 %collective-permute-done.6 = f32[8,80,128]{2,1,0:T(8,128)S(1)} collective-permute-done((f32[8,80,128]{2,1,0:T(8,128)S(1)}, f32[8,80,128]{2,1,0:T(8,128)S(1)}, u32[]{:S(2)}, u32[]{:S(2)}) %collective-permute-start.6) | collective-permute-done | bytes 327712 | tf_op jit(solution)/shard_map/ppermute | solution.py:422
  43.3 3.4 %all-to-all-start = ((f32[8,80,128]{2,1,0:T(8,128)}), f32[8,80,128]{2,1,0:T(8,128)S(1)}, u32[]{:S(2)}, u32[]{:S(2)}) async-start(f32[8,80,128]{2,1,0:T(8,128)} %add.6), calls=%async_computation | async-start | bytes 655360 | tf_op jit(solution)/shard_map/all_to_all | solution.py:427
  46.8 1.1 add.7
  47.9 5.4 %all-to-all-done.attn_ref = f32[8,80,128]{2,1,0:T(8,128)S(1)} async-done(((f32[8,80,128]{2,1,0:T(8,128)}), f32[8,80,128]{2,1,0:T(8,128)S(1)}, u32[]{:S(2)}, u32[]{:S(2)}) %all-to-all-start) | async-done | bytes 327712 | tf_op jit(solution)/shard_map/all_to_all | solution.py:427
  53.3 13.9 %all_to_all.25.ff_ref = f32[8,144,128]{2,1,0:T(8,128)S(1)} all-to-all(f32[8,144,128]{2,1,0:T(8,128)S(1)} %add.7), channel_id=1, replica_groups={{0,32,64,96,128,160,192,224},{16,48,80,112,144,176,208,240},{1,33,65,97..., dimensions={0} | all-to-all | bytes 1179648 | tf_op jit(solution)/shard_map/all_to_all | solution.py:427
  67.2 22.4 %all_to_all.26.in_ref = f32[16,80,128]{2,1,0:T(8,128)S(1)} all-to-all(f32[16,80,128]{2,1,0:T(8,128)S(1)} %join.1), channel_id=1, replica_groups=mesh['lat'=16,'lon'=16] {'lon'}, dimensions={0} | all-to-all | bytes 1310720 | tf_op jit(solution)/shard_map/all_to_all | solution.py:430
  89.7 23.7 %all_to_all.27.in_ref.sums_ref = f32[16,80,128]{2,1,0:T(8,128)S(1)} all-to-all(f32[16,80,128]{2,1,0:T(8,128)S(1)} %total.1), channel_id=1, replica_groups=mesh['lat'=16,'lon'=16] {'lon'}, dimensions={0} | all-to-all | bytes 1310720 | tf_op jit(solution)/shard_map/all_to_all | solution.py:430
  113.5 13.0 %all_to_all.28.mine_ref = f32[8,216,128]{2,1,0:T(8,128)S(1)} all-to-all(f32[8,216,128]{2,1,0:T(8,128)S(1)} %spread.1), channel_id=1, replica_groups={{0,32,64,96,128,160,192,224},{16,48,80,112,144,176,208,240},{1,33,65,97..., dimensions={0} | all-to-all | bytes 1769472 | tf_op jit(solution)/shard_map/all_to_all | solution.py:427
  126.5 5.7 %collective-permute-start.8 = (f32[8,216,128]{2,1,0:T(8,128)S(1)}, f32[8,216,128]{2,1,0:T(8,128)S(1)}, u32[]{:S(2)}, u32[]{:S(2)}) collective-permute-start(f32[8,216,128]{2,1,0:T(8,128)S(1)} %all_to_all.28.mine_ref), channel_id=1, source_target_pairs={{0,16},{16,0},{32,48},{48,32},{64,80},{80,64},{96,112},{112,96},{1... | collective-permute-start | bytes 2654216 | tf_op jit(solution)/shard_map/ppermute | solution.py:422
  132.2 3.2 %collective-permute-start.4 = (f32[216,192]{1,0:T(8,128)S(1)}, f32[216,192]{1,0:T(8,128)S(1)}, u32[]{:S(2)}, u32[]{:S(2)}) collective-permute-start(f32[216,192]{1,0:T(8,128)S(1)} %get-tuple-element.45), channel_id=1, source_target_pairs={{0,15},{1,0},{2,1},{3,2},{4,3},{5,4},{6,5},{7,6},{8,7},{9,8},{10,9... | collective-permute-start | bytes 497672 | tf_op jit(solution)/shard_map/ppermute | solution.py:417
  135.3 2.3 %collective-permute-start.5 = (f32[72,192]{1,0:T(8,128)S(1)}, f32[72,192]{1,0:T(8,128)S(1)}, u32[]{:S(2)}, u32[]{:S(2)}) collective-permute-start(f32[72,192]{1,0:T(8,128)S(1)} %get-tuple-element.46), channel_id=1, source_target_pairs={{0,255},{1,240},{2,241},{3,242},{4,243},{5,244},{6,245},{7,246},{8... | collective-permute-start | bytes 165896 | tf_op jit(solution)/shard_map/ppermute | solution.py:418
  137.6 3.6 %collective-permute-done.5.cor_ref = f32[72,192]{1,0:T(8,128)S(1)} collective-permute-done((f32[72,192]{1,0:T(8,128)S(1)}, f32[72,192]{1,0:T(8,128)S(1)}, u32[]{:S(2)}, u32[]{:S(2)}) %collective-permute-start.5) | collective-permute-done | bytes 55328 | tf_op jit(solution)/shard_map/ppermute | solution.py:418
  141.2 1.2 streams.1
  142.4 2.2 %last.1 = (f32[1,192]{1,0:T(1,128)}, f32[192,576]{1,0:T(8,128)}, f32[192,192]{1,0:T(8,128)}, f32[2,1,6,144,144]{4,3,2,1,0:T(8,128)}, f32[1,192]{1,0:T(1,128)}, /...) custom-call(f32[16,80,128]{2,1,0:T(8,128)S(1)} %all_to_all.27.in_ref.sums_ref, f32[8,216,128]{2,1,0:T(8,128)S(1)} %all_to_all.28.mine_ref, ...), custom_call_target="tpu_custom_call" | custom-call | bytes 6000000 | tf_op jit(solution)/shard_map/last/pallas_call | solution.py:465
  144.7 1.1 copy.23
  (43 shorter events, 8.7 us)
Async XLA Ops:
  1.8 1.1 copy-start
  2.8 1.0 copy-start.2
  3.8 1.1 copy-start.5
  4.9 1.0 copy-start.6
  5.8 1.0 copy-start.7
  7.5 19.6 %copy-start.4 = (bf16[2,1,6,144,144]{4,3,2,1,0:T(8,128)(2,1)S(1)}, bf16[2,1,6,144,144]{4,3,2,1,0:T(8,128)(2,1)}, u32[]{:S(2)}) copy-start(bf16[2,1,6,144,144]{4,3,2,1,0:T(8,128)(2,1)} %bias_ref.1) | copy-start | bytes 1492996
  7.5 19.6 %copy-start.8 = (bf16[192,576]{1,0:T(8,128)(2,1)S(1)}, bf16[192,576]{1,0:T(8,128)(2,1)}, u32[]{:S(2)}) copy-start(bf16[192,576]{1,0:T(8,128)(2,1)} %qkv_ref.1) | copy-start | bytes 663556
  7.5 19.6 %copy-start.11 = (bf16[192,192]{1,0:T(8,128)(2,1)S(1)}, bf16[192,192]{1,0:T(8,128)(2,1)}, u32[]{:S(2)}) copy-start(bf16[192,192]{1,0:T(8,128)(2,1)} %proj_ref.1) | copy-start | bytes 221188
  7.5 19.6 %copy-start.13 = (f32[192]{0:T(256)S(1)}, f32[192]{0:T(256)}, u32[]{:S(2)}) copy-start(f32[192]{0:T(256)} %param.15) | copy-start | bytes 2308
  10.9 16.0 %collective-permute-start = (f32[216,192]{1,0:T(8,128)S(1)}, f32[216,192]{1,0:T(8,128)S(1)}, u32[]{:S(2)}, u32[]{:S(2)}) collective-permute-start(f32[216,192]{1,0:T(8,128)S(1)} %get-tuple-element.38), channel_id=1, source_target_pairs={{0,16},{16,32},{32,48},{48,64},{64,80},{80,96},{96,112},{112,128},... | collective-permute-start | bytes 497672 | tf_op jit(solution)/shard_map/ppermute | solution.py:416
  13.6 13.5 %collective-permute-start.1 = (f32[216,192]{1,0:T(8,128)S(1)}, f32[216,192]{1,0:T(8,128)S(1)}, u32[]{:S(2)}, u32[]{:S(2)}) collective-permute-start(f32[216,192]{1,0:T(8,128)S(1)} %get-tuple-element.39), channel_id=1, source_target_pairs={{0,1},{1,2},{2,3},{3,4},{4,5},{5,6},{6,7},{7,8},{8,9},{9,10},{10,1... | collective-permute-start | bytes 497672 | tf_op jit(solution)/shard_map/ppermute | solution.py:417
  15.2 11.7 %collective-permute-start.2 = (f32[72,192]{1,0:T(8,128)S(1)}, f32[72,192]{1,0:T(8,128)S(1)}, u32[]{:S(2)}, u32[]{:S(2)}) collective-permute-start(f32[72,192]{1,0:T(8,128)S(1)} %get-tuple-element.40), channel_id=1, source_target_pairs={{0,17},{1,18},{2,19},{3,20},{4,21},{5,22},{6,23},{7,24},{8,25},{9,... | collective-permute-start | bytes 165896 | tf_op jit(solution)/shard_map/ppermute | solution.py:418
  27.1 1.1 copy-start.14
  28.2 1.1 copy-start.15
  37.0 5.6 %collective-permute-start.6 = (f32[8,80,128]{2,1,0:T(8,128)S(1)}, f32[8,80,128]{2,1,0:T(8,128)S(1)}, u32[]{:S(2)}, u32[]{:S(2)}) collective-permute-start(f32[8,80,128]{2,1,0:T(8,128)S(1)} %get-tuple-element.51), channel_id=1, source_target_pairs={{0,16},{16,0},{32,48},{48,32},{64,80},{80,64},{96,112},{112,96},{1... | collective-permute-start | bytes 983048 | tf_op jit(solution)/shard_map/ppermute | solution.py:422
  40.8 5.9 %collective-permute-start.7 = (f32[8,144,128]{2,1,0:T(8,128)S(1)}, f32[8,144,128]{2,1,0:T(8,128)}, u32[]{:S(2)}, u32[]{:S(2)}) collective-permute-start(f32[8,144,128]{2,1,0:T(8,128)S(1)} %get-tuple-element.53), channel_id=1, source_target_pairs={{0,16},{16,0},{32,48},{48,32},{64,80},{80,64},{96,112},{112,96},{1... | collective-permute-start | bytes 1769480 | tf_op jit(solution)/shard_map/ppermute | solution.py:422
  43.3 10.0 %all-to-all-start = ((f32[8,80,128]{2,1,0:T(8,128)}), f32[8,80,128]{2,1,0:T(8,128)S(1)}, u32[]{:S(2)}, u32[]{:S(2)}) async-start(f32[8,80,128]{2,1,0:T(8,128)} %add.6), calls=%async_computation | async-start | bytes 655360 | tf_op jit(solution)/shard_map/all_to_all | solution.py:427
  113.4 18.8 %copy-start.10 = (f32[216,192]{1,0:T(8,128)S(1)}, f32[216,192]{1,0:T(8,128)}, u32[]{:S(2)}) copy-start(f32[216,192]{1,0:T(8,128)} %copy-done.9) | copy-start | bytes 497668
  113.4 27.8 %copy-start.1 = (f32[2,12,24,192]{3,2,1,0:T(8,128)S(1)}, f32[2,12,24,192]{3,2,1,0:T(8,128)}, u32[]{:S(2)}) copy-start(f32[2,12,24,192]{3,2,1,0:T(8,128)} %first_ref.3) | copy-start | bytes 1327108
  113.4 27.8 %copy-start.3 = (bf16[2,12,24,192]{3,2,1,0:T(8,128)(2,1)S(1)}, bf16[2,12,24,192]{3,2,1,0:T(8,128)(2,1)}, u32[]{:S(2)}) copy-start(bf16[2,12,24,192]{3,2,1,0:T(8,128)(2,1)} %cot_second_ref.3) | copy-start | bytes 663556
  126.5 15.9 %collective-permute-start.8 = (f32[8,216,128]{2,1,0:T(8,128)S(1)}, f32[8,216,128]{2,1,0:T(8,128)S(1)}, u32[]{:S(2)}, u32[]{:S(2)}) collective-permute-start(f32[8,216,128]{2,1,0:T(8,128)S(1)} %all_to_all.28.mine_ref), channel_id=1, source_target_pairs={{0,16},{16,0},{32,48},{48,32},{64,80},{80,64},{96,112},{112,96},{1... | collective-permute-start | bytes 2654216 | tf_op jit(solution)/shard_map/ppermute | solution.py:422
  132.2 9.0 %collective-permute-start.3 = (f32[216,192]{1,0:T(8,128)S(1)}, f32[216,192]{1,0:T(8,128)S(1)}, u32[]{:S(2)}, u32[]{:S(2)}) collective-permute-start(f32[216,192]{1,0:T(8,128)S(1)} %copy-done.10), channel_id=1, source_target_pairs={{0,240},{16,0},{32,16},{48,32},{64,48},{80,64},{96,80},{112,96},{1... | collective-permute-start | bytes 497672 | tf_op jit(solution)/shard_map/ppermute | solution.py:416
  132.2 9.0 %collective-permute-start.4 = (f32[216,192]{1,0:T(8,128)S(1)}, f32[216,192]{1,0:T(8,128)S(1)}, u32[]{:S(2)}, u32[]{:S(2)}) collective-permute-start(f32[216,192]{1,0:T(8,128)S(1)} %get-tuple-element.45), channel_id=1, source_target_pairs={{0,15},{1,0},{2,1},{3,2},{4,3},{5,4},{6,5},{7,6},{8,7},{9,8},{10,9... | collective-permute-start | bytes 497672 | tf_op jit(solution)/shard_map/ppermute | solution.py:417
  135.3 5.8 %collective-permute-start.5 = (f32[72,192]{1,0:T(8,128)S(1)}, f32[72,192]{1,0:T(8,128)S(1)}, u32[]{:S(2)}, u32[]{:S(2)}) collective-permute-start(f32[72,192]{1,0:T(8,128)S(1)} %get-tuple-element.46), channel_id=1, source_target_pairs={{0,255},{1,240},{2,241},{3,242},{4,243},{5,244},{6,245},{7,246},{8... | collective-permute-start | bytes 165896 | tf_op jit(solution)/shard_map/ppermute | solution.py:418
  (2 other events, 1.4 us)

commit v2 on v1

--- a/solution.py
+++ b/solution.py
@@ -1,5 +1,3 @@
-import functools
-
 import jax
 import jax.numpy as jnp
 from jax import lax
@@ -90,17 +88,26 @@
 
 
 def ff_kernel(
-    first_ref, second_ref, cot_first_ref, cot_second_ref, gain_ref, up_ref, down_ref,
-    in_second_ref, grad_first_ref, lat_ref, lon_ref, cor_ref, keep_ref, send_ref, gain_out_ref,
-    hidden_ref, cot_up_ref, normed_ref,
+    first_hbm, second_hbm, cot_first_hbm, cot_second_hbm, gain_ref, up_hbm, down_hbm,
+    in_second_hbm, grad_first_hbm, x_ref, g_ref, lat_ref, lon_ref, cor_ref, keep_ref, send_ref, gain_out_ref,
+    first_ref, second_ref, cot_first_ref, cot_second_ref, up_ref, down_ref,
+    in_second_ref, grad_first_ref, hidden_ref, cot_up_ref, normed_ref, in_sems, out_sems,
 ):
+    sources = (first_hbm, up_hbm, cot_second_hbm, down_hbm, second_hbm, cot_first_hbm)
+    targets = (first_ref, up_ref, cot_second_ref, down_ref, second_ref, cot_first_ref)
+    loads = [pltpu.make_async_copy(x, y, in_sems.at[i]) for i, (x, y) in enumerate(zip(sources, targets))]
+    for load in loads:
+        load.start()
+    loads[0].wait()
     tokens = first_ref[...].reshape(TOKENS, D)
     gain = gain_ref[...]
     unit_field, inverse = norm_parts(tokens)
     normed_ref[...] = (unit_field * gain).astype(bf16)
+    for load in loads[1:4]:
+        load.wait()
     cot = cot_second_ref[...].astype(f32).reshape(TOKENS, D).astype(bf16)
     w_up = up_ref[...]
-    w_down = down_ref[...]
+    w_down_t = down_ref[...]
     step = 96
     for i in range(TOKENS // step):
         part = pl.ds(i * step, step)
@@ -108,7 +115,7 @@
         square = up_proj * up_proj
         half = 0.5 * (1.0 + jnp.tanh(up_proj * (gelu_scale + gelu_scale * gelu_cubic * square)))
         hidden_ref[part, :] = (up_proj * half).astype(bf16)
-        cot_hidden = nt(cot[i * step : (i + 1) * step], w_down)
+        cot_hidden = nn(cot[i * step : (i + 1) * step], w_down_t)
         slope = half + (half * (1.0 - half)) * up_proj * (
             2.0 * gelu_scale + 6.0 * gelu_scale * gelu_cubic * square
         )
@@ -116,11 +123,19 @@
     hidden = hidden_ref[...]
     cot_up = cot_up_ref[...]
     shape = (LEV, ROWS, COLS, D)
-    in_second_ref[...] = second_ref[...] - nn(hidden, w_down).reshape(shape)
+    loads[4].wait()
+    in_second_ref[...] = second_ref[...] - nt(hidden, w_down_t).reshape(shape)
+    stores = [
+        pltpu.make_async_copy(in_second_ref, in_second_hbm, out_sems.at[0]),
+        pltpu.make_async_copy(grad_first_ref, grad_first_hbm, out_sems.at[1]),
+    ]
+    stores[0].start()
     cot_normed = nt(cot_up, w_up)
     gain_out_ref[...] = jnp.sum(cot_normed * unit_field, 0, keepdims=True)
     back = norm_back(cot_normed, gain, unit_field, inverse)
+    loads[5].wait()
     grad_first_ref[...] = cot_first_ref[...].astype(f32) + back.reshape(shape)
+    stores[1].start()
     for array, ref in enumerate((in_second_ref, grad_first_ref)):
         for level in range(LEV):
             for row in range(HALF_LAT):
@@ -131,12 +146,18 @@
             for row in range(KEEP_R):
                 at = lon_row(array, level, row)
                 lon_ref[at : at + HALF_LON, :] = ref[level, row, KEEP_C:COLS, :]
+    for at, count, source, level, line, start in all_pieces():
+        if source == "own":
+            x_ref[at : at + count, :] = in_second_ref[level, line, start : start + count, :]
+            g_ref[at : at + count, :] = grad_first_ref[level, line, start : start + count, :]
     grad_up = tn(normed_ref[...], cot_up)
     grad_down = tn(cot, hidden)
     for k, grad in enumerate((grad_up, grad_down)):
         tiles = [grad[:, t * LANES : (t + 1) * LANES] for t in range(6)]
         halves = [jnp.concatenate(tiles[3 * h : 3 * h + 3], 0).reshape(8, CELLS, LANES) for h in range(2)]
         two_halves(*halves, keep_ref, send_ref, (slice(None), slice(k * CELLS, (k + 1) * CELLS), slice(None)))
+    for store in stores:
+        store.wait()
 
 
 def window_of(band, level, sector):
@@ -160,26 +181,30 @@
     return place(array, level, line) + column
 
 
-def attention_kernel(
-    in_second_ref, grad_first_ref, lat_ref, lon_ref, cor_ref,
-    bias_ref, gain_ref, qkv_ref, proj_ref, gain_mlp_ref,
-    own_f_ref, own_c_ref, out_lat_ref, out_lon_ref, out_cor_ref, bias_out_ref, keep_ref, send_ref,
-    x_ref, g_ref, q_ref, k_ref, v_ref, ca_ref, att_ref, cq_ref, ck_ref, cv_ref,
-):
-    strips = {"lat": lat_ref, "lon": lon_ref, "cor": cor_ref}
+def all_pieces():
     for band in range(BANDS):
         for level in range(LEV):
             initial = (level - LEV // 2) % LEV
             for sector in range(SECTORS):
                 base = window_of(band, level, sector) * CELLS
                 for row, col, count, source, line, start in pieces(band, sector):
-                    at = base + row * WIN_LON + col
-                    for array, (dst, own) in enumerate(((x_ref, in_second_ref), (g_ref, grad_first_ref))):
-                        if source == "own":
-                            dst[at : at + count, :] = own[initial, line, start : start + count, :]
-                        else:
-                            src = strip_row(source, array, initial, line, start)
-                            dst[at : at + count, :] = strips[source][src : src + count, :]
+                    yield base + row * WIN_LON + col, count, source, initial, line, start
+
+
+def attention_kernel(
+    x_in_ref, g_in_ref, lat_ref, lon_ref, cor_ref,
+    bias_ref, gain_ref, qkv_ref, proj_ref, gain_mlp_ref,
+    win_f_ref, win_c_ref, out_lat_ref, out_lon_ref, out_cor_ref, bias_out_ref, keep_ref, send_ref,
+    x_ref, g_ref, q_ref, k_ref, v_ref, ca_ref, att_ref, cq_ref, ck_ref, cv_ref,
+):
+    strips = {"lat": lat_ref, "lon": lon_ref, "cor": cor_ref}
+    for at, count, source, level, line, start in all_pieces():
+        for array, (dst, own) in enumerate(((x_ref, x_in_ref), (g_ref, g_in_ref))):
+            if source == "own":
+                dst[at : at + count, :] = own[at : at + count, :]
+            else:
+                src = strip_row(source, array, level, line, start)
+                dst[at : at + count, :] = strips[source][src : src + count, :]
     gain = gain_ref[...]
     unit_field, inverse = norm_parts(x_ref[...])
     normed = (unit_field * gain).astype(bf16)
@@ -268,22 +293,14 @@
         cot_normed = term if cot_normed is None else cot_normed + term
     grads.append(tn(attended, cot_low))
     gain_part = jnp.sum(cot_normed * unit_field, 0, keepdims=True)
-    x_ref[...] = branch
-    g_ref[...] = norm_back(cot_normed, gain, unit_field, inverse)
+    win_f_ref[...] = branch
+    win_c_ref[...] = norm_back(cot_normed, gain, unit_field, inverse)
     out_strips = {"lat": out_lat_ref, "lon": out_lon_ref, "cor": out_cor_ref}
-    for band in range(BANDS):
-        for level in range(LEV):
-            initial = (level - LEV // 2) % LEV
-            for sector in range(SECTORS):
-                base = window_of(band, level, sector) * CELLS
-                for row, col, count, source, line, start in pieces(band, sector):
-                    at = base + row * WIN_LON + col
-                    for array, (src, own) in enumerate(((x_ref, own_f_ref), (g_ref, own_c_ref))):
-                        if source == "own":
-                            own[initial, line, start : start + count, :] = src[at : at + count, :]
-                        else:
-                            dst = strip_row(source, array, initial, line, start)
-                            out_strips[source][dst : dst + count, :] = src[at : at + count, :]
+    for at, count, source, level, line, start in all_pieces():
+        if source != "own":
+            for array, src in enumerate((win_f_ref, win_c_ref)):
+                dst = strip_row(source, array, level, line, start)
+                out_strips[source][dst : dst + count, :] = src[at : at + count, :]
     tiles = [g[:, :LANES] for g in grads]
     tiles += [jnp.concatenate([grads[i][:, LANES:], grads[i + 1][:, LANES:]], 1) for i in (0, 2)]
     halves = [jnp.concatenate(tiles[3 * h : 3 * h + 3], 0).reshape(8, CELLS, LANES) for h in range(2)]
@@ -292,13 +309,26 @@
     right = jnp.concatenate([gains[:, LANES:], jnp.zeros((2, LANES - 64), f32)], 1)
     block = jnp.concatenate([gains[:, :LANES], right, jnp.zeros((4, LANES), f32)], 0)
     for ref in (keep_ref, send_ref):
-        ref[:, CELLS : CELLS + 8, :] = jnp.broadcast_to(block[None], (8, 8, LANES))
-
-
-def join_kernel(bias_ref, attn_ref, ff_ref, out_ref):
-    attn = jnp.sum(attn_ref[...], 0)
+        ref[:, CELLS:, :] = jnp.broadcast_to(block[None], (8, 8, LANES))
+
+
+def add_kernel(a_ref, b_ref, out_ref):
+    out_ref[...] = a_ref[...] + b_ref[...]
+
+
+def lat_bit(k):
+    return lax.rem(lax.axis_index("lat") // (1 << k), 2)
+
+
+def lat_join_kernel(keep_ref, recv_ref, ff_ref, out_ref):
+    out_ref[:, : CELLS + 8, :] = keep_ref[...] + recv_ref[...]
+    out_ref[:, CELLS + 8 :, :] = ff_ref[...]
+
+
+def lon_join_kernel(bias_ref, parts_ref, out_ref):
+    total = jnp.sum(parts_ref[...], 0)
     weights = jnp.concatenate(
-        [attn[:CELLS], jnp.sum(ff_ref[...], 0), attn[CELLS:], jnp.zeros((32, LANES), f32)], 0
+        [total[:CELLS], total[CELLS + 8 :], total[CELLS : CELLS + 8], jnp.zeros((32, LANES), f32)], 0
     )
     out_ref[:, :64, :] = bias_ref[...]
     out_ref[:, 64:, :] = weights.reshape(16, 16, LANES)
@@ -308,15 +338,13 @@
     out_ref[...] = jnp.broadcast_to(jnp.sum(in_ref[...], 0)[None], out_ref.shape)
 
 
-def spread_kernel(in_ref, out_ref):
-    weights = in_ref[:, 64:, :].reshape(256, LANES)[: 3 * CELLS]
-    out_ref[...] = jnp.broadcast_to(weights[None], out_ref.shape)
-
-
-def last_kernel(
-    sums_ref, mine_ref, other_ref,
-    gain_attn_ref, qkv_ref, proj_ref, bias_ref, gain_mlp_ref, up_ref, down_ref,
-):
+def spread_kernel(in_ref, out_ref, gains_ref):
+    weights = in_ref[:, 64:, :].reshape(256, LANES)
+    out_ref[...] = jnp.broadcast_to(weights[None, : 3 * CELLS], out_ref.shape)
+    gains_ref[...] = weights[3 * CELLS : 3 * CELLS + 8]
+
+
+def bias_kernel(sums_ref, bias_ref):
     packed = sums_ref[:, :64, :].reshape(1024, LANES)
     lane = lax.broadcasted_iota(jnp.int32, (STACK, LANES), 1)
     third = STACK // 3
@@ -335,11 +363,17 @@
                 if level == 1:
                     rows = pltpu.roll(rows, CELLS, 1)
                 bias_ref[band, 0, h, level * CELLS : (level + 1) * CELLS, :] = rows[:, : 2 * CELLS]
-    gains = sums_ref[:, 64:, :].reshape(256, LANES)[3 * CELLS : 3 * CELLS + 8]
+
+
+def last_kernel(
+    gains_in_ref, mine_ref, other_ref,
+    gain_attn_ref, qkv_ref, proj_ref, gain_mlp_ref, up_ref, down_ref,
+):
+    gains = gains_in_ref[...]
     gains = jnp.concatenate([gains[:2], gains[2:4, :64]], 1)
     gain_mlp_ref[...] = gains[0:1]
     gain_attn_ref[...] = gains[1:2]
-    own = lax.rem(lax.axis_index("lat"), 2) == 0
+    own = lat_bit(0) == 0
     mine, other = mine_ref[...], other_ref[...]
     halves = [jnp.where(own, mine, other), jnp.where(own, other, mine)]
 
@@ -358,43 +392,53 @@
     qkv_ref[...] = jnp.concatenate(parts[:3], 1)
     proj_ref[...] = parts[3]
     up_ref[...] = jnp.concatenate(tiles_of(1), 1)
-    for t, tile in enumerate(tiles_of(2)):
-        down_ref[t * LANES : (t + 1) * LANES, :] = tile.T
+    down_ref[...] = jnp.concatenate(tiles_of(2), 1)
 
 
 def stream_kernel(
-    first_ref, cot_second_ref, own_f_ref, own_c_ref, lat_ref, lon_ref, cor_ref,
+    first_ref, cot_second_ref, win_f_ref, win_c_ref, lat_ref, lon_ref, cor_ref,
     in_first_ref, grad_second_ref, cot_ref,
 ):
     cot_ref[...] = cot_second_ref[...].astype(f32)
-    inner = (slice(None), slice(0, KEEP_R), slice(0, KEEP_C))
-    in_first_ref[inner] = first_ref[inner] - own_f_ref[inner]
-    grad_second_ref[inner] = cot_ref[inner] + own_c_ref[inner]
-
-    def edge(level, row, cols, ref, place):
-        count = cols.stop - cols.start
-        at = place(0)
-        in_first_ref[level, row, cols] = first_ref[level, row, cols] - ref[at : at + count, :]
-        at = place(1)
-        grad_second_ref[level, row, cols] = cot_ref[level, row, cols] + ref[at : at + count, :]
-
-    for level in range(LEV):
-        for row in range(HALF_LAT):
-            edge(level, KEEP_R + row, slice(0, KEEP_C), lat_ref, lambda a: lat_row(a, level, row))
-            edge(level, KEEP_R + row, slice(KEEP_C, COLS), cor_ref, lambda a: cor_row(a, level, row))
-        for row in range(KEEP_R):
-            edge(level, row, slice(KEEP_C, COLS), lon_ref, lambda a: lon_row(a, level, row))
-
-
-def kernel(fn, out_shape, scratch=(), name=None, flops=0, nbytes=0):
-    return pl.pallas_call(
-        fn,
-        out_shape=[jax.ShapeDtypeStruct(s, f32) for s in out_shape],
-        scratch_shapes=[pltpu.VMEM(s, d) for s, d in scratch],
-        compiler_params=pltpu.CompilerParams(vmem_limit_bytes=48 * 1024 * 1024),
-        cost_estimate=pl.CostEstimate(flops=flops, bytes_accessed=nbytes, transcendentals=0),
-        name=name,
-    )
+    strips = {"lat": lat_ref, "lon": lon_ref, "cor": cor_ref}
+    for at, count, source, level, line, start in all_pieces():
+        if source == "own":
+            f_part, c_part = (ref[at : at + count, :] for ref in (win_f_ref, win_c_ref))
+            row, col = line, start
+        else:
+            row = line + (0 if source == "lon" else KEEP_R)
+            col = start + (0 if source == "lat" else KEEP_C)
+            at_f, at_c = (strip_row(source, array, level, line, start) for array in range(2))
+            f_part, c_part = (strips[source][p : p + count, :] for p in (at_f, at_c))
+        spot = (level, row, slice(col, col + count))
+        in_first_ref[spot] = first_ref[spot] - f_part
+        grad_second_ref[spot] = cot_ref[spot] + c_part
+
+
+def kernel(fn, out_shape, scratch=(), name=None, flops=0, nbytes=0, in_hbm=(), out_hbm=()):
+    def spec(far):
+        return pl.BlockSpec(memory_space=pltpu.HBM if far else pltpu.VMEM)
+
+    def in_specs(count):
+        return [spec(i in in_hbm) for i in range(count)]
+
+    def call(*args):
+        args = [
+            pltpu.with_memory_space_constraint(x, pltpu.HBM) if i in in_hbm else x
+            for i, x in enumerate(args)
+        ]
+        return pl.pallas_call(
+            fn,
+            out_shape=[jax.ShapeDtypeStruct(s, f32) for s in out_shape],
+            in_specs=in_specs(len(args)),
+            out_specs=[spec(i in out_hbm) for i in range(len(out_shape))],
+            scratch_shapes=[s if not isinstance(s, tuple) else pltpu.VMEM(*s) for s in scratch],
+            compiler_params=pltpu.CompilerParams(vmem_limit_bytes=32 * 1024 * 1024),
+            cost_estimate=pl.CostEstimate(flops=flops, bytes_accessed=nbytes, transcendentals=0),
+            name=name,
+        )(*args)
+
+    return call
 
 
 def body(
@@ -418,9 +462,6 @@
             lax.ppermute(cor, both, diagonal),
         )
 
-    def other_core(value):
-        return lax.ppermute(value, "lat", [(i, i ^ 1) for i in range(lat_count)])
-
     same_core = [list(range(c, lat_count, 2)) for c in range(2)]
 
     def swap_lat(value):
@@ -429,49 +470,67 @@
     def swap_lon(value):
         return lax.all_to_all(value, "lon", 0, 0, tiled=True)
 
+    def across(value, bit):
+        return lax.ppermute(value, "lat", [(i, i ^ (1 << bit)) for i in range(lat_count)])
+
     strip_shapes = [(LAT_ROWS, D), (LON_ROWS, D), (COR_ROWS, D)]
-    in_second, grad_first, lat, lon, cor, ff_keep, ff_send, gain_mlp_part = kernel(
+    win = (TOKENS, D)
+    ff_half = (8, 2 * CELLS, LANES)
+    in_second, grad_first, x_win, g_win, lat, lon, cor, ff_keep, ff_send, gain_mlp_part = kernel(
         ff_kernel,
-        [shape, shape, *strip_shapes, (8, 2 * CELLS, LANES), (8, 2 * CELLS, LANES), (1, D)],
-        [((TOKENS, FF), bf16), ((TOKENS, FF), bf16), ((TOKENS, D), bf16)],
+        [shape, shape, win, win, *strip_shapes, ff_half, ff_half, (1, D)],
+        [
+            (shape, f32), (shape, f32), (shape, bf16), (shape, bf16), ((D, FF), bf16), ((D, FF), bf16),
+            (shape, f32), (shape, f32), ((TOKENS, FF), bf16), ((TOKENS, FF), bf16), ((TOKENS, D), bf16),
+            pltpu.SemaphoreType.DMA((6,)), pltpu.SemaphoreType.DMA((2,)),
+        ],
         "feedforward",
         flops=12 * TOKENS * D * FF,
         nbytes=6_000_000,
-    )(out_first, out_second, cot_first, cot_second, gain_mlp.reshape(1, D), w_up, w_down)
+        in_hbm=(0, 1, 2, 3, 5, 6),
+        out_hbm=(0, 1),
+    )(out_first, out_second, cot_first, cot_second, gain_mlp.reshape(1, D), w_up, w_down.T)
     lat, lon, cor = halo(lat, lon, cor, 1)
-    ff_parts = swap_lat(ff_keep + other_core(ff_send))
-    own_f, own_c, lat, lon, cor, bias_part, at_keep, at_send = kernel(
+    (ff_sum,) = kernel(add_kernel, [ff_half], name="pair")(ff_keep, across(ff_send, 0))
+    x_win, ff_sum = lax.optimization_barrier((x_win, ff_sum))
+    at_half = (8, CELLS + 8, LANES)
+    win_f, win_c, lat, lon, cor, bias_part, keep, send = kernel(
         attention_kernel,
-        [shape, shape, *strip_shapes, (16, 64, LANES), (8, CELLS + 8, LANES), (8, CELLS + 8, LANES)],
-        [((TOKENS, D), f32)] * 10,
+        [win, win, *strip_shapes, (16, 64, LANES), at_half, at_half],
+        [(win, f32)] * 10,
         "attention",
-        flops=4_000_000_000,
-        nbytes=6_000_000,
+        flops=16_000_000_000,
+        nbytes=16_000_000,
     )(
-        in_second, grad_first, lat, lon, cor,
+        x_win, g_win, lat, lon, cor,
         earth_bias, gain_attn.reshape(1, D), w_qkv, w_proj, gain_mlp_part,
     )
     lat, lon, cor = halo(lat, lon, cor, -1)
-    at_parts = swap_lat(at_keep + other_core(at_send))
-    (joined,) = kernel(join_kernel, [(16, 80, LANES)], name="join")(bias_part, at_parts, ff_parts)
+    (parts,) = kernel(lat_join_kernel, [(8, 3 * CELLS + 8, LANES)], name="latjoin")(
+        keep, across(send, 0), ff_sum
+    )
+    parts = swap_lat(parts)
+    parts, lat, lon, cor = lax.optimization_barrier((parts, lat, lon, cor))
+    (joined,) = kernel(lon_join_kernel, [(16, 80, LANES)], name="lonjoin")(bias_part, parts)
     (totals,) = kernel(total_kernel, [(16, 80, LANES)], name="total")(swap_lon(joined))
     sums = swap_lon(totals)
-    (spread,) = kernel(spread_kernel, [(8, 3 * CELLS, LANES)], name="spread")(sums)
+    spread, gains = kernel(spread_kernel, [(8, 3 * CELLS, LANES), (8, LANES)], name="spread")(sums)
     mine = swap_lat(spread)
-    other = other_core(mine)
+    other = across(mine, 0)
     in_first, grad_second = kernel(
-        stream_kernel, [shape, shape], [(shape, f32)], "streams", nbytes=3_000_000
-    )(out_first, cot_second, own_f, own_c, lat, lon, cor)
-    grad_gain_attn, grad_qkv, grad_proj, grad_bias, grad_gain_mlp, grad_up, grad_down = kernel(
+        stream_kernel, [shape, shape], [(shape, f32)], "streams", nbytes=3_000_000, flops=2_000_000_000
+    )(out_first, cot_second, win_f, win_c, lat, lon, cor)
+    (grad_bias,) = kernel(bias_kernel, [(BANDS, 1, HEADS, 2 * CELLS, 2 * CELLS)], name="bias")(sums)
+    grad_gain_attn, grad_qkv, grad_proj, grad_gain_mlp, grad_up, grad_down = kernel(
         last_kernel,
-        [(1, D), (D, 3 * D), (D, D), (BANDS, 1, HEADS, 2 * CELLS, 2 * CELLS), (1, D), (D, FF), (FF, D)],
+        [(1, D), (D, 3 * D), (D, D), (1, D), (D, FF), (D, FF)],
         name="last",
         nbytes=6_000_000,
-    )(sums, mine, other)
+    )(gains, mine, other)
     return (
         in_first, in_second, grad_first, grad_second,
         grad_gain_attn.reshape(D), grad_qkv, grad_proj, grad_bias,
-        grad_gain_mlp.reshape(D), grad_up, grad_down,
+        grad_gain_mlp.reshape(D), grad_up, grad_down.T,
     )
 
 

time: 146 us -> 130 us (0.89)
  local copies, waits for them, and re-layouts: 10.7 us -> 1.53 us
  blocking collectives: 73 us -> 64.1 us
  Pallas kernels: 14.1 us -> 17.7 us
  other arithmetic: 1.91 us -> 0 us
    unnamed x34 -> x18, local copies, waits for them, and re-layouts: 10.7 us -> 1.53 us
    all_to_all x2 -> x1, blocking collectives: 26.9 us -> 18.1 us  [swap_lat(): lax.all_to_all(value, 'lat', 0, 0, tiled=True, axis_index_groups=same_core)]
    all_to_all x1, waiting for transfers between devices: 5.38 us -> 0.01 us  [swap_lat(): lax.all_to_all(value, 'lat', 0, 0, tiled=True, axis_index_groups=same_core)]
    ppermute x2, waiting for transfers between devices: 0.01 us -> 4.75 us  [halo(): lax.ppermute(lat, 'lat', ring(lat_count))]
    pallas_call x7 -> x10, Pallas kernels: 14.1 us -> 17.7 us  [call(): pl.pallas_call(fn, out_shape=[jax.ShapeDtypeStruct(s, f32) for s in out_s...]
    ppermute x2, starting transfers between devices: 3.89 us -> 6.4 us  [halo(): lax.ppermute(cor, both, diagonal)]
    ppermute x2, starting transfers between devices: 2.69 us -> 0.45 us  [halo(): lax.ppermute(lat, 'lat', ring(lat_count))]
    ppermute x2, starting transfers between devices: 4.81 us -> 2.75 us  [halo(): lax.ppermute(lon, 'lon', ring(lon_count))]
  transfers between devices with their start and end apart: 10 -> 10, of which waited for: 5 -> 4; matrix products, arithmetic and copies ran while one was open for 1% -> 0% of each run, Pallas kernels for 1% -> 2%
where the time goes in v2:
time: 130 us
  blocking collectives  64.1 us (49%)
  starting transfers between devices  24.6 us (19%)
  waiting for transfers between devices  20.8 us (16%)
  Pallas kernels  17.7 us (14%)
  local copies, waits for them, and re-layouts  1.53 us (1%)
    all_to_all x2, blocking collectives, swap_lon(): return lax.all_to_all(value, 'lon', 0, 0, tiled=True)  46.1 us
    all_to_all x1, blocking collectives, swap_lat(): lax.all_to_all(value, 'lat', 0, 0, tiled=True, axis_index_groups=same_core)  18.1 us
    pallas_call x10, Pallas kernels, call(): pl.pallas_call(fn, out_shape=[jax.ShapeDtypeStruct(s, f32) for s in out_s...  17.7 us
    ppermute x2, waiting for transfers between devices, halo(): lax.ppermute(cor, both, diagonal)  14.8 us
    ppermute x3, starting transfers between devices, across(): lax.ppermute(value, 'lat', [(i, i ^ 1 << bit) for i in range(lat_count)])  11.5 us
    ppermute x2, starting transfers between devices, halo(): lax.ppermute(cor, both, diagonal)  6.4 us
    ppermute x2, waiting for transfers between devices, halo(): lax.ppermute(lat, 'lat', ring(lat_count))  4.75 us
    all_to_all x1, starting transfers between devices, swap_lat(): lax.all_to_all(value, 'lat', 0, 0, tiled=True, axis_index_groups=same_core)  3.55 us
  transfers between devices with their start and end apart: 10, of which 4 were waited for; matrix products, arithmetic and copies ran while one was open for 0% of the time, Pallas kernels for 2%

profile of v2, /device:TPU:1, one launch (start us, length us, event | category | flops | bytes accessed | tf_op | source)
XLA Modules:
  0.0 129.6 jit_solution(2892086398824389070)
XLA Ops:
  0.7 0.7 copy-done.5
  1.3 4.9 %feedforward.1 = (f32[2,12,24,192]{3,2,1,0:T(8,128)}, f32[2,12,24,192]{3,2,1,0:T(8,128)}, f32[576,192]{1,0:T(8,128)S(1)}, f32[576,192]{1,0:T(8,128)S(1)}, f32[21...) custom-call(f32[2,12,24,192]{3,2,1,0:T(8,128)} %first_ref.1, ...), custom_call_target="tpu_custom_call" | custom-call | flops 1019215872 | bytes 6000000 | tf_op jit(solution)/shard_map/feedforward/pallas_call | solution.py:430
  6.3 3.3 %collective-permute-start = (f32[8,144,128]{2,1,0:T(8,128)S(1)}, f32[8,144,128]{2,1,0:T(8,128)S(1)}, u32[]{:S(2)}, u32[]{:S(2)}) collective-permute-start(f32[8,144,128]{2,1,0:T(8,128)S(1)} %get-tuple-element.47), channel_id=1, source_target_pairs={{0,16},{16,0},{32,48},{48,32},{64,80},{80,64},{96,112},{112,96},{1... | collective-permute-start | bytes 1769480 | tf_op jit(solution)/shard_map/ppermute | solution.py:474
  9.7 1.2 collective-permute-start.2
  10.8 2.1 %collective-permute-start.3 = (f32[72,192]{1,0:T(8,128)S(1)}, f32[72,192]{1,0:T(8,128)S(1)}, u32[]{:S(2)}, u32[]{:S(2)}) collective-permute-start(f32[72,192]{1,0:T(8,128)S(1)} %get-tuple-element.52), channel_id=1, source_target_pairs={{0,17},{1,18},{2,19},{3,20},{4,21},{5,22},{6,23},{7,24},{8,25},{9,... | collective-permute-start | bytes 165896 | tf_op jit(solution)/shard_map/ppermute | solution.py:462
  13.0 10.4 %collective-permute-done.3.cor_ref = f32[72,192]{1,0:T(8,128)S(1)} collective-permute-done((f32[72,192]{1,0:T(8,128)S(1)}, f32[72,192]{1,0:T(8,128)S(1)}, u32[]{:S(2)}, u32[]{:S(2)}) %collective-permute-start.3) | collective-permute-done | bytes 55328 | tf_op jit(solution)/shard_map/ppermute | solution.py:462
  23.4 6.9 %attention.1 = (f32[576,192]{1,0:T(8,128)S(1)}, f32[576,192]{1,0:T(8,128)S(1)}, f32[216,192]{1,0:T(8,128)S(1)}, f32[216,192]{1,0:T(8,128)S(1)}, f32[72,192]{1,0:...) custom-call(f32[576,192]{1,0:T(8,128)S(1)} %get-tuple-element.48.x_in_ref, ...), custom_call_target="tpu_custom_call" | custom-call | flops 16000000000 | bytes 16000000 | tf_op jit(solution)/shard_map/attention/pallas_call | solution.py:430
  30.4 0.8 copy-done.7
  31.2 2.9 %collective-permute-start.4 = (f32[8,80,128]{2,1,0:T(8,128)S(1)}, f32[8,80,128]{2,1,0:T(8,128)S(1)}, u32[]{:S(2)}, u32[]{:S(2)}) collective-permute-start(f32[8,80,128]{2,1,0:T(8,128)S(1)} %get-tuple-element.57), channel_id=1, source_target_pairs={{0,16},{16,0},{32,48},{48,32},{64,80},{80,64},{96,112},{112,96},{1... | collective-permute-start | bytes 983048 | tf_op jit(solution)/shard_map/ppermute | solution.py:474
  34.1 1.3 collective-permute-done.4.recv_ref
  35.4 1.0 latjoin.1
  36.4 3.6 %all-to-all-start = ((f32[8,224,128]{2,1,0:T(8,128)}), f32[8,224,128]{2,1,0:T(8,128)S(1)}, u32[]{:S(2)}, u32[]{:S(2)}) async-start(f32[8,224,128]{2,1,0:T(8,128)} %latjoin.1), calls=%async_computation | async-start | bytes 1835008 | tf_op jit(solution)/shard_map/all_to_all | solution.py:468
  39.9 0.5 collective-permute-start.5
  40.4 1.6 %collective-permute-start.6 = (f32[216,192]{1,0:T(8,128)S(1)}, f32[216,192]{1,0:T(8,128)S(1)}, u32[]{:S(2)}, u32[]{:S(2)}) collective-permute-start(f32[216,192]{1,0:T(8,128)S(1)} %get-tuple-element.60), channel_id=1, source_target_pairs={{0,15},{1,0},{2,1},{3,2},{4,3},{5,4},{6,5},{7,6},{8,7},{9,8},{10,9... | collective-permute-start | bytes 497672 | tf_op jit(solution)/shard_map/ppermute | solution.py:461
  42.0 4.3 %collective-permute-start.7 = (f32[72,192]{1,0:T(8,128)S(1)}, f32[72,192]{1,0:T(8,128)S(1)}, u32[]{:S(2)}, u32[]{:S(2)}) collective-permute-start(f32[72,192]{1,0:T(8,128)S(1)} %get-tuple-element.61), channel_id=1, source_target_pairs={{0,255},{1,240},{2,241},{3,242},{4,243},{5,244},{6,245},{7,246},{8... | collective-permute-start | bytes 165896 | tf_op jit(solution)/shard_map/ppermute | solution.py:462
  46.3 4.4 %collective-permute-done.7.cor_ref = f32[72,192]{1,0:T(8,128)S(1)} collective-permute-done((f32[72,192]{1,0:T(8,128)S(1)}, f32[72,192]{1,0:T(8,128)S(1)}, u32[]{:S(2)}, u32[]{:S(2)}) %collective-permute-start.7) | collective-permute-done | bytes 55328 | tf_op jit(solution)/shard_map/ppermute | solution.py:462
  50.7 4.7 %collective-permute-done.5.lat_ref = f32[216,192]{1,0:T(8,128)S(1)} collective-permute-done((f32[216,192]{1,0:T(8,128)S(1)}, f32[216,192]{1,0:T(8,128)S(1)}, u32[]{:S(2)}, u32[]{:S(2)}) %collective-permute-start.5) | collective-permute-done | bytes 165920 | tf_op jit(solution)/shard_map/ppermute | solution.py:460
  55.5 22.6 %all_to_all.20.in_ref = f32[16,80,128]{2,1,0:T(8,128)S(1)} all-to-all(f32[16,80,128]{2,1,0:T(8,128)S(1)} %lonjoin.1), channel_id=1, replica_groups=mesh['lat'=16,'lon'=16] {'lon'}, dimensions={0} | all-to-all | bytes 1310720 | tf_op jit(solution)/shard_map/all_to_all | solution.py:471
  78.2 23.5 %all_to_all.21.in_ref.sums_ref = f32[16,80,128]{2,1,0:T(8,128)S(1)} all-to-all(f32[16,80,128]{2,1,0:T(8,128)S(1)} %total.1), channel_id=1, replica_groups=mesh['lat'=16,'lon'=16] {'lon'}, dimensions={0} | all-to-all | bytes 1310720 | tf_op jit(solution)/shard_map/all_to_all | solution.py:471
  101.8 18.1 %all_to_all.22.mine_ref = f32[8,216,128]{2,1,0:T(8,128)S(1)} all-to-all(f32[8,216,128]{2,1,0:T(8,128)S(1)} %get-tuple-element.72), channel_id=1, replica_groups={{0,32,64,96,128,160,192,224},{16,48,80,112,144,176,208,240},{1,33,65,97..., dimensions={0} | all-to-all | bytes 1769472 | tf_op jit(solution)/shard_map/all_to_all | solution.py:468
  119.8 5.2 %collective-permute-start.8 = (f32[8,216,128]{2,1,0:T(8,128)S(1)}, f32[8,216,128]{2,1,0:T(8,128)S(1)}, u32[]{:S(2)}, u32[]{:S(2)}) collective-permute-start(f32[8,216,128]{2,1,0:T(8,128)S(1)} %all_to_all.22.mine_ref), channel_id=1, source_target_pairs={{0,16},{16,0},{32,48},{48,32},{64,80},{80,64},{96,112},{112,96},{1... | collective-permute-start | bytes 2654216 | tf_op jit(solution)/shard_map/ppermute | solution.py:474
  125.1 1.3 %streams.1 = (f32[2,12,24,192]{3,2,1,0:T(8,128)}, f32[2,12,24,192]{3,2,1,0:T(8,128)}) custom-call(f32[2,12,24,192]{3,2,1,0:T(8,128)S(1)} %copy-done.1, bf16[2,12,24,192]{3,2,1,0:T(8,128)(2,1)S(1)} %copy-done.2, f32[576,192]{1,0:T(8,128)S(1)} %get-tuple-element.54.win_f_ref, f32[576,192]{1,0:T(8,128)S(1)} %copy-done.8, ...), custom_call_target="tpu_custom_call" | custom-call | flops 2000000000 | bytes 3000000 | tf_op jit(solution)/shard_map/streams/pallas_call | solution.py:430
  126.4 1.8 %bias.1 = f32[2,1,6,144,144]{4,3,2,1,0:T(8,128)} custom-call(f32[16,80,128]{2,1,0:T(8,128)S(1)} %all_to_all.21.in_ref.sums_ref), custom_call_target="tpu_custom_call" | custom-call | tf_op jit(solution)/shard_map/bias/pallas_call | solution.py:430
  128.2 1.4 %last.1 = (f32[1,192]{1,0:T(1,128)}, f32[192,576]{1,0:T(8,128)}, f32[192,192]{1,0:T(8,128)}, f32[1,192]{1,0:T(1,128)}, f32[192,768]{1,0:T(8,128)}, /*index=5*/f32[192,768]{1,0:T(8,128)}) custom-call(f32[8,128]{1,0:T(8,128)S(1)} %get-tuple-element.71.gains_in_ref, f32[8,216,128]{2,1,0:T(8,128)S(1)} %all_to_all.22.mine_ref, ...), custom_call_target="tpu_custom_call" | custom-call | bytes 6000000 | tf_op jit(solution)/shard_map/last/pallas_call | solution.py:430
  (27 shorter events, 0.4 us)
Async XLA Ops:
  0.6 0.7 copy-start.5
  6.3 17.1 %copy-start = (bf16[2,1,6,144,144]{4,3,2,1,0:T(8,128)(2,1)S(1)}, bf16[2,1,6,144,144]{4,3,2,1,0:T(8,128)(2,1)}, u32[]{:S(2)}) copy-start(bf16[2,1,6,144,144]{4,3,2,1,0:T(8,128)(2,1)} %bias_ref.1) | copy-start | bytes 1492996
  6.3 17.1 %copy-start.3 = (bf16[192,576]{1,0:T(8,128)(2,1)S(1)}, bf16[192,576]{1,0:T(8,128)(2,1)}, u32[]{:S(2)}) copy-start(bf16[192,576]{1,0:T(8,128)(2,1)} %qkv_ref.1) | copy-start | bytes 663556
  6.3 17.1 %copy-start.4 = (bf16[192,192]{1,0:T(8,128)(2,1)S(1)}, bf16[192,192]{1,0:T(8,128)(2,1)}, u32[]{:S(2)}) copy-start(bf16[192,192]{1,0:T(8,128)(2,1)} %proj_ref.1) | copy-start | bytes 221188
  6.3 17.1 %copy-start.6 = (f32[192]{0:T(256)S(1)}, f32[192]{0:T(256)}, u32[]{:S(2)}) copy-start(f32[192]{0:T(256)} %param.15) | copy-start | bytes 2308
  6.3 6.6 %collective-permute-start = (f32[8,144,128]{2,1,0:T(8,128)S(1)}, f32[8,144,128]{2,1,0:T(8,128)S(1)}, u32[]{:S(2)}, u32[]{:S(2)}) collective-permute-start(f32[8,144,128]{2,1,0:T(8,128)S(1)} %get-tuple-element.47), channel_id=1, source_target_pairs={{0,16},{16,0},{32,48},{48,32},{64,80},{80,64},{96,112},{112,96},{1... | collective-permute-start | bytes 1769480 | tf_op jit(solution)/shard_map/ppermute | solution.py:474
  9.6 13.7 %collective-permute-start.1 = (f32[216,192]{1,0:T(8,128)S(1)}, f32[216,192]{1,0:T(8,128)S(1)}, u32[]{:S(2)}, u32[]{:S(2)}) collective-permute-start(f32[216,192]{1,0:T(8,128)S(1)} %get-tuple-element.50), channel_id=1, source_target_pairs={{0,16},{16,32},{32,48},{48,64},{64,80},{80,96},{96,112},{112,128},... | collective-permute-start | bytes 497672 | tf_op jit(solution)/shard_map/ppermute | solution.py:460
  9.7 13.7 %collective-permute-start.2 = (f32[216,192]{1,0:T(8,128)S(1)}, f32[216,192]{1,0:T(8,128)S(1)}, u32[]{:S(2)}, u32[]{:S(2)}) collective-permute-start(f32[216,192]{1,0:T(8,128)S(1)} %get-tuple-element.51), channel_id=1, source_target_pairs={{0,1},{1,2},{2,3},{3,4},{4,5},{5,6},{6,7},{7,8},{8,9},{9,10},{10,1... | collective-permute-start | bytes 497672 | tf_op jit(solution)/shard_map/ppermute | solution.py:461
  10.8 12.6 %collective-permute-start.3 = (f32[72,192]{1,0:T(8,128)S(1)}, f32[72,192]{1,0:T(8,128)S(1)}, u32[]{:S(2)}, u32[]{:S(2)}) collective-permute-start(f32[72,192]{1,0:T(8,128)S(1)} %get-tuple-element.52), channel_id=1, source_target_pairs={{0,17},{1,18},{2,19},{3,20},{4,21},{5,22},{6,23},{7,24},{8,25},{9,... | collective-permute-start | bytes 165896 | tf_op jit(solution)/shard_map/ppermute | solution.py:462
  30.4 0.8 copy-start.7
  31.2 4.2 %collective-permute-start.4 = (f32[8,80,128]{2,1,0:T(8,128)S(1)}, f32[8,80,128]{2,1,0:T(8,128)S(1)}, u32[]{:S(2)}, u32[]{:S(2)}) collective-permute-start(f32[8,80,128]{2,1,0:T(8,128)S(1)} %get-tuple-element.57), channel_id=1, source_target_pairs={{0,16},{16,0},{32,48},{48,32},{64,80},{80,64},{96,112},{112,96},{1... | collective-permute-start | bytes 983048 | tf_op jit(solution)/shard_map/ppermute | solution.py:474
  36.4 19.1 %all-to-all-start = ((f32[8,224,128]{2,1,0:T(8,128)}), f32[8,224,128]{2,1,0:T(8,128)S(1)}, u32[]{:S(2)}, u32[]{:S(2)}) async-start(f32[8,224,128]{2,1,0:T(8,128)} %latjoin.1), calls=%async_computation | async-start | bytes 1835008 | tf_op jit(solution)/shard_map/all_to_all | solution.py:468
  39.9 15.5 %collective-permute-start.5 = (f32[216,192]{1,0:T(8,128)S(1)}, f32[216,192]{1,0:T(8,128)S(1)}, u32[]{:S(2)}, u32[]{:S(2)}) collective-permute-start(f32[216,192]{1,0:T(8,128)S(1)} %get-tuple-element.59), channel_id=1, source_target_pairs={{0,240},{16,0},{32,16},{48,32},{64,48},{80,64},{96,80},{112,96},{1... | collective-permute-start | bytes 497672 | tf_op jit(solution)/shard_map/ppermute | solution.py:460
  40.4 15.1 %collective-permute-start.6 = (f32[216,192]{1,0:T(8,128)S(1)}, f32[216,192]{1,0:T(8,128)S(1)}, u32[]{:S(2)}, u32[]{:S(2)}) collective-permute-start(f32[216,192]{1,0:T(8,128)S(1)} %get-tuple-element.60), channel_id=1, source_target_pairs={{0,15},{1,0},{2,1},{3,2},{4,3},{5,4},{6,5},{7,6},{8,7},{9,8},{10,9... | collective-permute-start | bytes 497672 | tf_op jit(solution)/shard_map/ppermute | solution.py:461
  42.0 8.7 %collective-permute-start.7 = (f32[72,192]{1,0:T(8,128)S(1)}, f32[72,192]{1,0:T(8,128)S(1)}, u32[]{:S(2)}, u32[]{:S(2)}) collective-permute-start(f32[72,192]{1,0:T(8,128)S(1)} %get-tuple-element.61), channel_id=1, source_target_pairs={{0,255},{1,240},{2,241},{3,242},{4,243},{5,244},{6,245},{7,246},{8... | collective-permute-start | bytes 165896 | tf_op jit(solution)/shard_map/ppermute | solution.py:462
  78.2 46.9 %copy-start.1 = (f32[2,12,24,192]{3,2,1,0:T(8,128)S(1)}, f32[2,12,24,192]{3,2,1,0:T(8,128)}, u32[]{:S(2)}) copy-start(f32[2,12,24,192]{3,2,1,0:T(8,128)} %first_ref.1) | copy-start | bytes 1327108
  78.2 46.9 %copy-start.2 = (bf16[2,12,24,192]{3,2,1,0:T(8,128)(2,1)S(1)}, bf16[2,12,24,192]{3,2,1,0:T(8,128)(2,1)}, u32[]{:S(2)}) copy-start(bf16[2,12,24,192]{3,2,1,0:T(8,128)(2,1)} %cot_second_ref.1) | copy-start | bytes 663556
  78.2 46.9 %copy-start.8 = (f32[576,192]{1,0:T(8,128)S(1)}, f32[576,192]{1,0:T(8,128)}, u32[]{:S(2)}) copy-start(f32[576,192]{1,0:T(8,128)} %copy-done.7) | copy-start | bytes 1327108
  119.8 8.3 %collective-permute-start.8 = (f32[8,216,128]{2,1,0:T(8,128)S(1)}, f32[8,216,128]{2,1,0:T(8,128)S(1)}, u32[]{:S(2)}, u32[]{:S(2)}) collective-permute-start(f32[8,216,128]{2,1,0:T(8,128)S(1)} %all_to_all.22.mine_ref), channel_id=1, source_target_pairs={{0,16},{16,0},{32,48},{48,32},{64,80},{80,64},{96,112},{112,96},{1... | collective-permute-start | bytes 2654216 | tf_op jit(solution)/shard_map/ppermute | solution.py:474

commit v3 on v2

--- a/solution.py
+++ b/solution.py
@@ -1,3 +1,5 @@
+import functools
+
 import jax
 import jax.numpy as jnp
 from jax import lax
@@ -14,6 +16,8 @@
 WIN_LON = 12
 CELLS = WIN_LAT * WIN_LON
 BANDS = 2
+CHIPS = 16
+PART = 3 * 192 // 16
 SECTORS = 2
 ROWS = BANDS * WIN_LAT
 COLS = SECTORS * WIN_LON
@@ -62,10 +66,13 @@
     )
 
 
-def two_halves(first, second, keep_ref, send_ref, where):
-    mine = lax.rem(lax.axis_index("lat"), 2) == 0
-    keep_ref[where] = jnp.where(mine, first, second)
-    send_ref[where] = jnp.where(mine, second, first)
+def half_at(by):
+    x = lax.axis_index("lon") // 8 * 2 + lax.axis_index("lat") // 8
+    return lax.rem(x + by, 4) // 2
+
+
+def lat_bit(k):
+    return lax.rem(lax.axis_index("lat") // (1 << k), 2)
 
 
 def lat_row(array, level, row):
@@ -88,17 +95,19 @@
 
 
 def ff_kernel(
-    first_hbm, second_hbm, cot_first_hbm, cot_second_hbm, gain_ref, up_hbm, down_hbm,
-    in_second_hbm, grad_first_hbm, x_ref, g_ref, lat_ref, lon_ref, cor_ref, keep_ref, send_ref, gain_out_ref,
+    first_hbm, second_hbm, cot_first_hbm, cot_second_hbm, gain_hbm, up_hbm, down_hbm,
+    in_second_hbm, grad_first_hbm, x_ref, g_ref, lat_ref, lon_ref, cor_ref, gain_out_ref,
+    hidden_ref, cot_up_ref, normed_ref, cot_ref,
     first_ref, second_ref, cot_first_ref, cot_second_ref, up_ref, down_ref,
-    in_second_ref, grad_first_ref, hidden_ref, cot_up_ref, normed_ref, in_sems, out_sems,
+    in_second_ref, grad_first_ref, gain_ref, in_sems, out_sems,
 ):
-    sources = (first_hbm, up_hbm, cot_second_hbm, down_hbm, second_hbm, cot_first_hbm)
-    targets = (first_ref, up_ref, cot_second_ref, down_ref, second_ref, cot_first_ref)
+    sources = (first_hbm, up_hbm, cot_second_hbm, down_hbm, second_hbm, cot_first_hbm, gain_hbm)
+    targets = (first_ref, up_ref, cot_second_ref, down_ref, second_ref, cot_first_ref, gain_ref)
     loads = [pltpu.make_async_copy(x, y, in_sems.at[i]) for i, (x, y) in enumerate(zip(sources, targets))]
     for load in loads:
         load.start()
     loads[0].wait()
+    loads[6].wait()
     tokens = first_ref[...].reshape(TOKENS, D)
     gain = gain_ref[...]
     unit_field, inverse = norm_parts(tokens)
@@ -106,6 +115,7 @@
     for load in loads[1:4]:
         load.wait()
     cot = cot_second_ref[...].astype(f32).reshape(TOKENS, D).astype(bf16)
+    cot_ref[...] = cot
     w_up = up_ref[...]
     w_down_t = down_ref[...]
     step = 96
@@ -150,14 +160,22 @@
         if source == "own":
             x_ref[at : at + count, :] = in_second_ref[level, line, start : start + count, :]
             g_ref[at : at + count, :] = grad_first_ref[level, line, start : start + count, :]
-    grad_up = tn(normed_ref[...], cot_up)
-    grad_down = tn(cot, hidden)
+    for store in stores:
+        store.wait()
+
+
+def ff_grads_kernel(normed_ref, cot_up_ref, cot_ref, hidden_ref, keep_ref, send_ref):
+    grad_up = tn(normed_ref[...], cot_up_ref[...])
+    grad_down = tn(cot_ref[...], hidden_ref[...])
     for k, grad in enumerate((grad_up, grad_down)):
         tiles = [grad[:, t * LANES : (t + 1) * LANES] for t in range(6)]
-        halves = [jnp.concatenate(tiles[3 * h : 3 * h + 3], 0).reshape(8, CELLS, LANES) for h in range(2)]
-        two_halves(*halves, keep_ref, send_ref, (slice(None), slice(k * CELLS, (k + 1) * CELLS), slice(None)))
-    for store in stores:
-        store.wait()
+        halves = [jnp.concatenate(tiles[3 * h : 3 * h + 3], 0) for h in range(2)]
+        mine = lat_bit(0) == 0
+        kept = jnp.where(mine, halves[0], halves[1])
+        sent = jnp.where(mine, halves[1], halves[0])
+        for j in range(CHIPS):
+            keep_ref[j, k * PART : (k + 1) * PART, :] = kept[j * PART : (j + 1) * PART]
+            send_ref[j, k * PART : (k + 1) * PART, :] = sent[j * PART : (j + 1) * PART]
 
 
 def window_of(band, level, sector):
@@ -193,9 +211,9 @@
 
 def attention_kernel(
     x_in_ref, g_in_ref, lat_ref, lon_ref, cor_ref,
-    bias_ref, gain_ref, qkv_ref, proj_ref, gain_mlp_ref,
-    win_f_ref, win_c_ref, out_lat_ref, out_lon_ref, out_cor_ref, bias_out_ref, keep_ref, send_ref,
-    x_ref, g_ref, q_ref, k_ref, v_ref, ca_ref, att_ref, cq_ref, ck_ref, cv_ref,
+    bias_ref, gain_ref, qkv_ref, proj_ref,
+    bias_keep_ref, bias_send_ref, x_ref, normed_ref, cot_low_ref, att16_ref, cq16_ref, ck16_ref, cv16_ref,
+    g_ref, q_ref, k_ref, v_ref, ca_ref, att_ref, cq_ref, ck_ref, cv_ref,
 ):
     strips = {"lat": lat_ref, "lon": lon_ref, "cor": cor_ref}
     for at, count, source, level, line, start in all_pieces():
@@ -280,72 +298,109 @@
             inside = jnp.logical_and(lane3 >= place, lane3 < place + 8)
             rest = jnp.where(inside, pltpu.roll(piece, (place - 64) % LANES, 1), rest)
     packed = jnp.concatenate([*left, rest, jnp.zeros((16, LANES), f32)], 0)
-    bias_out_ref[...] = packed.reshape(16, 64, LANES)
-
-    attended = att_ref[...].astype(bf16)
-    branch = nn(attended, w_proj)
+    packed = packed.reshape(2, 8, 64, LANES)
+    for by, ref in ((1, bias_keep_ref), (3, bias_send_ref)):
+        ref[...] = jnp.where(half_at(by) == 0, packed[0], packed[1])
+
+    normed_ref[...] = normed
+    cot_low_ref[...] = cot_low
+    for src, dst in ((att_ref, att16_ref), (cq_ref, cq16_ref), (ck_ref, ck16_ref), (cv_ref, cv16_ref)):
+        dst[...] = src[...].astype(bf16)
+
+
+def attention_grads_kernel(
+    x_ref, normed_ref, cot_low_ref, att16_ref, cq_ref, ck_ref, cv_ref, qkv_ref, gain_mlp_ref,
+    keep_ref, send_ref, cot_normed_ref,
+):
+    unit_field, _ = norm_parts(x_ref[...])
+    normed = normed_ref[...]
     grads = []
     cot_normed = None
-    for ref, weight in zip((cq_ref, ck_ref, cv_ref), weights_qkv):
-        cot_part = ref[...].astype(bf16)
+    for i, ref in enumerate((cq_ref, ck_ref, cv_ref)):
+        weight = qkv_ref[:, i * D : (i + 1) * D]
+        cot_part = ref[...]
         grads.append(tn(normed, cot_part))
         term = nt(cot_part, weight)
         cot_normed = term if cot_normed is None else cot_normed + term
-    grads.append(tn(attended, cot_low))
+    grads.append(tn(att16_ref[...], cot_low_ref[...]))
     gain_part = jnp.sum(cot_normed * unit_field, 0, keepdims=True)
-    win_f_ref[...] = branch
-    win_c_ref[...] = norm_back(cot_normed, gain, unit_field, inverse)
+    cot_normed_ref[...] = cot_normed
+    tiles = [g[:, :LANES] for g in grads]
+    tiles += [jnp.concatenate([grads[i][:, LANES:], grads[i + 1][:, LANES:]], 1) for i in (0, 2)]
+    halves = [jnp.concatenate(tiles[3 * h : 3 * h + 3], 0) for h in range(2)]
+    mine = lat_bit(0) == 0
+    kept = jnp.where(mine, halves[0], halves[1])
+    sent = jnp.where(mine, halves[1], halves[0])
+    gains = jnp.concatenate([gain_mlp_ref[...], gain_part], 0)
+    right = jnp.concatenate([gains[:, LANES:], jnp.zeros((2, LANES - 64), f32)], 1)
+    block = jnp.concatenate([gains[:, :LANES], right], 0)
+    for ref, half in ((keep_ref, kept), (send_ref, sent)):
+        for j in range(CHIPS):
+            ref[j, :PART, :] = half[j * PART : (j + 1) * PART]
+            ref[j, PART:, :] = block
+
+
+def return_kernel(
+    x_ref, att16_ref, cot_normed_ref, gain_ref, proj_ref,
+    win_f_hbm, win_c_hbm, out_lat_ref, out_lon_ref, out_cor_ref,
+    win_f_ref, win_c_ref, sems,
+):
+    win_f_ref[...] = nn(att16_ref[...], proj_ref[...])
+    unit_field, inverse = norm_parts(x_ref[...])
+    win_c_ref[...] = norm_back(cot_normed_ref[...], gain_ref[...], unit_field, inverse)
+    stores = [
+        pltpu.make_async_copy(win_f_ref, win_f_hbm, sems.at[0]),
+        pltpu.make_async_copy(win_c_ref, win_c_hbm, sems.at[1]),
+    ]
+    for store in stores:
+        store.start()
     out_strips = {"lat": out_lat_ref, "lon": out_lon_ref, "cor": out_cor_ref}
     for at, count, source, level, line, start in all_pieces():
         if source != "own":
             for array, src in enumerate((win_f_ref, win_c_ref)):
                 dst = strip_row(source, array, level, line, start)
                 out_strips[source][dst : dst + count, :] = src[at : at + count, :]
-    tiles = [g[:, :LANES] for g in grads]
-    tiles += [jnp.concatenate([grads[i][:, LANES:], grads[i + 1][:, LANES:]], 1) for i in (0, 2)]
-    halves = [jnp.concatenate(tiles[3 * h : 3 * h + 3], 0).reshape(8, CELLS, LANES) for h in range(2)]
-    two_halves(*halves, keep_ref, send_ref, (slice(None), slice(0, CELLS), slice(None)))
-    gains = jnp.concatenate([gain_mlp_ref[...], gain_part], 0)
-    right = jnp.concatenate([gains[:, LANES:], jnp.zeros((2, LANES - 64), f32)], 1)
-    block = jnp.concatenate([gains[:, :LANES], right, jnp.zeros((4, LANES), f32)], 0)
-    for ref in (keep_ref, send_ref):
-        ref[:, CELLS:, :] = jnp.broadcast_to(block[None], (8, 8, LANES))
-
-
-def add_kernel(a_ref, b_ref, out_ref):
-    out_ref[...] = a_ref[...] + b_ref[...]
-
-
-def lat_bit(k):
-    return lax.rem(lax.axis_index("lat") // (1 << k), 2)
-
-
-def lat_join_kernel(keep_ref, recv_ref, ff_ref, out_ref):
-    out_ref[:, : CELLS + 8, :] = keep_ref[...] + recv_ref[...]
-    out_ref[:, CELLS + 8 :, :] = ff_ref[...]
-
-
-def lon_join_kernel(bias_ref, parts_ref, out_ref):
-    total = jnp.sum(parts_ref[...], 0)
+    for store in stores:
+        store.wait()
+
+
+def halve_kernel(bit, keep_ref, recv_ref, keep_out_ref, send_out_ref):
+    total = keep_ref[...] + recv_ref[...]
+    inner = {"x_low": 4, "y_low": 1, "y_high": 1, "x_high": 1}[bit]
+    total = total.reshape(-1, 2, inner, *total.shape[1:])
+    low, high = (total[:, i].reshape(keep_out_ref.shape) for i in range(2))
+    own = {"x_low": lambda: lat_bit(3), "y_low": lambda: lat_bit(1), "y_high": lambda: lat_bit(2),
+           "x_high": lambda: lax.axis_index("lon") // 8}[bit]()
+    keep_out_ref[...] = jnp.where(own == 0, low, high)
+    send_out_ref[...] = jnp.where(own == 0, high, low)
+
+
+def xy_join_kernel(keep_ref, recv_ref, out_ref):
+    out_ref[...] = keep_ref[...] + recv_ref[...]
+
+
+def z_join_kernel(bias_ref, recv_ref, parts_ref, ff_ref, ff_recv_ref, out_ref):
     weights = jnp.concatenate(
-        [total[:CELLS], total[CELLS + 8 :], total[CELLS : CELLS + 8], jnp.zeros((32, LANES), f32)], 0
+        [ff_ref[0] + ff_recv_ref[0], jnp.sum(parts_ref[...], 0), jnp.zeros((16, LANES), f32)], 0
     )
-    out_ref[:, :64, :] = bias_ref[...]
-    out_ref[:, 64:, :] = weights.reshape(16, 16, LANES)
+    out_ref[:, :64, :] = bias_ref[...] + recv_ref[...]
+    out_ref[:, 64:, :] = weights.reshape(8, 16, LANES)
 
 
 def total_kernel(in_ref, out_ref):
     out_ref[...] = jnp.broadcast_to(jnp.sum(in_ref[...], 0)[None], out_ref.shape)
 
 
-def spread_kernel(in_ref, out_ref, gains_ref):
-    weights = in_ref[:, 64:, :].reshape(256, LANES)
-    out_ref[...] = jnp.broadcast_to(weights[None, : 3 * CELLS], out_ref.shape)
-    gains_ref[...] = weights[3 * CELLS : 3 * CELLS + 8]
-
-
-def bias_kernel(sums_ref, bias_ref):
-    packed = sums_ref[:, :64, :].reshape(1024, LANES)
+def spread_kernel(in_ref, out_ref, bias_ref):
+    weights = in_ref[:, 64:, :].reshape(128, LANES)
+    out_ref[...] = jnp.broadcast_to(weights[None, : 3 * PART + 4], out_ref.shape)
+    bias_ref[...] = in_ref[:, :64, :]
+
+
+def bias_kernel(next_ref, before_ref, bias_ref):
+    first = half_at(1) == 0
+    after, before = (ref[...].reshape(512, LANES) for ref in (next_ref, before_ref))
+    packed = jnp.concatenate([jnp.where(first, after, before), jnp.where(first, before, after)], 0)
     lane = lax.broadcasted_iota(jnp.int32, (STACK, LANES), 1)
     third = STACK // 3
     rest = packed[2 * STACK : 2 * STACK + third]
@@ -366,40 +421,48 @@
 
 
 def last_kernel(
-    gains_in_ref, mine_ref, other_ref,
-    gain_attn_ref, qkv_ref, proj_ref, gain_mlp_ref, up_ref, down_ref,
+    mine_ref, other_ref,
+    gain_attn_ref, qkv_ref, proj_ref, gain_mlp_ref, up_ref, down_ref, rows_ref,
 ):
-    gains = gains_in_ref[...]
+    gains = mine_ref[0, 3 * PART :, :]
     gains = jnp.concatenate([gains[:2], gains[2:4, :64]], 1)
     gain_mlp_ref[...] = gains[0:1]
     gain_attn_ref[...] = gains[1:2]
     own = lat_bit(0) == 0
-    mine, other = mine_ref[...], other_ref[...]
-    halves = [jnp.where(own, mine, other), jnp.where(own, other, mine)]
 
     def tiles_of(k):
         found = []
-        for half in halves:
-            rows = half[:, k * CELLS : (k + 1) * CELLS].reshape(8 * CELLS, LANES)
-            found += [rows[t * D : (t + 1) * D] for t in range(3)]
+        for low in (True, False):
+            for j in range(CHIPS):
+                mine, other = (ref[j, k * PART : (k + 1) * PART, :] for ref in (mine_ref, other_ref))
+                rows_ref[j * PART : (j + 1) * PART, :] = jnp.where(own, mine, other) if low else jnp.where(own, other, mine)
+            found += [rows_ref[t * D : (t + 1) * D, :] for t in range(3)]
         return found
 
-    tiles = tiles_of(0)
+    tiles = tiles_of(2)
     parts = [
         jnp.concatenate([tiles[i], tiles[4 + i // 2][:, 64 * (i % 2) : 64 * (i % 2) + 64]], 1)
         for i in range(4)
     ]
     qkv_ref[...] = jnp.concatenate(parts[:3], 1)
     proj_ref[...] = parts[3]
-    up_ref[...] = jnp.concatenate(tiles_of(1), 1)
-    down_ref[...] = jnp.concatenate(tiles_of(2), 1)
+    up_ref[...] = jnp.concatenate(tiles_of(0), 1)
+    down_ref[...] = jnp.concatenate(tiles_of(1), 1)
 
 
 def stream_kernel(
-    first_ref, cot_second_ref, win_f_ref, win_c_ref, lat_ref, lon_ref, cor_ref,
-    in_first_ref, grad_second_ref, cot_ref,
+    first_ref, cot_second_ref, win_f_hbm, win_c_hbm, lat_ref, lon_ref, cor_ref,
+    in_first_ref, grad_second_ref, cot_ref, win_f_ref, win_c_ref, sems,
 ):
+    loads = [
+        pltpu.make_async_copy(win_f_hbm, win_f_ref, sems.at[0]),
+        pltpu.make_async_copy(win_c_hbm, win_c_ref, sems.at[1]),
+    ]
+    for load in loads:
+        load.start()
     cot_ref[...] = cot_second_ref[...].astype(f32)
+    for load in loads:
+        load.wait()
     strips = {"lat": lat_ref, "lon": lon_ref, "cor": cor_ref}
     for at, count, source, level, line, start in all_pieces():
         if source == "own":
@@ -429,7 +492,7 @@
         ]
         return pl.pallas_call(
             fn,
-            out_shape=[jax.ShapeDtypeStruct(s, f32) for s in out_shape],
+            out_shape=[s if hasattr(s, "dtype") else jax.ShapeDtypeStruct(s, f32) for s in out_shape],
             in_specs=in_specs(len(args)),
             out_specs=[spec(i in out_hbm) for i in range(len(out_shape))],
             scratch_shapes=[s if not isinstance(s, tuple) else pltpu.VMEM(*s) for s in scratch],
@@ -462,71 +525,138 @@
             lax.ppermute(cor, both, diagonal),
         )
 
-    same_core = [list(range(c, lat_count, 2)) for c in range(2)]
-
-    def swap_lat(value):
-        return lax.all_to_all(value, "lat", 0, 0, tiled=True, axis_index_groups=same_core)
-
-    def swap_lon(value):
-        return lax.all_to_all(value, "lon", 0, 0, tiled=True)
+    same_z = [
+        [(2 * chip + core) * lon_count + x * 8 + z for x in range(2) for chip in range(8)]
+        for core in range(2)
+        for z in range(8)
+    ]
+    same_x = [list(range(8)), list(range(8, 16))]
+
+    def swap_xy(value):
+        return lax.all_to_all(value, both, 0, 0, tiled=True, axis_index_groups=same_z)
+
+    def swap_z(value):
+        return lax.all_to_all(value, "lon", 0, 0, tiled=True, axis_index_groups=same_x)
+
+    def across_x(value):
+        return lax.ppermute(value, "lon", [(i, i ^ 8) for i in range(lon_count)])
+
+    def along_x(value, by):
+        def there(a, o):
+            x = (o // 8 * 2 + a // 8 + by) % 4
+            return (x % 2 * 8 + a % 8) * lon_count + x // 2 * 8 + o % 8
+
+        pairs = [(a * lon_count + o, there(a, o)) for a in range(lat_count) for o in range(lon_count)]
+        return lax.ppermute(value, both, pairs)
 
     def across(value, bit):
         return lax.ppermute(value, "lat", [(i, i ^ (1 << bit)) for i in range(lat_count)])
 
     strip_shapes = [(LAT_ROWS, D), (LON_ROWS, D), (COR_ROWS, D)]
     win = (TOKENS, D)
-    ff_half = (8, 2 * CELLS, LANES)
-    in_second, grad_first, x_win, g_win, lat, lon, cor, ff_keep, ff_send, gain_mlp_part = kernel(
+    ff_half = (CHIPS, 2 * PART, LANES)
+    half_bytes = lambda *dims: jax.ShapeDtypeStruct(dims, bf16)
+    (
+        in_second, grad_first, x_win, g_win, lat, lon, cor, gain_mlp_part, hidden, cot_up, normed, cot,
+    ) = kernel(
         ff_kernel,
-        [shape, shape, win, win, *strip_shapes, ff_half, ff_half, (1, D)],
+        [
+            shape, shape, win, win, *strip_shapes, (1, D),
+            half_bytes(TOKENS, FF), half_bytes(TOKENS, FF), half_bytes(TOKENS, D), half_bytes(TOKENS, D),
+        ],
         [
             (shape, f32), (shape, f32), (shape, bf16), (shape, bf16), ((D, FF), bf16), ((D, FF), bf16),
-            (shape, f32), (shape, f32), ((TOKENS, FF), bf16), ((TOKENS, FF), bf16), ((TOKENS, D), bf16),
-            pltpu.SemaphoreType.DMA((6,)), pltpu.SemaphoreType.DMA((2,)),
+            (shape, f32), (shape, f32), ((1, D), f32),
+            pltpu.SemaphoreType.DMA((7,)), pltpu.SemaphoreType.DMA((2,)),
         ],
         "feedforward",
-        flops=12 * TOKENS * D * FF,
+        flops=8 * TOKENS * D * FF,
         nbytes=6_000_000,
-        in_hbm=(0, 1, 2, 3, 5, 6),
+        in_hbm=tuple(range(7)),
         out_hbm=(0, 1),
     )(out_first, out_second, cot_first, cot_second, gain_mlp.reshape(1, D), w_up, w_down.T)
     lat, lon, cor = halo(lat, lon, cor, 1)
-    (ff_sum,) = kernel(add_kernel, [ff_half], name="pair")(ff_keep, across(ff_send, 0))
-    x_win, ff_sum = lax.optimization_barrier((x_win, ff_sum))
-    at_half = (8, CELLS + 8, LANES)
-    win_f, win_c, lat, lon, cor, bias_part, keep, send = kernel(
+    ff_keep, ff_send = kernel(
+        ff_grads_kernel, [ff_half, ff_half], name="ffgrads", flops=2_000_000_000, nbytes=4_000_000
+    )(normed, cot_up, cot, hidden)
+    def ff_step(bit, keep, recv):
+        parts = (keep.shape[0] // 2, *keep.shape[1:])
+        return kernel(functools.partial(halve_kernel, bit), [parts, parts], name="halve")(keep, recv)
+
+    ff_keep, ff_send = ff_step("x_low", ff_keep, across(ff_send, 0))
+    x_win, ff_keep, ff_send = lax.optimization_barrier((x_win, ff_keep, ff_send))
+    ff_recv = across(ff_send, 3)
+    at_half = (CHIPS, PART + 4, LANES)
+    bias_half = (8, 64, LANES)
+    gain = gain_attn.reshape(1, D)
+    half_win = half_bytes(*win)
+    bias_keep, bias_send, x_win, *attention_parts = kernel(
         attention_kernel,
-        [win, win, *strip_shapes, (16, 64, LANES), at_half, at_half],
-        [(win, f32)] * 10,
+        [bias_half, bias_half, win, *[half_win] * 6],
+        [(win, f32)] * 9,
         "attention",
-        flops=16_000_000_000,
+        flops=14_000_000_000,
         nbytes=16_000_000,
-    )(
-        x_win, g_win, lat, lon, cor,
-        earth_bias, gain_attn.reshape(1, D), w_qkv, w_proj, gain_mlp_part,
+    )(x_win, g_win, lat, lon, cor, earth_bias, gain, w_qkv, w_proj)
+    bias_keep, bias_recv = along_x(bias_keep, 1), along_x(bias_send, -1)
+    keep, send, cot_normed = kernel(
+        attention_grads_kernel, [at_half, at_half, win], name="attngrads", flops=2_000_000_000, nbytes=4_000_000
+    )(x_win, *attention_parts, w_qkv, gain_mlp_part)
+    attended = attention_parts[2]
+    keep, send, x_win, ff_recv = lax.optimization_barrier((keep, send, x_win, ff_recv))
+    ff_keep, ff_send = ff_step("y_low", ff_keep, ff_recv)
+    ff_keep, ff_send = ff_step("y_high", ff_keep, across(ff_send, 1))
+    ff_recv = across(ff_send, 2)
+    win_f, win_c, lat, lon, cor = kernel(
+        return_kernel,
+        [win, win, *strip_shapes],
+        [(win, f32), (win, f32), pltpu.SemaphoreType.DMA((2,))],
+        "returns",
+        flops=1_000_000_000,
+        nbytes=4_000_000,
+        out_hbm=(0, 1),
+    )(x_win, attended, cot_normed, gain, w_proj)
+    recv, win_f, win_c, lat, lon, cor = lax.optimization_barrier(
+        (across(send, 0), win_f, win_c, lat, lon, cor)
     )
     lat, lon, cor = halo(lat, lon, cor, -1)
-    (parts,) = kernel(lat_join_kernel, [(8, 3 * CELLS + 8, LANES)], name="latjoin")(
-        keep, across(send, 0), ff_sum
+    block = (CHIPS, 3 * PART + 4, LANES)
+    (parts,) = kernel(xy_join_kernel, [at_half], name="xyjoin")(keep, recv)
+    parts, bias_keep, bias_recv, ff_recv = lax.optimization_barrier((parts, bias_keep, bias_recv, ff_recv))
+    ff_keep, ff_send = ff_step("x_high", ff_keep, ff_recv)
+    ff_recv = across_x(ff_send)
+    parts = swap_xy(parts)
+    (joined,) = kernel(z_join_kernel, [(8, 80, LANES)], name="zjoin")(
+        bias_keep, bias_recv, parts, ff_keep, ff_recv
     )
-    parts = swap_lat(parts)
-    parts, lat, lon, cor = lax.optimization_barrier((parts, lat, lon, cor))
-    (joined,) = kernel(lon_join_kernel, [(16, 80, LANES)], name="lonjoin")(bias_part, parts)
-    (totals,) = kernel(total_kernel, [(16, 80, LANES)], name="total")(swap_lon(joined))
-    sums = swap_lon(totals)
-    spread, gains = kernel(spread_kernel, [(8, 3 * CELLS, LANES), (8, LANES)], name="spread")(sums)
-    mine = swap_lat(spread)
+    joined = swap_z(joined)
+    (totals,) = kernel(total_kernel, [(8, 80, LANES)], name="total")(joined)
+    totals = swap_z(totals)
+    spread, bias_mine = kernel(spread_kernel, [block, bias_half], name="spread")(totals)
+    bias_mine, bias_other = along_x(bias_mine, -1), along_x(bias_mine, 1)
+    mine = swap_xy(spread)
+    mine, lat, lon, cor = lax.optimization_barrier((mine, lat, lon, cor))
+    in_first, grad_second = kernel(
+        stream_kernel,
+        [shape, shape],
+        [(shape, f32), (win, f32), (win, f32), pltpu.SemaphoreType.DMA((2,))],
+        "streams",
+        nbytes=3_000_000,
+        flops=2_000_000_000,
+        in_hbm=(2, 3),
+    )(out_first, cot_second, win_f, win_c, lat, lon, cor)
+    mine, bias_mine, bias_other = lax.optimization_barrier((mine, bias_mine, bias_other))
     other = across(mine, 0)
-    in_first, grad_second = kernel(
-        stream_kernel, [shape, shape], [(shape, f32)], "streams", nbytes=3_000_000, flops=2_000_000_000
-    )(out_first, cot_second, win_f, win_c, lat, lon, cor)
-    (grad_bias,) = kernel(bias_kernel, [(BANDS, 1, HEADS, 2 * CELLS, 2 * CELLS)], name="bias")(sums)
+    (grad_bias,) = kernel(bias_kernel, [(BANDS, 1, HEADS, 2 * CELLS, 2 * CELLS)], name="bias")(
+        bias_mine, bias_other
+    )
     grad_gain_attn, grad_qkv, grad_proj, grad_gain_mlp, grad_up, grad_down = kernel(
         last_kernel,
         [(1, D), (D, 3 * D), (D, D), (1, D), (D, FF), (D, FF)],
+        [((3 * D, LANES), f32)],
         name="last",
         nbytes=6_000_000,
-    )(gains, mine, other)
+    )(mine, other)
     return (
         in_first, in_second, grad_first, grad_second,
         grad_gain_attn.reshape(D), grad_qkv, grad_proj, grad_bias,

time: 130 us -> 115 us (0.88)
  blocking collectives: 64.1 us -> 25.7 us
  starting transfers between devices: 24.6 us -> 37.6 us
  waiting for transfers between devices: 20.8 us -> 27.5 us
  Pallas kernels: 17.7 us -> 21.2 us
    all_to_all x3 -> x2, blocking collectives: 64.1 us -> 25.7 us  [swap_z(): lax.all_to_all(value, 'lon', 0, 0, tiled=True, axis_index_groups=same_x)]
    ppermute x0 -> x5, starting transfers between devices: none -> 8.54 us  [the longest x4 5.66 us: along_x(): return lax.ppermute(value, both, pairs)]
    ppermute x2, starting transfers between devices: 0.45 us -> 7.35 us  [halo(): lax.ppermute(lat, 'lat', ring(lat_count))]
    ppermute x2, waiting for transfers between devices: 4.75 us -> 0.01 us  [halo(): lax.ppermute(lat, 'lat', ring(lat_count))]
    ppermute x3 -> x6, waiting for transfers between devices: 1.26 us -> 5.81 us  [across(): lax.ppermute(value, 'lat', [(i, i ^ 1 << bit) for i in range(lat_count)])]
    all_to_all x1 -> x2, starting transfers between devices: 3.55 us -> 7.31 us  [swap_xy(): lax.all_to_all(value, both, 0, 0, tiled=True, axis_index_groups=same_z)]
    ppermute x2, starting transfers between devices: 6.4 us -> 2.86 us  [halo(): lax.ppermute(cor, both, diagonal)]
    pallas_call x10 -> x16, Pallas kernels: 17.7 us -> 21.2 us  [call(): pl.pallas_call(fn, out_shape=[s if hasattr(s, 'dtype') else jax.ShapeDtyp...]
  transfers between devices with their start and end apart: 10 -> 19, of which waited for: 4 -> 6; matrix products, arithmetic and copies ran while one was open for 0% -> 0% of each run, Pallas kernels for 2% -> 12%
where the time goes in v3:
time: 115 us; the launch traced here: 114 us
  starting transfers between devices  37.6 us (33%)
  waiting for transfers between devices  27.5 us (24%)
  blocking collectives  25.7 us (22%)
  Pallas kernels  21.2 us (18%)
  local copies, waits for them, and re-layouts  1.55 us (1%)
    all_to_all x2, blocking collectives, swap_z(): lax.all_to_all(value, 'lon', 0, 0, tiled=True, axis_index_groups=same_x)  25.7 us
    pallas_call x16, Pallas kernels, call(): pl.pallas_call(fn, out_shape=[s if hasattr(s, 'dtype') else jax.ShapeDtyp...  21.2 us
    ppermute x2, waiting for transfers between devices, halo(): lax.ppermute(cor, both, diagonal)  16.9 us
    ppermute x6, starting transfers between devices, across(): lax.ppermute(value, 'lat', [(i, i ^ 1 << bit) for i in range(lat_count)])  9.18 us
    ppermute x2, starting transfers between devices, halo(): lax.ppermute(lat, 'lat', ring(lat_count))  7.35 us
    all_to_all x2, starting transfers between devices, swap_xy(): lax.all_to_all(value, both, 0, 0, tiled=True, axis_index_groups=same_z)  7.31 us
    ppermute x6, waiting for transfers between devices, across(): lax.ppermute(value, 'lat', [(i, i ^ 1 << bit) for i in range(lat_count)])  5.81 us
    ppermute x4, starting transfers between devices, along_x(): return lax.ppermute(value, both, pairs)  5.66 us
  transfers between devices with their start and end apart: 19, of which 6 were waited for; matrix products, arithmetic and copies ran while one was open for 0% of the time, Pallas kernels for 12%

profile of v3, /device:TPU:1, one launch (start us, length us, event | category | flops | bytes accessed | tf_op | source)
XLA Modules:
  0.0 114.4 jit_solution(5071836516981171643)
XLA Ops:
  0.6 4.7 %feedforward.1 = (f32[2,12,24,192]{3,2,1,0:T(8,128)}, f32[2,12,24,192]{3,2,1,0:T(8,128)}, f32[576,192]{1,0:T(8,128)S(1)}, f32[576,192]{1,0:T(8,128)S(1)}, f32[21...) custom-call(f32[2,12,24,192]{3,2,1,0:T(8,128)} %first_ref.1, ...), custom_call_target="tpu_custom_call" | custom-call | flops 679477248 | bytes 6000000 | tf_op jit(solution)/shard_map/feedforward/pallas_call | solution.py:493
  6.1 3.3 %collective-permute-start = (f32[16,72,128]{2,1,0:T(8,128)S(1)}, f32[16,72,128]{2,1,0:T(8,128)S(1)}, u32[]{:S(2)}, u32[]{:S(2)}) collective-permute-start(f32[16,72,128]{2,1,0:T(8,128)S(1)} %get-tuple-element.90), channel_id=1, source_target_pairs={{0,16},{16,0},{32,48},{48,32},{64,80},{80,64},{96,112},{112,96},{1... | collective-permute-start | bytes 1769480 | tf_op jit(solution)/shard_map/ppermute | solution.py:553
  10.6 2.1 %collective-permute-start.3 = (f32[72,192]{1,0:T(8,128)S(1)}, f32[72,192]{1,0:T(8,128)S(1)}, u32[]{:S(2)}, u32[]{:S(2)}) collective-permute-start(f32[72,192]{1,0:T(8,128)S(1)} %get-tuple-element.97), channel_id=1, source_target_pairs={{0,17},{1,18},{2,19},{3,20},{4,21},{5,22},{6,23},{7,24},{8,25},{9,... | collective-permute-start | bytes 165896 | tf_op jit(solution)/shard_map/ppermute | solution.py:525
  12.8 1.5 %collective-permute-start.4 = (f32[8,72,128]{2,1,0:T(8,128)S(1)}, f32[8,72,128]{2,1,0:T(8,128)S(1)}, u32[]{:S(2)}, u32[]{:S(2)}) collective-permute-start(f32[8,72,128]{2,1,0:T(8,128)S(1)} %get-tuple-element.108), channel_id=1, source_target_pairs={{0,128},{16,144},{32,160},{48,176},{64,192},{80,208},{96,224},{112... | collective-permute-start | bytes 884744 | tf_op jit(solution)/shard_map/ppermute | solution.py:553
  14.2 9.0 %collective-permute-done.3.cor_ref = f32[72,192]{1,0:T(8,128)S(1)} collective-permute-done((f32[72,192]{1,0:T(8,128)S(1)}, f32[72,192]{1,0:T(8,128)S(1)}, u32[]{:S(2)}, u32[]{:S(2)}) %collective-permute-start.3) | collective-permute-done | bytes 55328 | tf_op jit(solution)/shard_map/ppermute | solution.py:525
  23.3 6.2 %attention.1 = (f32[8,64,128]{2,1,0:T(8,128)S(1)}, f32[8,64,128]{2,1,0:T(8,128)S(1)}, f32[576,192]{1,0:T(8,128)S(1)}, bf16[576,192]{1,0:T(8,128)(2,1)S(1)}, bf16...) custom-call(f32[576,192]{1,0:T(8,128)S(1)} %get-tuple-element.93.x_i, ...), custom_call_target="tpu_custom_call" | custom-call | flops 14000000000 | bytes 16000000 | tf_op jit(solution)/shard_map/attention/pallas_call | solution.py:493
  30.4 3.0 %collective-permute-start.5 = (f32[16,40,128]{2,1,0:T(8,128)S(1)}, f32[16,40,128]{2,1,0:T(8,128)S(1)}, u32[]{:S(2)}, u32[]{:S(2)}) collective-permute-start(f32[16,40,128]{2,1,0:T(8,128)S(1)} %get-tuple-element.109), channel_id=1, source_target_pairs={{0,16},{16,0},{32,48},{48,32},{64,80},{80,64},{96,112},{112,96},{1... | collective-permute-start | bytes 983048 | tf_op jit(solution)/shard_map/ppermute | solution.py:553
  33.6 2.5 %collective-permute-start.7 = (f32[8,64,128]{2,1,0:T(8,128)S(1)}, f32[8,64,128]{2,1,0:T(8,128)S(1)}, u32[]{:S(2)}, u32[]{:S(2)}) collective-permute-start(f32[8,64,128]{2,1,0:T(8,128)S(1)} %get-tuple-element.122), channel_id=1, source_target_pairs={{0,136},{1,137},{2,138},{3,139},{4,140},{5,141},{6,142},{7,143},{8... | collective-permute-start | bytes 786440 | tf_op jit(solution)/shard_map/ppermute | solution.py:550
  36.2 4.7 %collective-permute-done.8.recv_ref = f32[4,72,128]{2,1,0:T(8,128)S(1)} collective-permute-done((f32[4,72,128]{2,1,0:T(8,128)S(1)}, f32[4,72,128]{2,1,0:T(8,128)S(1)}, u32[]{:S(2)}, u32[]{:S(2)}) %collective-permute-start.8) | collective-permute-done | bytes 147488 | tf_op jit(solution)/shard_map/ppermute | solution.py:553
  45.8 3.5 %all-to-all-start = ((f32[16,40,128]{2,1,0:T(8,128)}), f32[16,40,128]{2,1,0:T(8,128)S(1)}, u32[]{:S(2)}, u32[]{:S(2)}) async-start(f32[16,40,128]{2,1,0:T(8,128)} %xyjoin.1), calls=%async_computation | async-start | bytes 655360 | tf_op jit(solution)/shard_map/all_to_all | solution.py:536
  49.4 2.9 %collective-permute-start.10 = (f32[1,72,128]{2,1,0:T(8,128)S(1)}, f32[1,72,128]{2,1,0:T(8,128)S(1)}, u32[]{:S(2)}, u32[]{:S(2)}) collective-permute-start(f32[1,72,128]{2,1,0:T(8,128)S(1)} %get-tuple-element.134), channel_id=1, source_target_pairs={{0,8},{1,9},{2,10},{3,11},{4,12},{5,13},{6,14},{7,15},{8,0},{9,1},... | collective-permute-start | bytes 110600 | tf_op jit(solution)/shard_map/ppermute | solution.py:542
  52.3 3.2 %collective-permute-done.10.ff_recv_ref = f32[1,72,128]{2,1,0:T(8,128)S(1)} collective-permute-done((f32[1,72,128]{2,1,0:T(8,128)S(1)}, f32[1,72,128]{2,1,0:T(8,128)S(1)}, u32[]{:S(2)}, u32[]{:S(2)}) %collective-permute-start.10) | collective-permute-done | bytes 36896 | tf_op jit(solution)/shard_map/ppermute | solution.py:542
  55.5 1.6 %all-to-all-done.parts_ref = f32[16,40,128]{2,1,0:T(8,128)S(1)} async-done(((f32[16,40,128]{2,1,0:T(8,128)}), f32[16,40,128]{2,1,0:T(8,128)S(1)}, u32[]{:S(2)}, u32[]{:S(2)}) %all-to-all-start) | async-done | bytes 327712 | tf_op jit(solution)/shard_map/all_to_all | solution.py:536
  57.1 13.3 %all_to_all.20.in_ref = f32[8,80,128]{2,1,0:T(8,128)S(1)} all-to-all(f32[8,80,128]{2,1,0:T(8,128)S(1)} %zjoin.1), channel_id=1, replica_groups={{0,1,2,3,4,5,6,7},{8,9,10,11,12,13,14,15},{16,17,18,19,20,21,22,23},{24..., dimensions={0} | all-to-all | bytes 655360 | tf_op jit(solution)/shard_map/all_to_all | solution.py:539
  70.5 12.4 %all_to_all.21.in_ref = f32[8,80,128]{2,1,0:T(8,128)S(1)} all-to-all(f32[8,80,128]{2,1,0:T(8,128)S(1)} %total.1), channel_id=1, replica_groups={{0,1,2,3,4,5,6,7},{8,9,10,11,12,13,14,15},{16,17,18,19,20,21,22,23},{24..., dimensions={0} | all-to-all | bytes 655360 | tf_op jit(solution)/shard_map/all_to_all | solution.py:539
  83.9 3.8 %all-to-all-start.3 = ((f32[16,112,128]{2,1,0:T(8,128)}), f32[16,112,128]{2,1,0:T(8,128)S(1)}, u32[]{:S(2)}, u32[]{:S(2)}) async-start(f32[16,112,128]{2,1,0:T(8,128)} %get-tuple-element.135), calls=%async_computation.3 | async-start | bytes 1835008 | tf_op jit(solution)/shard_map/all_to_all | solution.py:536
  87.7 1.3 %collective-permute-start.15 = (f32[8,64,128]{2,1,0:T(8,128)S(1)}, f32[8,64,128]{2,1,0:T(8,128)S(1)}, u32[]{:S(2)}, u32[]{:S(2)}) collective-permute-start(f32[8,64,128]{2,1,0:T(8,128)S(1)} %get-tuple-element.147), channel_id=1, source_target_pairs={{0,128},{1,129},{2,130},{3,131},{4,132},{5,133},{6,134},{7,135},{8... | collective-permute-start | bytes 786440 | tf_op jit(solution)/shard_map/ppermute | solution.py:550
  89.0 1.6 %collective-permute-start.14 = (f32[8,64,128]{2,1,0:T(8,128)S(1)}, f32[8,64,128]{2,1,0:T(8,128)S(1)}, u32[]{:S(2)}, u32[]{:S(2)}) collective-permute-start(f32[8,64,128]{2,1,0:T(8,128)S(1)} %get-tuple-element.147), channel_id=1, source_target_pairs={{0,136},{1,137},{2,138},{3,139},{4,140},{5,141},{6,142},{7,143},{8... | collective-permute-start | bytes 786440 | tf_op jit(solution)/shard_map/ppermute | solution.py:550
  90.6 7.3 %collective-permute-start.11 = (f32[216,192]{1,0:T(8,128)S(1)}, f32[216,192]{1,0:T(8,128)S(1)}, u32[]{:S(2)}, u32[]{:S(2)}) collective-permute-start(f32[216,192]{1,0:T(8,128)S(1)} %get-tuple-element.136), channel_id=1, source_target_pairs={{0,240},{16,0},{32,16},{48,32},{64,48},{80,64},{96,80},{112,96},{1... | collective-permute-start | bytes 497672 | tf_op jit(solution)/shard_map/ppermute | solution.py:523
  98.0 1.2 %collective-permute-start.12 = (f32[216,192]{1,0:T(8,128)S(1)}, f32[216,192]{1,0:T(8,128)S(1)}, u32[]{:S(2)}, u32[]{:S(2)}) collective-permute-start(f32[216,192]{1,0:T(8,128)S(1)} %get-tuple-element.137), channel_id=1, source_target_pairs={{0,15},{1,0},{2,1},{3,2},{4,3},{5,4},{6,5},{7,6},{8,7},{9,8},{10,9... | collective-permute-start | bytes 497672 | tf_op jit(solution)/shard_map/ppermute | solution.py:524
  100.0 7.8 %collective-permute-done.13.cor_ref = f32[72,192]{1,0:T(8,128)S(1)} collective-permute-done((f32[72,192]{1,0:T(8,128)S(1)}, f32[72,192]{1,0:T(8,128)S(1)}, u32[]{:S(2)}, u32[]{:S(2)}) %collective-permute-start.13) | collective-permute-done | bytes 55328 | tf_op jit(solution)/shard_map/ppermute | solution.py:525
  108.6 1.8 %bias.1 = f32[2,1,6,144,144]{4,3,2,1,0:T(8,128)} custom-call(f32[8,64,128]{2,1,0:T(8,128)S(1)} %collective-permute-done.14.next_ref, f32[8,64,128]{2,1,0:T(8,128)S(1)} %collective-permute-done.15.before_ref), custom_call_target="tpu_custom_call" | custom-call | tf_op jit(solution)/shard_map/bias/pallas_call | solution.py:493
  110.4 2.5 %streams.1 = (f32[2,12,24,192]{3,2,1,0:T(8,128)}, f32[2,12,24,192]{3,2,1,0:T(8,128)}) custom-call(f32[2,12,24,192]{3,2,1,0:T(8,128)S(1)} %copy-done.1, bf16[2,12,24,192]{3,2,1,0:T(8,128)(2,1)S(1)} %copy-done.2, f32[576,192]{1,0:T(8,128)} %copy-done.8, f32[576,192]{1,0:T(8,128)} %copy-done.9, f32[216,192]{1,0:T(8,128)S(1)} %collective-permute-done.11.lat_ref, ...), custom_call_target="tpu_custom_call" | custom-call | flops 2000000000 | bytes 3000000 | tf_op jit(solution)/shard_map/streams/pallas_call | solution.py:493
  112.9 1.5 %last.1 = (f32[1,192]{1,0:T(1,128)}, f32[192,576]{1,0:T(8,128)}, f32[192,192]{1,0:T(8,128)}, f32[1,192]{1,0:T(1,128)}, f32[192,768]{1,0:T(8,128)}, /*index=5*/f32[192,768]{1,0:T(8,128)}) custom-call(f32[16,112,128]{2,1,0:T(8,128)S(1)} %all-to-all-done.3.mine_ref, f32[16,112,128]{2,1,0:T(8,128)S(1)} %collective-permute-done.16.other_ref), custom_call_target="tpu_custom_call" | custom-call | bytes 6000000 | tf_op jit(solution)/shard_map/last/pallas_call | solution.py:493
  (52 shorter events, 10.5 us)
Async XLA Ops:
  5.4 17.9 %copy-start = (bf16[2,1,6,144,144]{4,3,2,1,0:T(8,128)(2,1)S(1)}, bf16[2,1,6,144,144]{4,3,2,1,0:T(8,128)(2,1)}, u32[]{:S(2)}) copy-start(bf16[2,1,6,144,144]{4,3,2,1,0:T(8,128)(2,1)} %bias_ref.1) | copy-start | bytes 1492996
  5.4 17.9 %copy-start.3 = (bf16[192,576]{1,0:T(8,128)(2,1)S(1)}, bf16[192,576]{1,0:T(8,128)(2,1)}, u32[]{:S(2)}) copy-start(bf16[192,576]{1,0:T(8,128)(2,1)} %qkv_ref.3) | copy-start | bytes 663556
  5.4 17.9 %copy-start.4 = (bf16[192,192]{1,0:T(8,128)(2,1)S(1)}, bf16[192,192]{1,0:T(8,128)(2,1)}, u32[]{:S(2)}) copy-start(bf16[192,192]{1,0:T(8,128)(2,1)} %proj_ref.3) | copy-start | bytes 221188
  6.1 6.6 %collective-permute-start = (f32[16,72,128]{2,1,0:T(8,128)S(1)}, f32[16,72,128]{2,1,0:T(8,128)S(1)}, u32[]{:S(2)}, u32[]{:S(2)}) collective-permute-start(f32[16,72,128]{2,1,0:T(8,128)S(1)} %get-tuple-element.90), channel_id=1, source_target_pairs={{0,16},{16,0},{32,48},{48,32},{64,80},{80,64},{96,112},{112,96},{1... | collective-permute-start | bytes 1769480 | tf_op jit(solution)/shard_map/ppermute | solution.py:553
  9.4 13.8 %collective-permute-start.1 = (f32[216,192]{1,0:T(8,128)S(1)}, f32[216,192]{1,0:T(8,128)S(1)}, u32[]{:S(2)}, u32[]{:S(2)}) collective-permute-start(f32[216,192]{1,0:T(8,128)S(1)} %get-tuple-element.95), channel_id=1, source_target_pairs={{0,16},{16,32},{32,48},{48,64},{64,80},{80,96},{96,112},{112,128},... | collective-permute-start | bytes 497672 | tf_op jit(solution)/shard_map/ppermute | solution.py:523
  9.4 13.8 %collective-permute-start.2 = (f32[216,192]{1,0:T(8,128)S(1)}, f32[216,192]{1,0:T(8,128)S(1)}, u32[]{:S(2)}, u32[]{:S(2)}) collective-permute-start(f32[216,192]{1,0:T(8,128)S(1)} %get-tuple-element.96), channel_id=1, source_target_pairs={{0,1},{1,2},{2,3},{3,4},{4,5},{5,6},{6,7},{7,8},{8,9},{9,10},{10,1... | collective-permute-start | bytes 497672 | tf_op jit(solution)/shard_map/ppermute | solution.py:524
  10.6 12.7 %collective-permute-start.3 = (f32[72,192]{1,0:T(8,128)S(1)}, f32[72,192]{1,0:T(8,128)S(1)}, u32[]{:S(2)}, u32[]{:S(2)}) collective-permute-start(f32[72,192]{1,0:T(8,128)S(1)} %get-tuple-element.97), channel_id=1, source_target_pairs={{0,17},{1,18},{2,19},{3,20},{4,21},{5,22},{6,23},{7,24},{8,25},{9,... | collective-permute-start | bytes 165896 | tf_op jit(solution)/shard_map/ppermute | solution.py:525
  12.8 17.6 %collective-permute-start.4 = (f32[8,72,128]{2,1,0:T(8,128)S(1)}, f32[8,72,128]{2,1,0:T(8,128)S(1)}, u32[]{:S(2)}, u32[]{:S(2)}) collective-permute-start(f32[8,72,128]{2,1,0:T(8,128)S(1)} %get-tuple-element.108), channel_id=1, source_target_pairs={{0,128},{16,144},{32,160},{48,176},{64,192},{80,208},{96,224},{112... | collective-permute-start | bytes 884744 | tf_op jit(solution)/shard_map/ppermute | solution.py:553
  30.4 13.5 %collective-permute-start.5 = (f32[16,40,128]{2,1,0:T(8,128)S(1)}, f32[16,40,128]{2,1,0:T(8,128)S(1)}, u32[]{:S(2)}, u32[]{:S(2)}) collective-permute-start(f32[16,40,128]{2,1,0:T(8,128)S(1)} %get-tuple-element.109), channel_id=1, source_target_pairs={{0,16},{16,0},{32,48},{48,32},{64,80},{80,64},{96,112},{112,96},{1... | collective-permute-start | bytes 983048 | tf_op jit(solution)/shard_map/ppermute | solution.py:553
  33.4 11.3 %collective-permute-start.6 = (f32[8,64,128]{2,1,0:T(8,128)S(1)}, f32[8,64,128]{2,1,0:T(8,128)S(1)}, u32[]{:S(2)}, u32[]{:S(2)}) collective-permute-start(f32[8,64,128]{2,1,0:T(8,128)S(1)} %get-tuple-element.121), channel_id=1, source_target_pairs={{0,128},{1,129},{2,130},{3,131},{4,132},{5,133},{6,134},{7,135},{8... | collective-permute-start | bytes 786440 | tf_op jit(solution)/shard_map/ppermute | solution.py:550
  33.6 11.1 %collective-permute-start.7 = (f32[8,64,128]{2,1,0:T(8,128)S(1)}, f32[8,64,128]{2,1,0:T(8,128)S(1)}, u32[]{:S(2)}, u32[]{:S(2)}) collective-permute-start(f32[8,64,128]{2,1,0:T(8,128)S(1)} %get-tuple-element.122), channel_id=1, source_target_pairs={{0,136},{1,137},{2,138},{3,139},{4,140},{5,141},{6,142},{7,143},{8... | collective-permute-start | bytes 786440 | tf_op jit(solution)/shard_map/ppermute | solution.py:550
  36.1 4.8 %collective-permute-start.8 = (f32[4,72,128]{2,1,0:T(8,128)S(1)}, f32[4,72,128]{2,1,0:T(8,128)S(1)}, u32[]{:S(2)}, u32[]{:S(2)}) collective-permute-start(f32[4,72,128]{2,1,0:T(8,128)S(1)} %get-tuple-element.126), channel_id=1, source_target_pairs={{0,32},{16,48},{32,0},{48,16},{64,96},{80,112},{96,64},{112,80},{1... | collective-permute-start | bytes 442376 | tf_op jit(solution)/shard_map/ppermute | solution.py:553
  41.0 4.8 %collective-permute-start.9 = (f32[2,72,128]{2,1,0:T(8,128)S(1)}, f32[2,72,128]{2,1,0:T(8,128)S(1)}, u32[]{:S(2)}, u32[]{:S(2)}) collective-permute-start(f32[2,72,128]{2,1,0:T(8,128)S(1)} %get-tuple-element.127), channel_id=1, source_target_pairs={{0,64},{16,80},{32,96},{48,112},{64,0},{80,16},{96,32},{112,48},{1... | collective-permute-start | bytes 221192 | tf_op jit(solution)/shard_map/ppermute | solution.py:553
  45.8 11.3 %all-to-all-start = ((f32[16,40,128]{2,1,0:T(8,128)}), f32[16,40,128]{2,1,0:T(8,128)S(1)}, u32[]{:S(2)}, u32[]{:S(2)}) async-start(f32[16,40,128]{2,1,0:T(8,128)} %xyjoin.1), calls=%async_computation | async-start | bytes 655360 | tf_op jit(solution)/shard_map/all_to_all | solution.py:536
  49.4 6.1 %collective-permute-start.10 = (f32[1,72,128]{2,1,0:T(8,128)S(1)}, f32[1,72,128]{2,1,0:T(8,128)S(1)}, u32[]{:S(2)}, u32[]{:S(2)}) collective-permute-start(f32[1,72,128]{2,1,0:T(8,128)S(1)} %get-tuple-element.134), channel_id=1, source_target_pairs={{0,8},{1,9},{2,10},{3,11},{4,12},{5,13},{6,14},{7,15},{8,0},{9,1},... | collective-permute-start | bytes 110600 | tf_op jit(solution)/shard_map/ppermute | solution.py:542
  83.9 26.5 %copy-start.1 = (f32[2,12,24,192]{3,2,1,0:T(8,128)S(1)}, f32[2,12,24,192]{3,2,1,0:T(8,128)}, u32[]{:S(2)}) copy-start(f32[2,12,24,192]{3,2,1,0:T(8,128)} %first_ref.1) | copy-start | bytes 1327108
  83.9 26.5 %copy-start.2 = (bf16[2,12,24,192]{3,2,1,0:T(8,128)(2,1)S(1)}, bf16[2,12,24,192]{3,2,1,0:T(8,128)(2,1)}, u32[]{:S(2)}) copy-start(bf16[2,12,24,192]{3,2,1,0:T(8,128)(2,1)} %cot_second_ref.1) | copy-start | bytes 663556
  83.9 24.5 %all-to-all-start.3 = ((f32[16,112,128]{2,1,0:T(8,128)}), f32[16,112,128]{2,1,0:T(8,128)S(1)}, u32[]{:S(2)}, u32[]{:S(2)}) async-start(f32[16,112,128]{2,1,0:T(8,128)} %get-tuple-element.135), calls=%async_computation.3 | async-start | bytes 1835008 | tf_op jit(solution)/shard_map/all_to_all | solution.py:536
  87.7 20.8 %collective-permute-start.15 = (f32[8,64,128]{2,1,0:T(8,128)S(1)}, f32[8,64,128]{2,1,0:T(8,128)S(1)}, u32[]{:S(2)}, u32[]{:S(2)}) collective-permute-start(f32[8,64,128]{2,1,0:T(8,128)S(1)} %get-tuple-element.147), channel_id=1, source_target_pairs={{0,128},{1,129},{2,130},{3,131},{4,132},{5,133},{6,134},{7,135},{8... | collective-permute-start | bytes 786440 | tf_op jit(solution)/shard_map/ppermute | solution.py:550
  89.0 19.5 %collective-permute-start.14 = (f32[8,64,128]{2,1,0:T(8,128)S(1)}, f32[8,64,128]{2,1,0:T(8,128)S(1)}, u32[]{:S(2)}, u32[]{:S(2)}) collective-permute-start(f32[8,64,128]{2,1,0:T(8,128)S(1)} %get-tuple-element.147), channel_id=1, source_target_pairs={{0,136},{1,137},{2,138},{3,139},{4,140},{5,141},{6,142},{7,143},{8... | collective-permute-start | bytes 786440 | tf_op jit(solution)/shard_map/ppermute | solution.py:550
  90.6 17.8 %collective-permute-start.11 = (f32[216,192]{1,0:T(8,128)S(1)}, f32[216,192]{1,0:T(8,128)S(1)}, u32[]{:S(2)}, u32[]{:S(2)}) collective-permute-start(f32[216,192]{1,0:T(8,128)S(1)} %get-tuple-element.136), channel_id=1, source_target_pairs={{0,240},{16,0},{32,16},{48,32},{64,48},{80,64},{96,80},{112,96},{1... | collective-permute-start | bytes 497672 | tf_op jit(solution)/shard_map/ppermute | solution.py:523
  98.0 10.4 %collective-permute-start.12 = (f32[216,192]{1,0:T(8,128)S(1)}, f32[216,192]{1,0:T(8,128)S(1)}, u32[]{:S(2)}, u32[]{:S(2)}) collective-permute-start(f32[216,192]{1,0:T(8,128)S(1)} %get-tuple-element.137), channel_id=1, source_target_pairs={{0,15},{1,0},{2,1},{3,2},{4,3},{5,4},{6,5},{7,6},{8,7},{9,8},{10,9... | collective-permute-start | bytes 497672 | tf_op jit(solution)/shard_map/ppermute | solution.py:524
  99.2 8.6 %collective-permute-start.13 = (f32[72,192]{1,0:T(8,128)S(1)}, f32[72,192]{1,0:T(8,128)S(1)}, u32[]{:S(2)}, u32[]{:S(2)}) collective-permute-start(f32[72,192]{1,0:T(8,128)S(1)} %get-tuple-element.138), channel_id=1, source_target_pairs={{0,255},{1,240},{2,241},{3,242},{4,243},{5,244},{6,245},{7,246},{8... | collective-permute-start | bytes 165896 | tf_op jit(solution)/shard_map/ppermute | solution.py:525
  108.5 4.5 %collective-permute-start.16 = (f32[16,112,128]{2,1,0:T(8,128)S(1)}, f32[16,112,128]{2,1,0:T(8,128)S(1)}, u32[]{:S(2)}, u32[]{:S(2)}) collective-permute-start(f32[16,112,128]{2,1,0:T(8,128)S(1)} %all-to-all-done.3.mine_ref), channel_id=1, source_target_pairs={{0,16},{16,0},{32,48},{48,32},{64,80},{80,64},{96,112},{112,96},{1... | collective-permute-start | bytes 2752520 | tf_op jit(solution)/shard_map/ppermute | solution.py:553
  (5 other events, 22.2 us)

commit v4 on v3

--- a/solution.py
+++ b/solution.py
@@ -209,9 +209,85 @@
                     yield base + row * WIN_LON + col, count, source, initial, line, start
 
 
+lane_head = lambda: lax.broadcasted_iota(jnp.int32, (CELLS, D), 1) // HEAD_DIM
+
+
+def bias_table(bias_ref, band, level):
+    query_low = lax.broadcasted_iota(jnp.int32, (CELLS, LANES), 0) < CELLS // 2
+    key = lax.broadcasted_iota(jnp.int32, (CELLS, LANES), 1)
+    first_band = lax.axis_index("lat") == 0
+    apart = jnp.logical_and(query_low != (key < CELLS // 2), first_band)
+    tables = []
+    low = level * CELLS
+    for h in range(HEADS):
+        table = bias_ref[band, 0, h].astype(f32)[low : low + CELLS, low : low + CELLS]
+        table = jnp.concatenate([table, jnp.full((CELLS, LANES - CELLS), padded_score, f32)], 1)
+        if band == 0:
+            table = jnp.where(jnp.logical_and(apart, key < CELLS), masked_score, table)
+        tables.append(table)
+    return jnp.concatenate(tables, 0)
+
+
+def attend(query, key, value, cot_attended, table):
+    heads = lane_head()
+    of_head = [heads == h for h in range(HEADS)]
+    pad = jnp.zeros((LANES - CELLS, D), f32)
+
+    def stacked(value):
+        return jnp.concatenate([jnp.where(m, value, 0.0) for m in of_head], 0).astype(bf16)
+
+    def gathered(value):
+        total = jnp.where(of_head[0], value[:CELLS], 0.0)
+        for h in range(1, HEADS):
+            total = jnp.where(of_head[h], value[h * CELLS : (h + 1) * CELLS], total)
+        return total
+
+    queries = stacked(query)
+    key_part = jnp.concatenate([key, pad], 0).astype(bf16)
+    value_part = jnp.concatenate([value, pad], 0).astype(bf16)
+    scores = nt(queries, key_part) * score_scale + table
+    exponent = jnp.exp(scores - jnp.max(scores, -1, keepdims=True))
+    probability = exponent * (1.0 / jnp.sum(exponent, -1, keepdims=True))
+    weights = probability.astype(bf16)
+    attended = gathered(nn(weights, value_part))
+    cot_att = stacked(cot_attended)
+    cot_weights = nt(cot_att, value_part)
+    cot_value = tn(weights, cot_att)[:CELLS]
+    inner = jnp.sum(cot_weights * probability, -1, keepdims=True)
+    cot_scores = probability * (cot_weights - inner)
+    scaled = (cot_scores * score_scale).astype(bf16)
+    cot_query = gathered(nn(scaled, key_part))
+    cot_key = tn(scaled, queries)[:CELLS]
+    return (attended, cot_query, cot_key, cot_value), cot_scores
+
+
+def inner_attention_kernel(
+    x_ref, g_ref, bias_ref, gain_ref, qkv_ref, proj_ref,
+    att_ref, cq_ref, ck_ref, cv_ref, cot_scores_ref,
+    q_ref, k_ref, v_ref, ca_ref,
+):
+    rows = [window_of(BANDS - 1, level, SECTORS - 1) * CELLS for level in range(LEV)]
+    x, g = (jnp.concatenate([ref[at : at + CELLS, :] for at in rows], 0) for ref in (x_ref, g_ref))
+    unit_field, _ = norm_parts(x)
+    normed = (unit_field * gain_ref[...]).astype(bf16)
+    for i, ref in enumerate((q_ref, k_ref, v_ref)):
+        ref[...] = nn(normed, qkv_ref[:, i * D : (i + 1) * D]).astype(bf16).astype(f32)
+    ca_ref[...] = nt(g.astype(bf16), proj_ref[...]).astype(bf16).astype(f32)
+    for level in range(LEV):
+        part = slice(level * CELLS, (level + 1) * CELLS)
+        found, cot_scores = attend(
+            q_ref[part, :], k_ref[part, :], v_ref[part, :], ca_ref[part, :],
+            bias_table(bias_ref, BANDS - 1, level),
+        )
+        for ref, value in zip((att_ref, cq_ref, ck_ref, cv_ref), found):
+            ref[part, :] = value
+        cot_scores_ref[level] = cot_scores
+
+
 def attention_kernel(
     x_in_ref, g_in_ref, lat_ref, lon_ref, cor_ref,
     bias_ref, gain_ref, qkv_ref, proj_ref,
+    in_att_ref, in_cq_ref, in_ck_ref, in_cv_ref, in_cot_scores_ref,
     bias_keep_ref, bias_send_ref, x_ref, normed_ref, cot_low_ref, att16_ref, cq16_ref, ck16_ref, cv16_ref,
     g_ref, q_ref, k_ref, v_ref, ca_ref, att_ref, cq_ref, ck_ref, cv_ref,
 ):
@@ -223,67 +299,32 @@
             else:
                 src = strip_row(source, array, level, line, start)
                 dst[at : at + count, :] = strips[source][src : src + count, :]
-    gain = gain_ref[...]
-    unit_field, inverse = norm_parts(x_ref[...])
-    normed = (unit_field * gain).astype(bf16)
-    weights_qkv = [qkv_ref[:, i * D : (i + 1) * D] for i in range(3)]
-    w_proj = proj_ref[...]
-    for ref, weight in zip((q_ref, k_ref, v_ref), weights_qkv):
-        ref[...] = nn(normed, weight).astype(bf16).astype(f32)
+    unit_field, _ = norm_parts(x_ref[...])
+    normed = (unit_field * gain_ref[...]).astype(bf16)
+    for i, ref in enumerate((q_ref, k_ref, v_ref)):
+        ref[...] = nn(normed, qkv_ref[:, i * D : (i + 1) * D]).astype(bf16).astype(f32)
     cot_low = g_ref[...].astype(bf16)
-    ca_ref[...] = nt(cot_low, w_proj).astype(bf16).astype(f32)
-
-    lane_head = lax.broadcasted_iota(jnp.int32, (CELLS, D), 1) // HEAD_DIM
-    of_head = [lane_head == h for h in range(HEADS)]
-    pad = jnp.zeros((LANES - CELLS, D), f32)
-
-    def stacked(value):
-        return jnp.concatenate([jnp.where(m, value, 0.0) for m in of_head], 0).astype(bf16)
-
-    def gathered(value):
-        total = jnp.where(of_head[0], value[:CELLS], 0.0)
-        for h in range(1, HEADS):
-            total = jnp.where(of_head[h], value[h * CELLS : (h + 1) * CELLS], total)
-        return total
-
-    first_band = lax.axis_index("lat") == 0
-    query_low = lax.broadcasted_iota(jnp.int32, (CELLS, LANES), 0) < CELLS // 2
-    key = lax.broadcasted_iota(jnp.int32, (CELLS, LANES), 1)
-    apart = jnp.logical_and(query_low != (key < CELLS // 2), first_band)
+    ca_ref[...] = nt(cot_low, proj_ref[...]).astype(bf16).astype(f32)
     lane = lax.broadcasted_iota(jnp.int32, (STACK, LANES), 1)
     bias_grads = []
     for band in range(BANDS):
         for level in range(LEV):
-            tables = []
-            low = level * CELLS
-            for h in range(HEADS):
-                table = bias_ref[band, 0, h].astype(f32)[low : low + CELLS, low : low + CELLS]
-                table = jnp.concatenate([table, jnp.full((CELLS, LANES - CELLS), padded_score, f32)], 1)
-                if band == 0:
-                    table = jnp.where(jnp.logical_and(apart, key < CELLS), masked_score, table)
-                tables.append(table)
-            table = jnp.concatenate(tables, 0)
+            table = bias_table(bias_ref, band, level)
             bias_grad = None
             for sector in range(SECTORS):
                 base = window_of(band, level, sector) * CELLS
                 part = slice(base, base + CELLS)
-                queries = stacked(q_ref[part, :])
-                key_part = jnp.concatenate([k_ref[part, :], pad], 0).astype(bf16)
-                value_part = jnp.concatenate([v_ref[part, :], pad], 0).astype(bf16)
-                scores = nt(queries, key_part) * score_scale + table
-                exponent = jnp.exp(scores - jnp.max(scores, -1, keepdims=True))
-                probability = exponent * (1.0 / jnp.sum(exponent, -1, keepdims=True))
-                weights = probability.astype(bf16)
-                att_ref[part, :] = gathered(nn(weights, value_part))
-                cot_att = stacked(ca_ref[part, :])
-                cot_weights = nt(cot_att, value_part)
-                cv_ref[part, :] = tn(weights, cot_att)[:CELLS]
-                inner = jnp.sum(cot_weights * probability, -1, keepdims=True)
-                cot_scores = probability * (cot_weights - inner)
+                if band == BANDS - 1 and sector == SECTORS - 1:
+                    given = slice(level * CELLS, (level + 1) * CELLS)
+                    found = tuple(ref[given, :] for ref in (in_att_ref, in_cq_ref, in_ck_ref, in_cv_ref))
+                    cot_scores = in_cot_scores_ref[level]
+                else:
+                    found, cot_scores = attend(
+                        q_ref[part, :], k_ref[part, :], v_ref[part, :], ca_ref[part, :], table
+                    )
+                for ref, value in zip((att_ref, cq_ref, ck_ref, cv_ref), found):
+                    ref[part, :] = value
                 bias_grad = cot_scores if bias_grad is None else bias_grad + cot_scores
-                scaled = (cot_scores * score_scale).astype(bf16)
-                cq_ref[part, :] = gathered(nn(scaled, key_part))
-                ck_ref[part, :] = tn(scaled, queries)[:CELLS]
             bias_grads.append(bias_grad)
     left = [
         jnp.where(lane < 64, bias_grads[2 * b], pltpu.roll(bias_grads[2 * b + 1], 64, 1))
@@ -461,21 +502,23 @@
     for load in loads:
         load.start()
     cot_ref[...] = cot_second_ref[...].astype(f32)
-    for load in loads:
-        load.wait()
     strips = {"lat": lat_ref, "lon": lon_ref, "cor": cor_ref}
-    for at, count, source, level, line, start in all_pieces():
-        if source == "own":
-            f_part, c_part = (ref[at : at + count, :] for ref in (win_f_ref, win_c_ref))
-            row, col = line, start
-        else:
-            row = line + (0 if source == "lon" else KEEP_R)
-            col = start + (0 if source == "lat" else KEEP_C)
-            at_f, at_c = (strip_row(source, array, level, line, start) for array in range(2))
-            f_part, c_part = (strips[source][p : p + count, :] for p in (at_f, at_c))
-        spot = (level, row, slice(col, col + count))
-        in_first_ref[spot] = first_ref[spot] - f_part
-        grad_second_ref[spot] = cot_ref[spot] + c_part
+    for array, window_ref in enumerate((win_f_ref, win_c_ref)):
+        loads[array].wait()
+        for at, count, source, level, line, start in all_pieces():
+            if source == "own":
+                part = window_ref[at : at + count, :]
+                row, col = line, start
+            else:
+                row = line + (0 if source == "lon" else KEEP_R)
+                col = start + (0 if source == "lat" else KEEP_C)
+                place = strip_row(source, array, level, line, start)
+                part = strips[source][place : place + count, :]
+            spot = (level, row, slice(col, col + count))
+            if array == 0:
+                in_first_ref[spot] = first_ref[spot] - part
+            else:
+                grad_second_ref[spot] = cot_ref[spot] + part
 
 
 def kernel(fn, out_shape, scratch=(), name=None, flops=0, nbytes=0, in_hbm=(), out_hbm=()):
@@ -584,12 +627,22 @@
         return kernel(functools.partial(halve_kernel, bit), [parts, parts], name="halve")(keep, recv)
 
     ff_keep, ff_send = ff_step("x_low", ff_keep, across(ff_send, 0))
+    x_inner = x_win
     x_win, ff_keep, ff_send = lax.optimization_barrier((x_win, ff_keep, ff_send))
     ff_recv = across(ff_send, 3)
     at_half = (CHIPS, PART + 4, LANES)
     bias_half = (8, 64, LANES)
     gain = gain_attn.reshape(1, D)
     half_win = half_bytes(*win)
+    one = (LEV * CELLS, D)
+    inner = kernel(
+        inner_attention_kernel,
+        [one, one, one, one, (LEV, STACK, LANES)],
+        [(one, f32)] * 4,
+        "inner",
+        flops=4_000_000_000,
+        nbytes=3_000_000,
+    )(x_inner, g_win, earth_bias, gain, w_qkv, w_proj)
     bias_keep, bias_send, x_win, *attention_parts = kernel(
         attention_kernel,
         [bias_half, bias_half, win, *[half_win] * 6],
@@ -597,7 +650,7 @@
         "attention",
         flops=14_000_000_000,
         nbytes=16_000_000,
-    )(x_win, g_win, lat, lon, cor, earth_bias, gain, w_qkv, w_proj)
+    )(x_win, g_win, lat, lon, cor, earth_bias, gain, w_qkv, w_proj, *inner)
     bias_keep, bias_recv = along_x(bias_keep, 1), along_x(bias_send, -1)
     keep, send, cot_normed = kernel(
         attention_grads_kernel, [at_half, at_half, win], name="attngrads", flops=2_000_000_000, nbytes=4_000_000

time: 115 us -> 114 us (level)
  waiting for transfers between devices: 27.5 us -> 23.3 us
  blocking collectives: 25.7 us -> 26.9 us
    ppermute x2, waiting for transfers between devices: 16.9 us -> 10.4 us  [halo(): lax.ppermute(cor, both, diagonal)]
    ppermute x2, waiting for transfers between devices: 0.01 us -> 4.66 us  [halo(): lax.ppermute(lon, 'lon', ring(lon_count))]
    ppermute x6, waiting for transfers between devices: 5.81 us -> 3.48 us  [across(): lax.ppermute(value, 'lat', [(i, i ^ 1 << bit) for i in range(lat_count)])]
    all_to_all x2, blocking collectives: 25.7 us -> 26.9 us  [swap_z(): lax.all_to_all(value, 'lon', 0, 0, tiled=True, axis_index_groups=same_x)]
    ppermute x2, starting transfers between devices: 2.86 us -> 1.69 us  [halo(): lax.ppermute(cor, both, diagonal)]
    pallas_call x16 -> x17, Pallas kernels: 21.2 us -> 22.3 us  [call(): pl.pallas_call(fn, out_shape=[s if hasattr(s, 'dtype') else jax.ShapeDtyp...]
  transfers between devices with their start and end apart: 19 -> 19, of which waited for: 6 -> 6; matrix products, arithmetic and copies ran while one was open for 0% -> 0% of each run, Pallas kernels for 12% -> 13%
where the time goes in v4:
time: 114 us; the launch traced here: 113 us
  starting transfers between devices  38.4 us (34%)
  blocking collectives  26.9 us (24%)
  waiting for transfers between devices  23.3 us (20%)
  Pallas kernels  22.3 us (20%)
  local copies, waits for them, and re-layouts  1.55 us (1%)
    all_to_all x2, blocking collectives, swap_z(): lax.all_to_all(value, 'lon', 0, 0, tiled=True, axis_index_groups=same_x)  26.9 us
    pallas_call x17, Pallas kernels, call(): pl.pallas_call(fn, out_shape=[s if hasattr(s, 'dtype') else jax.ShapeDtyp...  22.3 us
    ppermute x2, waiting for transfers between devices, halo(): lax.ppermute(cor, both, diagonal)  10.4 us
    ppermute x6, starting transfers between devices, across(): lax.ppermute(value, 'lat', [(i, i ^ 1 << bit) for i in range(lat_count)])  10 us
    ppermute x2, starting transfers between devices, halo(): lax.ppermute(lat, 'lat', ring(lat_count))  7.96 us
    all_to_all x2, starting transfers between devices, swap_xy(): lax.all_to_all(value, both, 0, 0, tiled=True, axis_index_groups=same_z)  7.33 us
    ppermute x4, starting transfers between devices, along_x(): return lax.ppermute(value, both, pairs)  5.55 us
    ppermute x2, waiting for transfers between devices, halo(): lax.ppermute(lon, 'lon', ring(lon_count))  4.66 us
  transfers between devices with their start and end apart: 19, of which 6 were waited for; matrix products, arithmetic and copies ran while one was open for 0% of the time, Pallas kernels for 13%

profile of v4, /device:TPU:1, one launch (start us, length us, event | category | flops | bytes accessed | tf_op | source)
XLA Modules:
  0.0 113.4 jit_solution(5059064948724041473)
XLA Ops:
  0.6 4.7 %feedforward.1 = (f32[2,12,24,192]{3,2,1,0:T(8,128)}, f32[2,12,24,192]{3,2,1,0:T(8,128)}, f32[576,192]{1,0:T(8,128)S(1)}, f32[576,192]{1,0:T(8,128)S(1)}, f32[21...) custom-call(f32[2,12,24,192]{3,2,1,0:T(8,128)} %first_ref.1, ...), custom_call_target="tpu_custom_call" | custom-call | flops 679477248 | bytes 6000000 | tf_op jit(solution)/shard_map/feedforward/pallas_call | solution.py:536
  6.1 3.3 %collective-permute-start = (f32[16,72,128]{2,1,0:T(8,128)S(1)}, f32[16,72,128]{2,1,0:T(8,128)S(1)}, u32[]{:S(2)}, u32[]{:S(2)}) collective-permute-start(f32[16,72,128]{2,1,0:T(8,128)S(1)} %get-tuple-element.95), channel_id=1, source_target_pairs={{0,16},{16,0},{32,48},{48,32},{64,80},{80,64},{96,112},{112,96},{1... | collective-permute-start | bytes 1769480 | tf_op jit(solution)/shard_map/ppermute | solution.py:596
  10.9 1.6 %collective-permute-start.2 = (f32[216,192]{1,0:T(8,128)S(1)}, f32[216,192]{1,0:T(8,128)S(1)}, u32[]{:S(2)}, u32[]{:S(2)}) collective-permute-start(f32[216,192]{1,0:T(8,128)S(1)} %get-tuple-element.101), channel_id=1, source_target_pairs={{0,1},{1,2},{2,3},{3,4},{4,5},{5,6},{6,7},{7,8},{8,9},{9,10},{10,1... | collective-permute-start | bytes 497672 | tf_op jit(solution)/shard_map/ppermute | solution.py:567
  12.6 1.8 %inner.1 = (f32[144,192]{1,0:T(8,128)S(1)}, f32[144,192]{1,0:T(8,128)S(1)}, f32[144,192]{1,0:T(8,128)S(1)}, f32[144,192]{1,0:T(8,128)S(1)}, f32[2,432,128]{2,1,0:T(8,128)S(1)}) custom-call(f32[576,192]{1,0:T(8,128)S(1)} %get-tuple-element.98.x_ref.x_in_ref, f32[576,192]{1,0:T(8,128)S(1)} %get-tuple-element.99.g_ref.g_in_ref, ...), custom_call_target="tpu_custom_call" | custom-call | flops 4000000000 | bytes 3000000 | tf_op jit(solution)/shard_map/inner/pallas_call | solution.py:536
  14.4 1.5 %collective-permute-start.4 = (f32[8,72,128]{2,1,0:T(8,128)S(1)}, f32[8,72,128]{2,1,0:T(8,128)S(1)}, u32[]{:S(2)}, u32[]{:S(2)}) collective-permute-start(f32[8,72,128]{2,1,0:T(8,128)S(1)} %get-tuple-element.118), channel_id=1, source_target_pairs={{0,128},{16,144},{32,160},{48,176},{64,192},{80,208},{96,224},{112... | collective-permute-start | bytes 884744 | tf_op jit(solution)/shard_map/ppermute | solution.py:596
  15.9 2.5 %collective-permute-done.3.cor_ref = f32[72,192]{1,0:T(8,128)S(1)} collective-permute-done((f32[72,192]{1,0:T(8,128)S(1)}, f32[72,192]{1,0:T(8,128)S(1)}, u32[]{:S(2)}, u32[]{:S(2)}) %collective-permute-start.3) | collective-permute-done | bytes 55328 | tf_op jit(solution)/shard_map/ppermute | solution.py:568
  18.5 4.7 %collective-permute-done.2.lon_ref = f32[216,192]{1,0:T(8,128)S(1)} collective-permute-done((f32[216,192]{1,0:T(8,128)S(1)}, f32[216,192]{1,0:T(8,128)S(1)}, u32[]{:S(2)}, u32[]{:S(2)}) %collective-permute-start.2) | collective-permute-done | bytes 165920 | tf_op jit(solution)/shard_map/ppermute | solution.py:567
  23.1 5.8 %attention.1 = (f32[8,64,128]{2,1,0:T(8,128)S(1)}, f32[8,64,128]{2,1,0:T(8,128)S(1)}, f32[576,192]{1,0:T(8,128)S(1)}, bf16[576,192]{1,0:T(8,128)(2,1)S(1)}, bf16...) custom-call(f32[576,192]{1,0:T(8,128)S(1)} %get-tuple-element.98.x_r, ...), custom_call_target="tpu_custom_call" | custom-call | flops 14000000000 | bytes 16000000 | tf_op jit(solution)/shard_map/attention/pallas_call | solution.py:536
  30.8 2.4 %collective-permute-start.7 = (f32[8,64,128]{2,1,0:T(8,128)S(1)}, f32[8,64,128]{2,1,0:T(8,128)S(1)}, u32[]{:S(2)}, u32[]{:S(2)}) collective-permute-start(f32[8,64,128]{2,1,0:T(8,128)S(1)} %get-tuple-element.132), channel_id=1, source_target_pairs={{0,136},{1,137},{2,138},{3,139},{4,140},{5,141},{6,142},{7,143},{8... | collective-permute-start | bytes 786440 | tf_op jit(solution)/shard_map/ppermute | solution.py:593
  34.6 3.5 %collective-permute-done.8.recv_ref = f32[4,72,128]{2,1,0:T(8,128)S(1)} collective-permute-done((f32[4,72,128]{2,1,0:T(8,128)S(1)}, f32[4,72,128]{2,1,0:T(8,128)S(1)}, u32[]{:S(2)}, u32[]{:S(2)}) %collective-permute-start.8) | collective-permute-done | bytes 147488 | tf_op jit(solution)/shard_map/ppermute | solution.py:596
  38.1 3.0 %collective-permute-start.9 = (f32[2,72,128]{2,1,0:T(8,128)S(1)}, f32[2,72,128]{2,1,0:T(8,128)S(1)}, u32[]{:S(2)}, u32[]{:S(2)}) collective-permute-start(f32[2,72,128]{2,1,0:T(8,128)S(1)} %get-tuple-element.137), channel_id=1, source_target_pairs={{0,64},{16,80},{32,96},{48,112},{64,0},{80,16},{96,32},{112,48},{1... | collective-permute-start | bytes 221192 | tf_op jit(solution)/shard_map/ppermute | solution.py:596
  43.7 3.6 %all-to-all-start = ((f32[16,40,128]{2,1,0:T(8,128)}), f32[16,40,128]{2,1,0:T(8,128)S(1)}, u32[]{:S(2)}, u32[]{:S(2)}) async-start(f32[16,40,128]{2,1,0:T(8,128)} %xyjoin.1), calls=%async_computation | async-start | bytes 655360 | tf_op jit(solution)/shard_map/all_to_all | solution.py:579
  47.3 3.0 %collective-permute-start.10 = (f32[1,72,128]{2,1,0:T(8,128)S(1)}, f32[1,72,128]{2,1,0:T(8,128)S(1)}, u32[]{:S(2)}, u32[]{:S(2)}) collective-permute-start(f32[1,72,128]{2,1,0:T(8,128)S(1)} %get-tuple-element.144), channel_id=1, source_target_pairs={{0,8},{1,9},{2,10},{3,11},{4,12},{5,13},{6,14},{7,15},{8,0},{9,1},... | collective-permute-start | bytes 110600 | tf_op jit(solution)/shard_map/ppermute | solution.py:585
  50.2 3.2 %collective-permute-done.10.ff_recv_ref = f32[1,72,128]{2,1,0:T(8,128)S(1)} collective-permute-done((f32[1,72,128]{2,1,0:T(8,128)S(1)}, f32[1,72,128]{2,1,0:T(8,128)S(1)}, u32[]{:S(2)}, u32[]{:S(2)}) %collective-permute-start.10) | collective-permute-done | bytes 36896 | tf_op jit(solution)/shard_map/ppermute | solution.py:585
  53.4 1.6 %all-to-all-done.parts_ref = f32[16,40,128]{2,1,0:T(8,128)S(1)} async-done(((f32[16,40,128]{2,1,0:T(8,128)}), f32[16,40,128]{2,1,0:T(8,128)S(1)}, u32[]{:S(2)}, u32[]{:S(2)}) %all-to-all-start) | async-done | bytes 327712 | tf_op jit(solution)/shard_map/all_to_all | solution.py:579
  55.1 14.5 %all_to_all.20.in_ref = f32[8,80,128]{2,1,0:T(8,128)S(1)} all-to-all(f32[8,80,128]{2,1,0:T(8,128)S(1)} %zjoin.1), channel_id=1, replica_groups={{0,1,2,3,4,5,6,7},{8,9,10,11,12,13,14,15},{16,17,18,19,20,21,22,23},{24..., dimensions={0} | all-to-all | bytes 655360 | tf_op jit(solution)/shard_map/all_to_all | solution.py:582
  69.6 12.4 %all_to_all.21.in_ref = f32[8,80,128]{2,1,0:T(8,128)S(1)} all-to-all(f32[8,80,128]{2,1,0:T(8,128)S(1)} %total.1), channel_id=1, replica_groups={{0,1,2,3,4,5,6,7},{8,9,10,11,12,13,14,15},{16,17,18,19,20,21,22,23},{24..., dimensions={0} | all-to-all | bytes 655360 | tf_op jit(solution)/shard_map/all_to_all | solution.py:582
  83.0 3.8 %all-to-all-start.3 = ((f32[16,112,128]{2,1,0:T(8,128)}), f32[16,112,128]{2,1,0:T(8,128)S(1)}, u32[]{:S(2)}, u32[]{:S(2)}) async-start(f32[16,112,128]{2,1,0:T(8,128)} %get-tuple-element.145), calls=%async_computation.3 | async-start | bytes 1835008 | tf_op jit(solution)/shard_map/all_to_all | solution.py:579
  88.1 1.5 %collective-permute-start.14 = (f32[8,64,128]{2,1,0:T(8,128)S(1)}, f32[8,64,128]{2,1,0:T(8,128)S(1)}, u32[]{:S(2)}, u32[]{:S(2)}) collective-permute-start(f32[8,64,128]{2,1,0:T(8,128)S(1)} %get-tuple-element.157), channel_id=1, source_target_pairs={{0,136},{1,137},{2,138},{3,139},{4,140},{5,141},{6,142},{7,143},{8... | collective-permute-start | bytes 786440 | tf_op jit(solution)/shard_map/ppermute | solution.py:593
  89.6 7.4 %collective-permute-start.11 = (f32[216,192]{1,0:T(8,128)S(1)}, f32[216,192]{1,0:T(8,128)S(1)}, u32[]{:S(2)}, u32[]{:S(2)}) collective-permute-start(f32[216,192]{1,0:T(8,128)S(1)} %get-tuple-element.146), channel_id=1, source_target_pairs={{0,240},{16,0},{32,16},{48,32},{64,48},{80,64},{96,80},{112,96},{1... | collective-permute-start | bytes 497672 | tf_op jit(solution)/shard_map/ppermute | solution.py:566
  99.0 7.9 %collective-permute-done.13.cor_ref = f32[72,192]{1,0:T(8,128)S(1)} collective-permute-done((f32[72,192]{1,0:T(8,128)S(1)}, f32[72,192]{1,0:T(8,128)S(1)}, u32[]{:S(2)}, u32[]{:S(2)}) %collective-permute-start.13) | collective-permute-done | bytes 55328 | tf_op jit(solution)/shard_map/ppermute | solution.py:568
  107.7 1.8 %bias.1 = f32[2,1,6,144,144]{4,3,2,1,0:T(8,128)} custom-call(f32[8,64,128]{2,1,0:T(8,128)S(1)} %collective-permute-done.14.next_ref, f32[8,64,128]{2,1,0:T(8,128)S(1)} %collective-permute-done.15.before_ref), custom_call_target="tpu_custom_call" | custom-call | tf_op jit(solution)/shard_map/bias/pallas_call | solution.py:536
  109.5 2.4 %streams.1 = (f32[2,12,24,192]{3,2,1,0:T(8,128)}, f32[2,12,24,192]{3,2,1,0:T(8,128)}) custom-call(f32[2,12,24,192]{3,2,1,0:T(8,128)S(1)} %copy-done.1, bf16[2,12,24,192]{3,2,1,0:T(8,128)(2,1)S(1)} %copy-done.2, f32[576,192]{1,0:T(8,128)} %copy-done.8, f32[576,192]{1,0:T(8,128)} %copy-done.9, f32[216,192]{1,0:T(8,128)S(1)} %collective-permute-done.11.lat_ref, ...), custom_call_target="tpu_custom_call" | custom-call | flops 2000000000 | bytes 3000000 | tf_op jit(solution)/shard_map/streams/pallas_call | solution.py:536
  111.9 1.5 %last.1 = (f32[1,192]{1,0:T(1,128)}, f32[192,576]{1,0:T(8,128)}, f32[192,192]{1,0:T(8,128)}, f32[1,192]{1,0:T(1,128)}, f32[192,768]{1,0:T(8,128)}, /*index=5*/f32[192,768]{1,0:T(8,128)}) custom-call(f32[16,112,128]{2,1,0:T(8,128)S(1)} %all-to-all-done.3.mine_ref, f32[16,112,128]{2,1,0:T(8,128)S(1)} %collective-permute-done.16.other_ref), custom_call_target="tpu_custom_call" | custom-call | bytes 6000000 | tf_op jit(solution)/shard_map/last/pallas_call | solution.py:536
  (53 shorter events, 13.3 us)
Async XLA Ops:
  5.4 7.2 %copy-start = (bf16[2,1,6,144,144]{4,3,2,1,0:T(8,128)(2,1)S(1)}, bf16[2,1,6,144,144]{4,3,2,1,0:T(8,128)(2,1)}, u32[]{:S(2)}) copy-start(bf16[2,1,6,144,144]{4,3,2,1,0:T(8,128)(2,1)} %bias_ref.3) | copy-start | bytes 1492996
  5.4 7.2 %copy-start.3 = (bf16[192,576]{1,0:T(8,128)(2,1)S(1)}, bf16[192,576]{1,0:T(8,128)(2,1)}, u32[]{:S(2)}) copy-start(bf16[192,576]{1,0:T(8,128)(2,1)} %qkv_ref.5) | copy-start | bytes 663556
  5.4 7.1 %copy-start.4 = (bf16[192,192]{1,0:T(8,128)(2,1)S(1)}, bf16[192,192]{1,0:T(8,128)(2,1)}, u32[]{:S(2)}) copy-start(bf16[192,192]{1,0:T(8,128)(2,1)} %proj_ref.5) | copy-start | bytes 221188
  6.1 8.2 %collective-permute-start = (f32[16,72,128]{2,1,0:T(8,128)S(1)}, f32[16,72,128]{2,1,0:T(8,128)S(1)}, u32[]{:S(2)}, u32[]{:S(2)}) collective-permute-start(f32[16,72,128]{2,1,0:T(8,128)S(1)} %get-tuple-element.95), channel_id=1, source_target_pairs={{0,16},{16,0},{32,48},{48,32},{64,80},{80,64},{96,112},{112,96},{1... | collective-permute-start | bytes 1769480 | tf_op jit(solution)/shard_map/ppermute | solution.py:596
  9.4 9.0 %collective-permute-start.3 = (f32[72,192]{1,0:T(8,128)S(1)}, f32[72,192]{1,0:T(8,128)S(1)}, u32[]{:S(2)}, u32[]{:S(2)}) collective-permute-start(f32[72,192]{1,0:T(8,128)S(1)} %get-tuple-element.102), channel_id=1, source_target_pairs={{0,17},{1,18},{2,19},{3,20},{4,21},{5,22},{6,23},{7,24},{8,25},{9,... | collective-permute-start | bytes 165896 | tf_op jit(solution)/shard_map/ppermute | solution.py:568
  10.3 8.2 %collective-permute-start.1 = (f32[216,192]{1,0:T(8,128)S(1)}, f32[216,192]{1,0:T(8,128)S(1)}, u32[]{:S(2)}, u32[]{:S(2)}) collective-permute-start(f32[216,192]{1,0:T(8,128)S(1)} %get-tuple-element.100), channel_id=1, source_target_pairs={{0,16},{16,32},{32,48},{48,64},{64,80},{80,96},{96,112},{112,128},... | collective-permute-start | bytes 497672 | tf_op jit(solution)/shard_map/ppermute | solution.py:566
  10.9 12.2 %collective-permute-start.2 = (f32[216,192]{1,0:T(8,128)S(1)}, f32[216,192]{1,0:T(8,128)S(1)}, u32[]{:S(2)}, u32[]{:S(2)}) collective-permute-start(f32[216,192]{1,0:T(8,128)S(1)} %get-tuple-element.101), channel_id=1, source_target_pairs={{0,1},{1,2},{2,3},{3,4},{4,5},{5,6},{6,7},{7,8},{8,9},{9,10},{10,1... | collective-permute-start | bytes 497672 | tf_op jit(solution)/shard_map/ppermute | solution.py:567
  14.4 15.3 %collective-permute-start.4 = (f32[8,72,128]{2,1,0:T(8,128)S(1)}, f32[8,72,128]{2,1,0:T(8,128)S(1)}, u32[]{:S(2)}, u32[]{:S(2)}) collective-permute-start(f32[8,72,128]{2,1,0:T(8,128)S(1)} %get-tuple-element.118), channel_id=1, source_target_pairs={{0,128},{16,144},{32,160},{48,176},{64,192},{80,208},{96,224},{112... | collective-permute-start | bytes 884744 | tf_op jit(solution)/shard_map/ppermute | solution.py:596
  29.8 13.0 %collective-permute-start.5 = (f32[16,40,128]{2,1,0:T(8,128)S(1)}, f32[16,40,128]{2,1,0:T(8,128)S(1)}, u32[]{:S(2)}, u32[]{:S(2)}) collective-permute-start(f32[16,40,128]{2,1,0:T(8,128)S(1)} %get-tuple-element.119), channel_id=1, source_target_pairs={{0,16},{16,0},{32,48},{48,32},{64,80},{80,64},{96,112},{112,96},{1... | collective-permute-start | bytes 983048 | tf_op jit(solution)/shard_map/ppermute | solution.py:596
  30.5 13.1 %collective-permute-start.6 = (f32[8,64,128]{2,1,0:T(8,128)S(1)}, f32[8,64,128]{2,1,0:T(8,128)S(1)}, u32[]{:S(2)}, u32[]{:S(2)}) collective-permute-start(f32[8,64,128]{2,1,0:T(8,128)S(1)} %get-tuple-element.131), channel_id=1, source_target_pairs={{0,128},{1,129},{2,130},{3,131},{4,132},{5,133},{6,134},{7,135},{8... | collective-permute-start | bytes 786440 | tf_op jit(solution)/shard_map/ppermute | solution.py:593
  30.8 12.8 %collective-permute-start.7 = (f32[8,64,128]{2,1,0:T(8,128)S(1)}, f32[8,64,128]{2,1,0:T(8,128)S(1)}, u32[]{:S(2)}, u32[]{:S(2)}) collective-permute-start(f32[8,64,128]{2,1,0:T(8,128)S(1)} %get-tuple-element.132), channel_id=1, source_target_pairs={{0,136},{1,137},{2,138},{3,139},{4,140},{5,141},{6,142},{7,143},{8... | collective-permute-start | bytes 786440 | tf_op jit(solution)/shard_map/ppermute | solution.py:593
  33.2 4.8 %collective-permute-start.8 = (f32[4,72,128]{2,1,0:T(8,128)S(1)}, f32[4,72,128]{2,1,0:T(8,128)S(1)}, u32[]{:S(2)}, u32[]{:S(2)}) collective-permute-start(f32[4,72,128]{2,1,0:T(8,128)S(1)} %get-tuple-element.136), channel_id=1, source_target_pairs={{0,32},{16,48},{32,0},{48,16},{64,96},{80,112},{96,64},{112,80},{1... | collective-permute-start | bytes 442376 | tf_op jit(solution)/shard_map/ppermute | solution.py:596
  38.1 5.6 %collective-permute-start.9 = (f32[2,72,128]{2,1,0:T(8,128)S(1)}, f32[2,72,128]{2,1,0:T(8,128)S(1)}, u32[]{:S(2)}, u32[]{:S(2)}) collective-permute-start(f32[2,72,128]{2,1,0:T(8,128)S(1)} %get-tuple-element.137), channel_id=1, source_target_pairs={{0,64},{16,80},{32,96},{48,112},{64,0},{80,16},{96,32},{112,48},{1... | collective-permute-start | bytes 221192 | tf_op jit(solution)/shard_map/ppermute | solution.py:596
  43.7 11.3 %all-to-all-start = ((f32[16,40,128]{2,1,0:T(8,128)}), f32[16,40,128]{2,1,0:T(8,128)S(1)}, u32[]{:S(2)}, u32[]{:S(2)}) async-start(f32[16,40,128]{2,1,0:T(8,128)} %xyjoin.1), calls=%async_computation | async-start | bytes 655360 | tf_op jit(solution)/shard_map/all_to_all | solution.py:579
  47.3 6.1 %collective-permute-start.10 = (f32[1,72,128]{2,1,0:T(8,128)S(1)}, f32[1,72,128]{2,1,0:T(8,128)S(1)}, u32[]{:S(2)}, u32[]{:S(2)}) collective-permute-start(f32[1,72,128]{2,1,0:T(8,128)S(1)} %get-tuple-element.144), channel_id=1, source_target_pairs={{0,8},{1,9},{2,10},{3,11},{4,12},{5,13},{6,14},{7,15},{8,0},{9,1},... | collective-permute-start | bytes 110600 | tf_op jit(solution)/shard_map/ppermute | solution.py:585
  83.0 26.5 %copy-start.1 = (f32[2,12,24,192]{3,2,1,0:T(8,128)S(1)}, f32[2,12,24,192]{3,2,1,0:T(8,128)}, u32[]{:S(2)}) copy-start(f32[2,12,24,192]{3,2,1,0:T(8,128)} %first_ref.1) | copy-start | bytes 1327108
  83.0 26.5 %copy-start.2 = (bf16[2,12,24,192]{3,2,1,0:T(8,128)(2,1)S(1)}, bf16[2,12,24,192]{3,2,1,0:T(8,128)(2,1)}, u32[]{:S(2)}) copy-start(bf16[2,12,24,192]{3,2,1,0:T(8,128)(2,1)} %cot_second_ref.1) | copy-start | bytes 663556
  83.0 24.5 %all-to-all-start.3 = ((f32[16,112,128]{2,1,0:T(8,128)}), f32[16,112,128]{2,1,0:T(8,128)S(1)}, u32[]{:S(2)}, u32[]{:S(2)}) async-start(f32[16,112,128]{2,1,0:T(8,128)} %get-tuple-element.145), calls=%async_computation.3 | async-start | bytes 1835008 | tf_op jit(solution)/shard_map/all_to_all | solution.py:579
  86.8 20.8 %collective-permute-start.15 = (f32[8,64,128]{2,1,0:T(8,128)S(1)}, f32[8,64,128]{2,1,0:T(8,128)S(1)}, u32[]{:S(2)}, u32[]{:S(2)}) collective-permute-start(f32[8,64,128]{2,1,0:T(8,128)S(1)} %get-tuple-element.157), channel_id=1, source_target_pairs={{0,128},{1,129},{2,130},{3,131},{4,132},{5,133},{6,134},{7,135},{8... | collective-permute-start | bytes 786440 | tf_op jit(solution)/shard_map/ppermute | solution.py:593
  88.1 19.5 %collective-permute-start.14 = (f32[8,64,128]{2,1,0:T(8,128)S(1)}, f32[8,64,128]{2,1,0:T(8,128)S(1)}, u32[]{:S(2)}, u32[]{:S(2)}) collective-permute-start(f32[8,64,128]{2,1,0:T(8,128)S(1)} %get-tuple-element.157), channel_id=1, source_target_pairs={{0,136},{1,137},{2,138},{3,139},{4,140},{5,141},{6,142},{7,143},{8... | collective-permute-start | bytes 786440 | tf_op jit(solution)/shard_map/ppermute | solution.py:593
  89.6 17.9 %collective-permute-start.11 = (f32[216,192]{1,0:T(8,128)S(1)}, f32[216,192]{1,0:T(8,128)S(1)}, u32[]{:S(2)}, u32[]{:S(2)}) collective-permute-start(f32[216,192]{1,0:T(8,128)S(1)} %get-tuple-element.146), channel_id=1, source_target_pairs={{0,240},{16,0},{32,16},{48,32},{64,48},{80,64},{96,80},{112,96},{1... | collective-permute-start | bytes 497672 | tf_op jit(solution)/shard_map/ppermute | solution.py:566
  97.0 10.5 %collective-permute-start.12 = (f32[216,192]{1,0:T(8,128)S(1)}, f32[216,192]{1,0:T(8,128)S(1)}, u32[]{:S(2)}, u32[]{:S(2)}) collective-permute-start(f32[216,192]{1,0:T(8,128)S(1)} %get-tuple-element.147), channel_id=1, source_target_pairs={{0,15},{1,0},{2,1},{3,2},{4,3},{5,4},{6,5},{7,6},{8,7},{9,8},{10,9... | collective-permute-start | bytes 497672 | tf_op jit(solution)/shard_map/ppermute | solution.py:567
  98.2 8.7 %collective-permute-start.13 = (f32[72,192]{1,0:T(8,128)S(1)}, f32[72,192]{1,0:T(8,128)S(1)}, u32[]{:S(2)}, u32[]{:S(2)}) collective-permute-start(f32[72,192]{1,0:T(8,128)S(1)} %get-tuple-element.148), channel_id=1, source_target_pairs={{0,255},{1,240},{2,241},{3,242},{4,243},{5,244},{6,245},{7,246},{8... | collective-permute-start | bytes 165896 | tf_op jit(solution)/shard_map/ppermute | solution.py:568
  107.6 4.3 %collective-permute-start.16 = (f32[16,112,128]{2,1,0:T(8,128)S(1)}, f32[16,112,128]{2,1,0:T(8,128)S(1)}, u32[]{:S(2)}, u32[]{:S(2)}) collective-permute-start(f32[16,112,128]{2,1,0:T(8,128)S(1)} %all-to-all-done.3.mine_ref), channel_id=1, source_target_pairs={{0,16},{16,0},{32,48},{48,32},{64,80},{80,64},{96,112},{112,96},{1... | collective-permute-start | bytes 2752520 | tf_op jit(solution)/shard_map/ppermute | solution.py:596
  (5 other events, 11.4 us)

commit v5 on v4

--- a/solution.py
+++ b/solution.py
@@ -438,7 +438,7 @@
     bias_ref[...] = in_ref[:, :64, :]
 
 
-def bias_kernel(next_ref, before_ref, bias_ref):
+def write_bias(next_ref, before_ref, bias_ref):
     first = half_at(1) == 0
     after, before = (ref[...].reshape(512, LANES) for ref in (next_ref, before_ref))
     packed = jnp.concatenate([jnp.where(first, after, before), jnp.where(first, before, after)], 0)
@@ -492,8 +492,8 @@
 
 
 def stream_kernel(
-    first_ref, cot_second_ref, win_f_hbm, win_c_hbm, lat_ref, lon_ref, cor_ref,
-    in_first_ref, grad_second_ref, cot_ref, win_f_ref, win_c_ref, sems,
+    first_ref, cot_second_ref, win_f_hbm, win_c_hbm, lat_ref, lon_ref, cor_ref, bias_next_ref, bias_before_ref,
+    in_first_ref, grad_second_ref, bias_ref, cot_ref, win_f_ref, win_c_ref, sems,
 ):
     loads = [
         pltpu.make_async_copy(win_f_hbm, win_f_ref, sems.at[0]),
@@ -501,6 +501,7 @@
     ]
     for load in loads:
         load.start()
+    write_bias(bias_next_ref, bias_before_ref, bias_ref)
     cot_ref[...] = cot_second_ref[...].astype(f32)
     strips = {"lat": lat_ref, "lon": lon_ref, "cor": cor_ref}
     for array, window_ref in enumerate((win_f_ref, win_c_ref)):
@@ -689,20 +690,17 @@
     bias_mine, bias_other = along_x(bias_mine, -1), along_x(bias_mine, 1)
     mine = swap_xy(spread)
     mine, lat, lon, cor = lax.optimization_barrier((mine, lat, lon, cor))
-    in_first, grad_second = kernel(
+    mine, bias_mine, bias_other = lax.optimization_barrier((mine, bias_mine, bias_other))
+    other = across(mine, 0)
+    in_first, grad_second, grad_bias = kernel(
         stream_kernel,
-        [shape, shape],
+        [shape, shape, (BANDS, 1, HEADS, 2 * CELLS, 2 * CELLS)],
         [(shape, f32), (win, f32), (win, f32), pltpu.SemaphoreType.DMA((2,))],
         "streams",
         nbytes=3_000_000,
         flops=2_000_000_000,
         in_hbm=(2, 3),
-    )(out_first, cot_second, win_f, win_c, lat, lon, cor)
-    mine, bias_mine, bias_other = lax.optimization_barrier((mine, bias_mine, bias_other))
-    other = across(mine, 0)
-    (grad_bias,) = kernel(bias_kernel, [(BANDS, 1, HEADS, 2 * CELLS, 2 * CELLS)], name="bias")(
-        bias_mine, bias_other
-    )
+    )(out_first, cot_second, win_f, win_c, lat, lon, cor, bias_mine, bias_other)
     grad_gain_attn, grad_qkv, grad_proj, grad_gain_mlp, grad_up, grad_down = kernel(
         last_kernel,
         [(1, D), (D, 3 * D), (D, D), (1, D), (D, FF), (D, FF)],

time: 114 us -> 114 us (level)
    pallas_call x17 -> x16, Pallas kernels: 22.3 us -> 21.4 us  [call(): pl.pallas_call(fn, out_shape=[s if hasattr(s, 'dtype') else jax.ShapeDtyp...]
  transfers between devices with their start and end apart: 19 -> 19, of which waited for: 6 -> 6; matrix products, arithmetic and copies ran while one was open for 0% -> 0% of each run, Pallas kernels for 13% -> 12%
where the time goes in v5:
time: 114 us; the launch traced here: 113 us
  starting transfers between devices  38.2 us (34%)
  blocking collectives  27 us (24%)
  waiting for transfers between devices  23.3 us (20%)
  Pallas kernels  21.4 us (19%)
  local copies, waits for them, and re-layouts  2.42 us (2%)
    all_to_all x2, blocking collectives, swap_z(): lax.all_to_all(value, 'lon', 0, 0, tiled=True, axis_index_groups=same_x)  27 us
    pallas_call x16, Pallas kernels, call(): pl.pallas_call(fn, out_shape=[s if hasattr(s, 'dtype') else jax.ShapeDtyp...  21.4 us
    ppermute x2, waiting for transfers between devices, halo(): lax.ppermute(cor, both, diagonal)  10.4 us
    ppermute x6, starting transfers between devices, across(): lax.ppermute(value, 'lat', [(i, i ^ 1 << bit) for i in range(lat_count)])  10 us
    ppermute x2, starting transfers between devices, halo(): lax.ppermute(lat, 'lat', ring(lat_count))  7.96 us
    all_to_all x2, starting transfers between devices, swap_xy(): lax.all_to_all(value, both, 0, 0, tiled=True, axis_index_groups=same_z)  7.2 us
    ppermute x4, starting transfers between devices, along_x(): return lax.ppermute(value, both, pairs)  5.55 us
    ppermute x2, waiting for transfers between devices, halo(): lax.ppermute(lon, 'lon', ring(lon_count))  4.66 us
  transfers between devices with their start and end apart: 19, of which 6 were waited for; matrix products, arithmetic and copies ran while one was open for 0% of the time, Pallas kernels for 12%

profile of v5, /device:TPU:1, one launch (start us, length us, event | category | flops | bytes accessed | tf_op | source)
XLA Modules:
  0.0 113.4 jit_solution(9363139155633832806)
XLA Ops:
  0.6 4.7 %feedforward.1 = (f32[2,12,24,192]{3,2,1,0:T(8,128)}, f32[2,12,24,192]{3,2,1,0:T(8,128)}, f32[576,192]{1,0:T(8,128)S(1)}, f32[576,192]{1,0:T(8,128)S(1)}, f32[21...) custom-call(f32[2,12,24,192]{3,2,1,0:T(8,128)} %first_ref.1, ...), custom_call_target="tpu_custom_call" | custom-call | flops 679477248 | bytes 6000000 | tf_op jit(solution)/shard_map/feedforward/pallas_call | solution.py:537
  6.1 3.3 %collective-permute-start = (f32[16,72,128]{2,1,0:T(8,128)S(1)}, f32[16,72,128]{2,1,0:T(8,128)S(1)}, u32[]{:S(2)}, u32[]{:S(2)}) collective-permute-start(f32[16,72,128]{2,1,0:T(8,128)S(1)} %get-tuple-element.96), channel_id=1, source_target_pairs={{0,16},{16,0},{32,48},{48,32},{64,80},{80,64},{96,112},{112,96},{1... | collective-permute-start | bytes 1769480 | tf_op jit(solution)/shard_map/ppermute | solution.py:597
  10.9 1.6 %collective-permute-start.2 = (f32[216,192]{1,0:T(8,128)S(1)}, f32[216,192]{1,0:T(8,128)S(1)}, u32[]{:S(2)}, u32[]{:S(2)}) collective-permute-start(f32[216,192]{1,0:T(8,128)S(1)} %get-tuple-element.102), channel_id=1, source_target_pairs={{0,1},{1,2},{2,3},{3,4},{4,5},{5,6},{6,7},{7,8},{8,9},{9,10},{10,1... | collective-permute-start | bytes 497672 | tf_op jit(solution)/shard_map/ppermute | solution.py:568
  12.6 1.8 %inner.1 = (f32[144,192]{1,0:T(8,128)S(1)}, f32[144,192]{1,0:T(8,128)S(1)}, f32[144,192]{1,0:T(8,128)S(1)}, f32[144,192]{1,0:T(8,128)S(1)}, f32[2,432,128]{2,1,0:T(8,128)S(1)}) custom-call(f32[576,192]{1,0:T(8,128)S(1)} %get-tuple-element.99.x_ref.x_in_ref, f32[576,192]{1,0:T(8,128)S(1)} %get-tuple-element.100.g_ref.g_in_ref, ...), custom_call_target="tpu_custom_call" | custom-call | flops 4000000000 | bytes 3000000 | tf_op jit(solution)/shard_map/inner/pallas_call | solution.py:537
  14.4 1.5 %collective-permute-start.4 = (f32[8,72,128]{2,1,0:T(8,128)S(1)}, f32[8,72,128]{2,1,0:T(8,128)S(1)}, u32[]{:S(2)}, u32[]{:S(2)}) collective-permute-start(f32[8,72,128]{2,1,0:T(8,128)S(1)} %get-tuple-element.119), channel_id=1, source_target_pairs={{0,128},{16,144},{32,160},{48,176},{64,192},{80,208},{96,224},{112... | collective-permute-start | bytes 884744 | tf_op jit(solution)/shard_map/ppermute | solution.py:597
  15.9 2.5 %collective-permute-done.3.cor_ref = f32[72,192]{1,0:T(8,128)S(1)} collective-permute-done((f32[72,192]{1,0:T(8,128)S(1)}, f32[72,192]{1,0:T(8,128)S(1)}, u32[]{:S(2)}, u32[]{:S(2)}) %collective-permute-start.3) | collective-permute-done | bytes 55328 | tf_op jit(solution)/shard_map/ppermute | solution.py:569
  18.5 4.7 %collective-permute-done.2.lon_ref = f32[216,192]{1,0:T(8,128)S(1)} collective-permute-done((f32[216,192]{1,0:T(8,128)S(1)}, f32[216,192]{1,0:T(8,128)S(1)}, u32[]{:S(2)}, u32[]{:S(2)}) %collective-permute-start.2) | collective-permute-done | bytes 165920 | tf_op jit(solution)/shard_map/ppermute | solution.py:568
  23.1 5.8 %attention.1 = (f32[8,64,128]{2,1,0:T(8,128)S(1)}, f32[8,64,128]{2,1,0:T(8,128)S(1)}, f32[576,192]{1,0:T(8,128)S(1)}, bf16[576,192]{1,0:T(8,128)(2,1)S(1)}, bf16...) custom-call(f32[576,192]{1,0:T(8,128)S(1)} %get-tuple-element.99.x_r, ...), custom_call_target="tpu_custom_call" | custom-call | flops 14000000000 | bytes 16000000 | tf_op jit(solution)/shard_map/attention/pallas_call | solution.py:537
  30.8 2.4 %collective-permute-start.7 = (f32[8,64,128]{2,1,0:T(8,128)S(1)}, f32[8,64,128]{2,1,0:T(8,128)S(1)}, u32[]{:S(2)}, u32[]{:S(2)}) collective-permute-start(f32[8,64,128]{2,1,0:T(8,128)S(1)} %get-tuple-element.133), channel_id=1, source_target_pairs={{0,136},{1,137},{2,138},{3,139},{4,140},{5,141},{6,142},{7,143},{8... | collective-permute-start | bytes 786440 | tf_op jit(solution)/shard_map/ppermute | solution.py:594
  33.2 1.4 %collective-permute-start.8 = (f32[4,72,128]{2,1,0:T(8,128)S(1)}, f32[4,72,128]{2,1,0:T(8,128)S(1)}, u32[]{:S(2)}, u32[]{:S(2)}) collective-permute-start(f32[4,72,128]{2,1,0:T(8,128)S(1)} %get-tuple-element.137), channel_id=1, source_target_pairs={{0,32},{16,48},{32,0},{48,16},{64,96},{80,112},{96,64},{112,80},{1... | collective-permute-start | bytes 442376 | tf_op jit(solution)/shard_map/ppermute | solution.py:597
  34.6 3.5 %collective-permute-done.8.recv_ref = f32[4,72,128]{2,1,0:T(8,128)S(1)} collective-permute-done((f32[4,72,128]{2,1,0:T(8,128)S(1)}, f32[4,72,128]{2,1,0:T(8,128)S(1)}, u32[]{:S(2)}, u32[]{:S(2)}) %collective-permute-start.8) | collective-permute-done | bytes 147488 | tf_op jit(solution)/shard_map/ppermute | solution.py:597
  38.1 3.0 %collective-permute-start.9 = (f32[2,72,128]{2,1,0:T(8,128)S(1)}, f32[2,72,128]{2,1,0:T(8,128)S(1)}, u32[]{:S(2)}, u32[]{:S(2)}) collective-permute-start(f32[2,72,128]{2,1,0:T(8,128)S(1)} %get-tuple-element.138), channel_id=1, source_target_pairs={{0,64},{16,80},{32,96},{48,112},{64,0},{80,16},{96,32},{112,48},{1... | collective-permute-start | bytes 221192 | tf_op jit(solution)/shard_map/ppermute | solution.py:597
  43.7 3.6 %all-to-all-start = ((f32[16,40,128]{2,1,0:T(8,128)}), f32[16,40,128]{2,1,0:T(8,128)S(1)}, u32[]{:S(2)}, u32[]{:S(2)}) async-start(f32[16,40,128]{2,1,0:T(8,128)} %xyjoin.1), calls=%async_computation | async-start | bytes 655360 | tf_op jit(solution)/shard_map/all_to_all | solution.py:580
  47.3 3.0 %collective-permute-start.10 = (f32[1,72,128]{2,1,0:T(8,128)S(1)}, f32[1,72,128]{2,1,0:T(8,128)S(1)}, u32[]{:S(2)}, u32[]{:S(2)}) collective-permute-start(f32[1,72,128]{2,1,0:T(8,128)S(1)} %get-tuple-element.145), channel_id=1, source_target_pairs={{0,8},{1,9},{2,10},{3,11},{4,12},{5,13},{6,14},{7,15},{8,0},{9,1},... | collective-permute-start | bytes 110600 | tf_op jit(solution)/shard_map/ppermute | solution.py:586
  50.2 3.2 %collective-permute-done.10.ff_recv_ref = f32[1,72,128]{2,1,0:T(8,128)S(1)} collective-permute-done((f32[1,72,128]{2,1,0:T(8,128)S(1)}, f32[1,72,128]{2,1,0:T(8,128)S(1)}, u32[]{:S(2)}, u32[]{:S(2)}) %collective-permute-start.10) | collective-permute-done | bytes 36896 | tf_op jit(solution)/shard_map/ppermute | solution.py:586
  53.4 1.6 %all-to-all-done.parts_ref = f32[16,40,128]{2,1,0:T(8,128)S(1)} async-done(((f32[16,40,128]{2,1,0:T(8,128)}), f32[16,40,128]{2,1,0:T(8,128)S(1)}, u32[]{:S(2)}, u32[]{:S(2)}) %all-to-all-start) | async-done | bytes 327712 | tf_op jit(solution)/shard_map/all_to_all | solution.py:580
  55.1 14.5 %all_to_all.20.in_ref = f32[8,80,128]{2,1,0:T(8,128)S(1)} all-to-all(f32[8,80,128]{2,1,0:T(8,128)S(1)} %zjoin.1), channel_id=1, replica_groups={{0,1,2,3,4,5,6,7},{8,9,10,11,12,13,14,15},{16,17,18,19,20,21,22,23},{24..., dimensions={0} | all-to-all | bytes 655360 | tf_op jit(solution)/shard_map/all_to_all | solution.py:583
  69.6 12.5 %all_to_all.21.in_ref = f32[8,80,128]{2,1,0:T(8,128)S(1)} all-to-all(f32[8,80,128]{2,1,0:T(8,128)S(1)} %total.1), channel_id=1, replica_groups={{0,1,2,3,4,5,6,7},{8,9,10,11,12,13,14,15},{16,17,18,19,20,21,22,23},{24..., dimensions={0} | all-to-all | bytes 655360 | tf_op jit(solution)/shard_map/all_to_all | solution.py:583
  83.1 3.6 %all-to-all-start.3 = ((f32[16,112,128]{2,1,0:T(8,128)}), f32[16,112,128]{2,1,0:T(8,128)S(1)}, u32[]{:S(2)}, u32[]{:S(2)}) async-start(f32[16,112,128]{2,1,0:T(8,128)} %get-tuple-element.146), calls=%async_computation.3 | async-start | bytes 1835008 | tf_op jit(solution)/shard_map/all_to_all | solution.py:580
  88.1 1.5 %collective-permute-start.14 = (f32[8,64,128]{2,1,0:T(8,128)S(1)}, f32[8,64,128]{2,1,0:T(8,128)S(1)}, u32[]{:S(2)}, u32[]{:S(2)}) collective-permute-start(f32[8,64,128]{2,1,0:T(8,128)S(1)} %get-tuple-element.154), channel_id=1, source_target_pairs={{0,136},{1,137},{2,138},{3,139},{4,140},{5,141},{6,142},{7,143},{8... | collective-permute-start | bytes 786440 | tf_op jit(solution)/shard_map/ppermute | solution.py:594
  89.6 7.4 %collective-permute-start.11 = (f32[216,192]{1,0:T(8,128)S(1)}, f32[216,192]{1,0:T(8,128)S(1)}, u32[]{:S(2)}, u32[]{:S(2)}) collective-permute-start(f32[216,192]{1,0:T(8,128)S(1)} %get-tuple-element.147), channel_id=1, source_target_pairs={{0,240},{16,0},{32,16},{48,32},{64,48},{80,64},{96,80},{112,96},{1... | collective-permute-start | bytes 497672 | tf_op jit(solution)/shard_map/ppermute | solution.py:567
  99.0 7.9 %collective-permute-done.13.cor_ref = f32[72,192]{1,0:T(8,128)S(1)} collective-permute-done((f32[72,192]{1,0:T(8,128)S(1)}, f32[72,192]{1,0:T(8,128)S(1)}, u32[]{:S(2)}, u32[]{:S(2)}) %collective-permute-start.13) | collective-permute-done | bytes 55328 | tf_op jit(solution)/shard_map/ppermute | solution.py:569
  108.6 3.3 %streams.1 = (f32[2,12,24,192]{3,2,1,0:T(8,128)}, f32[2,12,24,192]{3,2,1,0:T(8,128)}, f32[2,1,6,144,144]{4,3,2,1,0:T(8,128)}) custom-call(f32[2,12,24,192]{3,2,1,0:T(8,128)S(1)} %copy-done.1, bf16[2,12,24,192]{3,2,1,0:T(8,128)(2,1)S(1)} %copy-done.2, f32[576,192]{1,0:T(8,128)} %copy-done.8, f32[576,192]{1,0:T(8,128)} %copy-done.9, ...), custom_call_target="tpu_custom_call" | custom-call | flops 2000000000 | bytes 3000000 | tf_op jit(solution)/shard_map/streams/pallas_call | solution.py:537
  111.8 1.5 %last.1 = (f32[1,192]{1,0:T(1,128)}, f32[192,576]{1,0:T(8,128)}, f32[192,192]{1,0:T(8,128)}, f32[1,192]{1,0:T(1,128)}, f32[192,768]{1,0:T(8,128)}, /*index=5*/f32[192,768]{1,0:T(8,128)}) custom-call(f32[16,112,128]{2,1,0:T(8,128)S(1)} %all-to-all-done.3.mine_ref, f32[16,112,128]{2,1,0:T(8,128)S(1)} %collective-permute-done.16.other_ref), custom_call_target="tpu_custom_call" | custom-call | bytes 6000000 | tf_op jit(solution)/shard_map/last/pallas_call | solution.py:537
  (52 shorter events, 12.8 us)
Async XLA Ops:
  5.4 7.2 %copy-start = (bf16[2,1,6,144,144]{4,3,2,1,0:T(8,128)(2,1)S(1)}, bf16[2,1,6,144,144]{4,3,2,1,0:T(8,128)(2,1)}, u32[]{:S(2)}) copy-start(bf16[2,1,6,144,144]{4,3,2,1,0:T(8,128)(2,1)} %bias_ref.3) | copy-start | bytes 1492996
  5.4 7.2 %copy-start.3 = (bf16[192,576]{1,0:T(8,128)(2,1)S(1)}, bf16[192,576]{1,0:T(8,128)(2,1)}, u32[]{:S(2)}) copy-start(bf16[192,576]{1,0:T(8,128)(2,1)} %qkv_ref.5) | copy-start | bytes 663556
  5.4 7.1 %copy-start.4 = (bf16[192,192]{1,0:T(8,128)(2,1)S(1)}, bf16[192,192]{1,0:T(8,128)(2,1)}, u32[]{:S(2)}) copy-start(bf16[192,192]{1,0:T(8,128)(2,1)} %proj_ref.5) | copy-start | bytes 221188
  6.1 8.2 %collective-permute-start = (f32[16,72,128]{2,1,0:T(8,128)S(1)}, f32[16,72,128]{2,1,0:T(8,128)S(1)}, u32[]{:S(2)}, u32[]{:S(2)}) collective-permute-start(f32[16,72,128]{2,1,0:T(8,128)S(1)} %get-tuple-element.96), channel_id=1, source_target_pairs={{0,16},{16,0},{32,48},{48,32},{64,80},{80,64},{96,112},{112,96},{1... | collective-permute-start | bytes 1769480 | tf_op jit(solution)/shard_map/ppermute | solution.py:597
  9.4 9.0 %collective-permute-start.3 = (f32[72,192]{1,0:T(8,128)S(1)}, f32[72,192]{1,0:T(8,128)S(1)}, u32[]{:S(2)}, u32[]{:S(2)}) collective-permute-start(f32[72,192]{1,0:T(8,128)S(1)} %get-tuple-element.103), channel_id=1, source_target_pairs={{0,17},{1,18},{2,19},{3,20},{4,21},{5,22},{6,23},{7,24},{8,25},{9,... | collective-permute-start | bytes 165896 | tf_op jit(solution)/shard_map/ppermute | solution.py:569
  10.3 8.2 %collective-permute-start.1 = (f32[216,192]{1,0:T(8,128)S(1)}, f32[216,192]{1,0:T(8,128)S(1)}, u32[]{:S(2)}, u32[]{:S(2)}) collective-permute-start(f32[216,192]{1,0:T(8,128)S(1)} %get-tuple-element.101), channel_id=1, source_target_pairs={{0,16},{16,32},{32,48},{48,64},{64,80},{80,96},{96,112},{112,128},... | collective-permute-start | bytes 497672 | tf_op jit(solution)/shard_map/ppermute | solution.py:567
  10.9 12.2 %collective-permute-start.2 = (f32[216,192]{1,0:T(8,128)S(1)}, f32[216,192]{1,0:T(8,128)S(1)}, u32[]{:S(2)}, u32[]{:S(2)}) collective-permute-start(f32[216,192]{1,0:T(8,128)S(1)} %get-tuple-element.102), channel_id=1, source_target_pairs={{0,1},{1,2},{2,3},{3,4},{4,5},{5,6},{6,7},{7,8},{8,9},{9,10},{10,1... | collective-permute-start | bytes 497672 | tf_op jit(solution)/shard_map/ppermute | solution.py:568
  14.4 15.3 %collective-permute-start.4 = (f32[8,72,128]{2,1,0:T(8,128)S(1)}, f32[8,72,128]{2,1,0:T(8,128)S(1)}, u32[]{:S(2)}, u32[]{:S(2)}) collective-permute-start(f32[8,72,128]{2,1,0:T(8,128)S(1)} %get-tuple-element.119), channel_id=1, source_target_pairs={{0,128},{16,144},{32,160},{48,176},{64,192},{80,208},{96,224},{112... | collective-permute-start | bytes 884744 | tf_op jit(solution)/shard_map/ppermute | solution.py:597
  29.8 13.0 %collective-permute-start.5 = (f32[16,40,128]{2,1,0:T(8,128)S(1)}, f32[16,40,128]{2,1,0:T(8,128)S(1)}, u32[]{:S(2)}, u32[]{:S(2)}) collective-permute-start(f32[16,40,128]{2,1,0:T(8,128)S(1)} %get-tuple-element.120), channel_id=1, source_target_pairs={{0,16},{16,0},{32,48},{48,32},{64,80},{80,64},{96,112},{112,96},{1... | collective-permute-start | bytes 983048 | tf_op jit(solution)/shard_map/ppermute | solution.py:597
  30.5 13.1 %collective-permute-start.6 = (f32[8,64,128]{2,1,0:T(8,128)S(1)}, f32[8,64,128]{2,1,0:T(8,128)S(1)}, u32[]{:S(2)}, u32[]{:S(2)}) collective-permute-start(f32[8,64,128]{2,1,0:T(8,128)S(1)} %get-tuple-element.132), channel_id=1, source_target_pairs={{0,128},{1,129},{2,130},{3,131},{4,132},{5,133},{6,134},{7,135},{8... | collective-permute-start | bytes 786440 | tf_op jit(solution)/shard_map/ppermute | solution.py:594
  30.8 12.8 %collective-permute-start.7 = (f32[8,64,128]{2,1,0:T(8,128)S(1)}, f32[8,64,128]{2,1,0:T(8,128)S(1)}, u32[]{:S(2)}, u32[]{:S(2)}) collective-permute-start(f32[8,64,128]{2,1,0:T(8,128)S(1)} %get-tuple-element.133), channel_id=1, source_target_pairs={{0,136},{1,137},{2,138},{3,139},{4,140},{5,141},{6,142},{7,143},{8... | collective-permute-start | bytes 786440 | tf_op jit(solution)/shard_map/ppermute | solution.py:594
  33.2 4.8 %collective-permute-start.8 = (f32[4,72,128]{2,1,0:T(8,128)S(1)}, f32[4,72,128]{2,1,0:T(8,128)S(1)}, u32[]{:S(2)}, u32[]{:S(2)}) collective-permute-start(f32[4,72,128]{2,1,0:T(8,128)S(1)} %get-tuple-element.137), channel_id=1, source_target_pairs={{0,32},{16,48},{32,0},{48,16},{64,96},{80,112},{96,64},{112,80},{1... | collective-permute-start | bytes 442376 | tf_op jit(solution)/shard_map/ppermute | solution.py:597
  38.1 5.6 %collective-permute-start.9 = (f32[2,72,128]{2,1,0:T(8,128)S(1)}, f32[2,72,128]{2,1,0:T(8,128)S(1)}, u32[]{:S(2)}, u32[]{:S(2)}) collective-permute-start(f32[2,72,128]{2,1,0:T(8,128)S(1)} %get-tuple-element.138), channel_id=1, source_target_pairs={{0,64},{16,80},{32,96},{48,112},{64,0},{80,16},{96,32},{112,48},{1... | collective-permute-start | bytes 221192 | tf_op jit(solution)/shard_map/ppermute | solution.py:597
  43.7 11.3 %all-to-all-start = ((f32[16,40,128]{2,1,0:T(8,128)}), f32[16,40,128]{2,1,0:T(8,128)S(1)}, u32[]{:S(2)}, u32[]{:S(2)}) async-start(f32[16,40,128]{2,1,0:T(8,128)} %xyjoin.1), calls=%async_computation | async-start | bytes 655360 | tf_op jit(solution)/shard_map/all_to_all | solution.py:580
  47.3 6.1 %collective-permute-start.10 = (f32[1,72,128]{2,1,0:T(8,128)S(1)}, f32[1,72,128]{2,1,0:T(8,128)S(1)}, u32[]{:S(2)}, u32[]{:S(2)}) collective-permute-start(f32[1,72,128]{2,1,0:T(8,128)S(1)} %get-tuple-element.145), channel_id=1, source_target_pairs={{0,8},{1,9},{2,10},{3,11},{4,12},{5,13},{6,14},{7,15},{8,0},{9,1},... | collective-permute-start | bytes 110600 | tf_op jit(solution)/shard_map/ppermute | solution.py:586
  69.5 38.1 %copy-start.1 = (f32[2,12,24,192]{3,2,1,0:T(8,128)S(1)}, f32[2,12,24,192]{3,2,1,0:T(8,128)}, u32[]{:S(2)}) copy-start(f32[2,12,24,192]{3,2,1,0:T(8,128)} %first_ref.1) | copy-start | bytes 1327108
  69.5 38.1 %copy-start.2 = (bf16[2,12,24,192]{3,2,1,0:T(8,128)(2,1)S(1)}, bf16[2,12,24,192]{3,2,1,0:T(8,128)(2,1)}, u32[]{:S(2)}) copy-start(bf16[2,12,24,192]{3,2,1,0:T(8,128)(2,1)} %cot_second_ref.1) | copy-start | bytes 663556
  83.1 24.4 %all-to-all-start.3 = ((f32[16,112,128]{2,1,0:T(8,128)}), f32[16,112,128]{2,1,0:T(8,128)S(1)}, u32[]{:S(2)}, u32[]{:S(2)}) async-start(f32[16,112,128]{2,1,0:T(8,128)} %get-tuple-element.146), calls=%async_computation.3 | async-start | bytes 1835008 | tf_op jit(solution)/shard_map/all_to_all | solution.py:580
  86.8 20.8 %collective-permute-start.15 = (f32[8,64,128]{2,1,0:T(8,128)S(1)}, f32[8,64,128]{2,1,0:T(8,128)S(1)}, u32[]{:S(2)}, u32[]{:S(2)}) collective-permute-start(f32[8,64,128]{2,1,0:T(8,128)S(1)} %get-tuple-element.154), channel_id=1, source_target_pairs={{0,128},{1,129},{2,130},{3,131},{4,132},{5,133},{6,134},{7,135},{8... | collective-permute-start | bytes 786440 | tf_op jit(solution)/shard_map/ppermute | solution.py:594
  88.1 19.4 %collective-permute-start.14 = (f32[8,64,128]{2,1,0:T(8,128)S(1)}, f32[8,64,128]{2,1,0:T(8,128)S(1)}, u32[]{:S(2)}, u32[]{:S(2)}) collective-permute-start(f32[8,64,128]{2,1,0:T(8,128)S(1)} %get-tuple-element.154), channel_id=1, source_target_pairs={{0,136},{1,137},{2,138},{3,139},{4,140},{5,141},{6,142},{7,143},{8... | collective-permute-start | bytes 786440 | tf_op jit(solution)/shard_map/ppermute | solution.py:594
  89.6 17.9 %collective-permute-start.11 = (f32[216,192]{1,0:T(8,128)S(1)}, f32[216,192]{1,0:T(8,128)S(1)}, u32[]{:S(2)}, u32[]{:S(2)}) collective-permute-start(f32[216,192]{1,0:T(8,128)S(1)} %get-tuple-element.147), channel_id=1, source_target_pairs={{0,240},{16,0},{32,16},{48,32},{64,48},{80,64},{96,80},{112,96},{1... | collective-permute-start | bytes 497672 | tf_op jit(solution)/shard_map/ppermute | solution.py:567
  97.0 10.5 %collective-permute-start.12 = (f32[216,192]{1,0:T(8,128)S(1)}, f32[216,192]{1,0:T(8,128)S(1)}, u32[]{:S(2)}, u32[]{:S(2)}) collective-permute-start(f32[216,192]{1,0:T(8,128)S(1)} %get-tuple-element.148), channel_id=1, source_target_pairs={{0,15},{1,0},{2,1},{3,2},{4,3},{5,4},{6,5},{7,6},{8,7},{9,8},{10,9... | collective-permute-start | bytes 497672 | tf_op jit(solution)/shard_map/ppermute | solution.py:568
  98.2 8.7 %collective-permute-start.13 = (f32[72,192]{1,0:T(8,128)S(1)}, f32[72,192]{1,0:T(8,128)S(1)}, u32[]{:S(2)}, u32[]{:S(2)}) collective-permute-start(f32[72,192]{1,0:T(8,128)S(1)} %get-tuple-element.149), channel_id=1, source_target_pairs={{0,255},{1,240},{2,241},{3,242},{4,243},{5,244},{6,245},{7,246},{8... | collective-permute-start | bytes 165896 | tf_op jit(solution)/shard_map/ppermute | solution.py:569
  107.6 4.3 %collective-permute-start.16 = (f32[16,112,128]{2,1,0:T(8,128)S(1)}, f32[16,112,128]{2,1,0:T(8,128)S(1)}, u32[]{:S(2)}, u32[]{:S(2)}) collective-permute-start(f32[16,112,128]{2,1,0:T(8,128)S(1)} %all-to-all-done.3.mine_ref), channel_id=1, source_target_pairs={{0,16},{16,0},{32,48},{48,32},{64,80},{80,64},{96,112},{112,96},{1... | collective-permute-start | bytes 2752520 | tf_op jit(solution)/shard_map/ppermute | solution.py:597
  (5 other events, 10.4 us)
